TPU v7x, 512 devices: a whole 4x4x16 slice. The times are simulated.
512 devices in a mesh: rows: 128 (over z, x, core), modes: 4 (over y).
Axes of the slice: x: 4, y: 4, z: 16, core: 2. Of those that a mesh axis runs over, the one named last changes fastest.
Arguments:
- test_basis: bfloat16 [65536, 5, 256], P('rows'), may hold values from -0.009765625 to 0.009765625
- deim_basis: bfloat16 [65536, 5, 512], P('rows', None, 'modes'), may hold values from -6 to 6
- trial_basis: bfloat16 [65536, 5, 256], P('rows'), may hold values from -6 to 6
- jacobian: float32 [2048, 7, 5], P('rows'), may hold values from -1 to 1
- neighbours: int32 [2048, 7], P('rows'), may hold values from 0 to 65535, as said below
- counts: int32 [128], P('rows'), may hold values from 1 to 16, 512 in all
- sample_inverse: float32 [512, 512], P('modes'), may hold values from -0.01171875 to 0.01171875
Outputs:
- reduced_operator: float32 [256, 256], P('modes', 'rows')
Inputs may be any that keep to these rules, and one draw needn't show every extreme that they name: `neighbours`: the first entry of row g is the sampled cell, which lies among the 512 cells of device g // 16; every other entry lies within 128 cells of it. Device r uses its first counts[r] slots; the counts sum to 512.
All inputs are finite; a program needn't handle non-finite values.
Results may differ from a plain program's by a relative error of at most 0.0003.
Values may be sent and summed in bfloat16 or wider, within the bound.
No kernel may reach another device: no remote copies, remote signals or barrier semaphores. Data moves between devices by JAX's collectives and lax.ppermute only.
A program may use at most 64 MiB of HBM per device.

v0:
```python
import jax
import jax.numpy as jnp
from jax import lax
from jax.sharding import Mesh
from jax.sharding import PartitionSpec as P

ROWS = ("rows_0", "rows_1", "rows_2")


def filled_with(x, identity):
    return jnp.zeros_like(x) + jnp.asarray(identity, x.dtype)


def entering(x, axes, combine, identity):
    before = start = filled_with(x, identity)
    so_far = x
    for axis in reversed(axes):
        length, position = (lax.axis_size(axis), lax.axis_index(axis))
        pieces = lax.all_gather(so_far, axis)
        inside, so_far = (start, start)
        for k in range(length):
            passed = k < position
            so_far = combine(so_far, pieces[k])
            inside = jnp.where(passed, so_far, inside)
        before = combine(inside, before)
    return before


def extended(block, sides, width):
    for axis, dim in sides:
        count = lax.axis_size(axis)
        forward = [(i, i + 1) for i in range(count - 1)]
        backward = [(target, source) for source, target in forward]
        low = lax.ppermute(
            lax.slice_in_dim(block, block.shape[dim] - width, None, axis=dim), axis, forward
        )
        high = lax.ppermute(lax.slice_in_dim(block, 0, width, axis=dim), axis, backward)
        block = jnp.concatenate([low, block, high], axis=dim)
    return block


def rows_for(lines, length):
    spare = -lines.shape[0] % length
    if not spare:
        return lines
    return jnp.concatenate([lines, jnp.zeros((spare, *lines.shape[1:]), lines.dtype)])


def copy_for_each(x, axis):
    copies = jnp.broadcast_to(x, (lax.axis_size(axis), *x.shape))
    return lax.all_to_all(copies, axis, split_axis=0, concat_axis=0, tiled=True)


def in_order(parts, dim):
    shape = list(parts.shape[1:])
    shape[dim] *= parts.shape[0]
    return jnp.moveaxis(parts, 0, dim).reshape(shape)


def whole_of(x, axes, dim):
    far, near = axes
    parts = copy_for_each(copy_for_each(x, far), near)
    return in_order(parts.swapaxes(0, 1).reshape(-1, *x.shape), dim)


def split_up(x, dim, length):
    shape = x.shape
    parts = x.reshape(*shape[:dim], length, shape[dim] // length, *shape[dim + 1 :])
    return jnp.moveaxis(parts, dim, 0)


def summed_on_arrival(x, axis, dim):
    length = lax.axis_size(axis)
    parts = lax.all_to_all(split_up(x, dim, length), axis, 0, 0, tiled=True)
    return jnp.sum(parts, axis=0)


def sum_by_axis(x, axes, dim):
    far, near = axes
    parts = split_up(x, dim, lax.axis_size(far))
    nearer = summed_on_arrival(parts, near, dim + 1)
    arrived = lax.all_to_all(nearer, far, split_axis=0, concat_axis=0, tiled=True)
    return arrived.sum(axis=0)


def nested_sum(x, axes):
    lines = x.reshape(-1, x.shape[-1])
    padded = rows_for(lines, lax.axis_size(axes[0]) * lax.axis_size(axes[1]))
    whole = whole_of(sum_by_axis(padded, axes, 0), axes, 0)
    return lax.slice_in_dim(whole, 0, len(lines)).reshape(x.shape)


def add_ints(earlier, later):
    return earlier + later


def shards(test_basis, deim_basis, trial_basis, jacobian, neighbours, counts, sample_inverse):
    cells, comps, width = trial_basis.shape
    slots, coupled = neighbours.shape
    total_modes = sample_inverse.shape[1]
    rank = lax.axis_index(ROWS)
    groups = lax.axis_size(ROWS)
    flat_test = test_basis.reshape(cells * comps, width)
    flat_deim = deim_basis.reshape(cells * comps, deim_basis.shape[2])
    partial_g = lax.dot_general(
        flat_test, flat_deim, (((0,), (0,)), ((), ())), preferred_element_type=jnp.float32
    )
    offset = entering(counts, ROWS, add_ints, jnp.zeros((1,), jnp.int32))
    slot_ids = jnp.arange(slots, dtype=jnp.int32)
    live = slot_ids < counts[0]
    row_ids = jnp.where(live, offset[0] + slot_ids, -1)
    first_cell = rank * cells
    packed = jnp.concatenate(
        [
            jacobian.reshape(slots, coupled * comps),
            neighbours.astype(jnp.float32),
            row_ids[:, None].astype(jnp.float32),
        ],
        axis=1,
    )
    nearby = extended(packed, ((ROWS, 0),), slots)
    near_jac = nearby[:, : coupled * comps].reshape(-1, coupled, comps)
    near_cells = nearby[:, coupled * comps : coupled * comps + coupled].astype(jnp.int32)
    owner_rows = nearby[:, -1].astype(jnp.int32)
    inside = (near_cells >= first_cell) & (near_cells < first_cell + cells)
    local = jnp.clip(near_cells - first_cell, 0, cells - 1)
    weighted = near_jac * inside[:, :, None].astype(jnp.float32)
    picked = trial_basis[local].astype(jnp.float32)
    contrib = jnp.einsum("snj,snjk->sk", weighted, picked, precision=lax.Precision.HIGHEST)
    mode_ids = jnp.arange(total_modes, dtype=jnp.int32)[None, :]
    total_g = nested_sum(partial_g, (("rows_0", "rows_1"), "rows_2"))
    folded = jnp.dot(
        total_g, sample_inverse, precision=lax.Precision.HIGHEST, preferred_element_type=jnp.float32
    )
    row_tags = jnp.broadcast_to(
        owner_rows[:, None].astype(jnp.float32), (owner_rows.shape[0], groups)
    )
    arrived, arrived_tags = (
        lax.all_to_all(contrib, ROWS, split_axis=1, concat_axis=0, tiled=True),
        lax.all_to_all(row_tags, ROWS, split_axis=1, concat_axis=0, tiled=True),
    )
    received_ids = arrived_tags[:, 0].astype(jnp.int32)
    selector = (received_ids[:, None] == mode_ids).astype(jnp.float32)
    column_b = lax.dot_general(
        selector,
        arrived,
        (((0,), (0,)), ((), ())),
        precision=lax.Precision.HIGHEST,
        preferred_element_type=jnp.float32,
    )
    column_share = jnp.dot(
        folded, column_b, precision=lax.Precision.HIGHEST, preferred_element_type=jnp.float32
    )
    return summed_on_arrival(column_share, "modes", 0)


def solution(mesh):
    split = Mesh(
        mesh.devices.reshape(16, 4, 2, mesh.shape["modes"]), ("rows_0", "rows_1", "rows_2", "modes")
    )
    placed = (
        P(ROWS, None, None),
        P(ROWS, None, "modes"),
        P(ROWS, None, None),
        P(ROWS, None, None),
        P(ROWS, None),
        P(ROWS),
        P("modes", None),
    )
    return jax.shard_map(
        shards, mesh=split, in_specs=placed, out_specs=P("modes", ROWS), check_vma=False
    )
```

profile of v0, /device:TPU:1, one launch (start us, length us, event | category | flops | bytes accessed | tf_op | source)
XLA Modules:
  0.0 191.9 jit_solution(14824528799125073414)
XLA Ops:
  0.8 1.3 dynamic-slice
  2.0 0.8 dynamic-update-slice
  2.8 8.3 %all-reduce = s32[2]{0:T(128)S(1)} all-reduce(s32[2]{0:T(128)S(1)} %dynamic-update-slice), channel_id=2, replica_groups=mesh['rows_0'=16,'rows_1'=4,'rows_2'=2,'modes'=4] {'rows_2'}, use_global_device_ids=true, to_apply=%add | all-reduce | flops 2 | bytes 16
  11.8 1.3 dynamic-slice.1
  13.0 1.4 dynamic-update-slice.1
  14.4 4.6 %all-reduce.1 = s32[4]{0:T(128)S(1)} all-reduce(s32[4]{0:T(128)S(1)} %dynamic-update-slice.1), channel_id=3, replica_groups=mesh['rows_0'=16,'rows_1'=4,'rows_2'=2,'modes'=4] {'rows_1'}, use_global_device_ids=true, to_apply=%add.1 | all-reduce | flops 4 | bytes 32
  19.6 1.3 slice_add_fusion
  20.9 1.3 dynamic-slice.2
  22.2 1.4 dynamic-update-slice.2
  23.6 19.8 %all-reduce.2 = s32[16]{0:T(128)S(1)} all-reduce(s32[16]{0:T(128)S(1)} %dynamic-update-slice.2), channel_id=4, replica_groups=mesh['rows_0'=16,'rows_1'=4,'rows_2'=2,'modes'=4] {'rows_0'}, use_global_device_ids=true, to_apply=%add.2 | all-reduce | flops 16 | bytes 128
  60.2 8.0 %collective-permute-start.1 = (f32[16,43]{0,1:T(8,128)S(1)}, f32[16,43]{0,1:T(8,128)S(1)}, u32[]{:S(2)}, u32[]{:S(2)}) collective-permute-start(f32[16,43]{0,1:T(8,128)S(1)} %pad_maximum_fusion), channel_id=1, source_target_pairs={{4,0},{8,4},{12,8},{16,12},{20,16},{24,20},{28,24},{32,28},{36,32}... | collective-permute-start | bytes 8264 | tf_op jit(solution)/shard_map/ppermute | solution.py:37
  68.2 2.1 %collective-permute-start = (f32[16,43]{0,1:T(8,128)S(1)}, f32[16,43]{0,1:T(8,128)S(1)}, u32[]{:S(2)}, u32[]{:S(2)}) collective-permute-start(f32[16,43]{0,1:T(8,128)S(1)} %pad_maximum_fusion), channel_id=1, source_target_pairs={{0,4},{4,8},{8,12},{12,16},{16,20},{20,24},{24,28},{28,32},{32,36}... | collective-permute-start | bytes 8264 | tf_op jit(solution)/shard_map/ppermute | solution.py:34
  70.4 2.2 %copy.67 = bf16[512,5,256]{2,1,0:T(8,128)(2,1)S(1)} copy(bf16[512,5,256]{2,0,1:T(8,128)(2,1)} %param.7) | data formatting | bytes 2621440 | tf_op args[0]
  72.5 1.4 reshape.79
  73.9 1.6 copy.68
  75.6 1.4 dot_general.20
  77.7 2.5 %fusion.4 = f32[2,64,2,128]{3,1,2,0:T(8,128)} fusion(bf16[64,2,2,2560]{3,2,1,0:T(2,128)(2,1)} %dot_general.20, bf16[2560,128,1,1]{1,0,2,3:T(8,128)(2,1)S(1)} %reshape.156), kind=kOutput, calls=%fused_computation.7 | convolution fusion | flops 167772160 | bytes 2097152 | tf_op jit(solution)/shard_map/dot_general | solution.py:105
  80.2 3.7 %all-to-all-start = ((f32[2,64,2,128]{3,1,2,0:T(8,128)}), f32[2,64,2,128]{3,1,2,0:T(8,128)S(1)}, u32[]{:S(2)}, u32[]{:S(2)}) async-start(f32[2,64,2,128]{3,1,2,0:T(8,128)} %fusion.4), calls=%async_computation | async-start | bytes 262144 | tf_op jit(solution)/shard_map/all_to_all | solution.py:74
  83.8 1.1 all-to-all-done
  86.5 9.7 %all-to-all-start.4 = ((f32[48,128,1]{0,2,1:T(1,128)}), f32[48,128,1]{0,2,1:T(1,128)S(1)}, u32[]{:S(2)}, u32[]{:S(2)}) async-start(f32[48,128,1]{0,2,1:T(1,128)} %broadcast_in_dim.26), calls=%async_computation.4 | async-start | bytes 131072 | tf_op jit(solution)/shard_map/all_to_all | solution.py:140
  96.6 14.4 %all-to-all-done.4 = f32[48,128,1]{0,2,1:T(1,128)S(1)} async-done(((f32[48,128,1]{0,2,1:T(1,128)}), f32[48,128,1]{0,2,1:T(1,128)S(1)}, u32[]{:S(2)}, u32[]{:S(2)}) %all-to-all-start.4) | async-done | bytes 24608 | tf_op jit(solution)/shard_map/all_to_all | solution.py:140
  111.0 4.6 %all-to-all-start.1 = ((f32[64,2,128]{2,1,0:T(2,128)}), f32[64,2,128]{2,1,0:T(2,128)S(1)}, u32[]{:S(2)}, u32[]{:S(2)}) async-start(f32[64,2,128]{2,1,0:T(2,128)} %copy.71), calls=%async_computation.1 | async-start | bytes 131072 | tf_op jit(solution)/shard_map/all_to_all | solution.py:82
  115.6 5.2 %gather_fusion = bf16[336,5,256]{2,0,1:T(8,128)(2,1)S(1)} fusion(bf16[512,5,256]{2,0,1:T(8,128)(2,1)S(1)} %copy-done, s32[1024]{0:T(1024)S(1)} %pad_clamp_fusion), kind=kCustom, calls=%fused_computation | custom fusion | bytes 1721664 | tf_op jit(solution)/shard_map/gather | solution.py:128
  121.5 0.7 copy.84
  122.3 7.3 %all-to-all-done.1 = f32[64,2,128]{2,1,0:T(2,128)S(1)} async-done(((f32[64,2,128]{2,1,0:T(2,128)}), f32[64,2,128]{2,1,0:T(2,128)S(1)}, u32[]{:S(2)}, u32[]{:S(2)}) %all-to-all-start.1) | async-done | bytes 65568 | tf_op jit(solution)/shard_map/all_to_all | solution.py:82
  129.6 8.8 %all-to-all-start.5 = ((f32[48,128,2]{0,2,1:T(2,128)}), f32[48,128,2]{0,2,1:T(2,128)S(1)}, u32[]{:S(2)}, u32[]{:S(2)}) async-start(f32[48,128,2]{0,2,1:T(2,128)} %bitcast.36), calls=%async_computation.5 | async-start | bytes 262144 | tf_op jit(solution)/shard_map/all_to_all | solution.py:139
  138.5 16.0 %all-to-all-done.5 = f32[48,128,2]{0,2,1:T(2,128)S(1)} async-done(((f32[48,128,2]{0,2,1:T(2,128)}), f32[48,128,2]{0,2,1:T(2,128)S(1)}, u32[]{:S(2)}, u32[]{:S(2)}) %all-to-all-start.5) | async-done | bytes 49184 | tf_op jit(solution)/shard_map/all_to_all | solution.py:139
  155.1 6.0 %all-to-all-start.2 = ((f32[64,2,128]{2,1,0:T(2,128)}), f32[64,2,128]{2,1,0:T(2,128)S(1)}, u32[]{:S(2)}, u32[]{:S(2)}) async-start(f32[64,2,128]{2,1,0:T(2,128)} %broadcast_in_dim.12), calls=%async_computation.2 | async-start | bytes 131072 | tf_op jit(solution)/shard_map/all_to_all | solution.py:51
  161.6 4.0 %fusion = f32[512,2]{0,1:T(2,128)S(1)} fusion(f32[6144,2]{0,1:T(2,128)S(1)} %all_to_all.45, s32[6144]{0:T(1024)S(1)} %convert_element_type.54), kind=kOutput, calls=%fused_computation.2 | convolution fusion | flops 78643200 | bytes 77824 | tf_op jit(solution)/shard_map/dot_general | solution.py:144
  165.6 9.6 %all-to-all-done.2 = f32[64,2,128]{2,1,0:T(2,128)S(1)} async-done(((f32[64,2,128]{2,1,0:T(2,128)}), f32[64,2,128]{2,1,0:T(2,128)S(1)}, u32[]{:S(2)}, u32[]{:S(2)}) %all-to-all-start.2) | async-done | bytes 65568 | tf_op jit(solution)/shard_map/all_to_all | solution.py:51
  175.2 5.5 %all_to_all.54 = f32[2,64,2,128]{3,2,1,0:T(2,128)S(1)} all-to-all(f32[2,64,2,128]{3,2,1,0:T(2,128)S(1)} %broadcast_in_dim.24), channel_id=1, replica_groups=mesh['rows_0'=16,'rows_1'=4,'rows_2'=2,'modes'=4] {'rows_2'}, dimensions={0} | all-to-all | bytes 262144 | tf_op jit(solution)/shard_map/all_to_all | solution.py:51
  182.0 8.1 %all_to_all.55 = f32[4,1,128]{2,1,0:T(1,128)S(1)} all-to-all(f32[4,1,128]{2,1,0:T(1,128)S(1)} %reshape.167), channel_id=1, replica_groups=mesh['rows_0'=16,'rows_1'=4,'rows_2'=2,'modes'=4] {'modes'}, dimensions={0} | all-to-all | bytes 4096 | tf_op jit(solution)/shard_map/all_to_all | solution.py:74
  (54 shorter events, 11.1 us)
Async XLA Ops:
  0.0 115.6 %copy-start = (bf16[512,5,256]{2,0,1:T(8,128)(2,1)S(1)}, bf16[512,5,256]{2,0,1:T(8,128)(2,1)}, u32[]{:S(2)}) copy-start(bf16[512,5,256]{2,0,1:T(8,128)(2,1)} %param.9) | copy-start | bytes 3932164
  60.2 25.4 %collective-permute-start.1 = (f32[16,43]{0,1:T(8,128)S(1)}, f32[16,43]{0,1:T(8,128)S(1)}, u32[]{:S(2)}, u32[]{:S(2)}) collective-permute-start(f32[16,43]{0,1:T(8,128)S(1)} %pad_maximum_fusion), channel_id=1, source_target_pairs={{4,0},{8,4},{12,8},{16,12},{20,16},{24,20},{28,24},{32,28},{36,32}... | collective-permute-start | bytes 8264 | tf_op jit(solution)/shard_map/ppermute | solution.py:37
  68.2 17.4 %collective-permute-start = (f32[16,43]{0,1:T(8,128)S(1)}, f32[16,43]{0,1:T(8,128)S(1)}, u32[]{:S(2)}, u32[]{:S(2)}) collective-permute-start(f32[16,43]{0,1:T(8,128)S(1)} %pad_maximum_fusion), channel_id=1, source_target_pairs={{0,4},{4,8},{8,12},{12,16},{16,20},{20,24},{24,28},{28,32},{32,36}... | collective-permute-start | bytes 8264 | tf_op jit(solution)/shard_map/ppermute | solution.py:34
  75.5 1.4 copy-start.1
  80.2 4.8 %all-to-all-start = ((f32[2,64,2,128]{3,1,2,0:T(8,128)}), f32[2,64,2,128]{3,1,2,0:T(8,128)S(1)}, u32[]{:S(2)}, u32[]{:S(2)}) async-start(f32[2,64,2,128]{3,1,2,0:T(8,128)} %fusion.4), calls=%async_computation | async-start | bytes 262144 | tf_op jit(solution)/shard_map/all_to_all | solution.py:74
  86.5 24.5 %all-to-all-start.4 = ((f32[48,128,1]{0,2,1:T(1,128)}), f32[48,128,1]{0,2,1:T(1,128)S(1)}, u32[]{:S(2)}, u32[]{:S(2)}) async-start(f32[48,128,1]{0,2,1:T(1,128)} %broadcast_in_dim.26), calls=%async_computation.4 | async-start | bytes 131072 | tf_op jit(solution)/shard_map/all_to_all | solution.py:140
  111.0 18.6 %all-to-all-start.1 = ((f32[64,2,128]{2,1,0:T(2,128)}), f32[64,2,128]{2,1,0:T(2,128)S(1)}, u32[]{:S(2)}, u32[]{:S(2)}) async-start(f32[64,2,128]{2,1,0:T(2,128)} %copy.71), calls=%async_computation.1 | async-start | bytes 131072 | tf_op jit(solution)/shard_map/all_to_all | solution.py:82
  129.6 24.9 %all-to-all-start.5 = ((f32[48,128,2]{0,2,1:T(2,128)}), f32[48,128,2]{0,2,1:T(2,128)S(1)}, u32[]{:S(2)}, u32[]{:S(2)}) async-start(f32[48,128,2]{0,2,1:T(2,128)} %bitcast.36), calls=%async_computation.5 | async-start | bytes 262144 | tf_op jit(solution)/shard_map/all_to_all | solution.py:139
  155.1 20.1 %all-to-all-start.2 = ((f32[64,2,128]{2,1,0:T(2,128)}), f32[64,2,128]{2,1,0:T(2,128)S(1)}, u32[]{:S(2)}, u32[]{:S(2)}) async-start(f32[64,2,128]{2,1,0:T(2,128)} %broadcast_in_dim.12), calls=%async_computation.2 | async-start | bytes 131072 | tf_op jit(solution)/shard_map/all_to_all | solution.py:51
  161.6 19.1 %copy-start.2 = (f32[128,512]{1,0:T(8,128)S(1)}, f32[128,512]{1,0:T(8,128)}, u32[]{:S(2)}) copy-start(f32[128,512]{1,0:T(8,128)} %param.13) | copy-start | bytes 786436
where the time goes:
time: 193 us; the launch traced here: 192 us
  waiting for transfers between devices  48.4 us (25%)
  blocking collectives  46.3 us (24%)
  starting transfers between devices  42.9 us (22%)
  local copies, waits for them, and re-layouts  25.7 us (13%)
  between operations  15.6 us (8%)
  matrix products  7.5 us (4%)
  other arithmetic  5.42 us (3%)
    unnamed x3, blocking collectives  32.8 us
    all_to_all x1, waiting for transfers between devices, shards(): lax.all_to_all(contrib, ROWS, split_axis=1, concat_axis=0, tiled=True)  16 us
    all_to_all x1, waiting for transfers between devices, shards(): lax.all_to_all(row_tags, ROWS, split_axis=1, concat_axis=0, tiled=True)  14.4 us
    unnamed x21, local copies, waits for them, and re-layouts  11 us
    all_to_all x1, starting transfers between devices, shards(): lax.all_to_all(row_tags, ROWS, split_axis=1, concat_axis=0, tiled=True)  9.69 us
    all_to_all x1, waiting for transfers between devices, copy_for_each(): return lax.all_to_all(copies, axis, split_axis=0, concat_axis=0, tiled=True)  9.58 us
    all_to_all x1, starting transfers between devices, shards(): lax.all_to_all(contrib, ROWS, split_axis=1, concat_axis=0, tiled=True)  8.8 us
    all_to_all x1, blocking collectives, summed_on_arrival(): parts = lax.all_to_all(split_up(x, dim, length), axis, 0, 0, tiled=True)  8.09 us
  transfers between devices with their start and end apart: 7, of which 5 were waited for; matrix products, arithmetic and copies ran while one was open for 11% of the time, Pallas kernels for 0%

commit v1 on v0

v1 whole, which is shorter than its diff:
```python
import jax
import jax.numpy as jnp
from jax import lax
from jax.experimental import pallas as pl
from jax.experimental.pallas import tpu as pltpu
from jax.sharding import Mesh
from jax.sharding import PartitionSpec as P

ROWS = ("z", "x", "c")
PLANE = ("x", "c")
CUBE = ("x", "c", "y")
F32 = jnp.float32
BF16 = jnp.bfloat16
NC, NB = 5, 7
JAC, NBR, CNT = 0, 35, 42
PLANE_CNT, LOW_CNT, OWN_CNT, RANK = 48, 56, 57, 58


def whole(shape):
    return pl.BlockSpec(shape, lambda *_: (0,) * len(shape))


def lanes(shape):
    return lax.broadcasted_iota(jnp.int32, shape, len(shape) - 1)


def project_kernel(v_ref, d_ref, table_ref, out_ref, acc_ref):
    step = pl.program_id(0)
    part = lax.dot_general(
        d_ref[0], v_ref[0], (((0,), (0,)), ((), ())), preferred_element_type=F32
    )

    @pl.when(step == 0)
    def _():
        acc_ref[...] = part

    @pl.when(step > 0)
    def _():
        acc_ref[...] += part

    @pl.when(step == NC - 1)
    def _():
        g = acc_ref[...].T
        count = jnp.broadcast_to(table_ref[0:8, CNT : CNT + 1], (8, 128))
        for p in range(8):
            for m in range(4):
                row = 64 * m + 8 * p
                out_ref[p, 8 * m : 8 * m + 8, :] = g[row : row + 8, :]
            out_ref[p, 32:40, :] = count


def project(test, deim, table):
    return pl.pallas_call(
        project_kernel,
        grid=(NC,),
        in_specs=[
            pl.BlockSpec((1, 512, 256), lambda j: (j, 0, 0)),
            pl.BlockSpec((1, 512, 128), lambda j: (j, 0, 0)),
            whole((16, 128)),
        ],
        out_specs=whole((8, 40, 128)),
        out_shape=jax.ShapeDtypeStruct((8, 40, 128), F32),
        scratch_shapes=[pltpu.VMEM((128, 256), F32)],
        name="project",
    )(test, deim, table)


def sample_kernel(low_ref, own_ref, high_ref, u_ref, out_ref):
    rank = jnp.floor(own_ref[0:1, NBR : NBR + 1] * (1.0 / 512.0))
    slot = lax.broadcasted_iota(jnp.int32, (16, 128), 0).astype(F32)
    entry = lanes((16, 128)) < NBR
    tables = []
    for ref in (low_ref, own_ref, high_ref):
        rows = ref[...]
        dead = entry & (slot >= rows[:, CNT : CNT + 1])
        tables.append(jnp.where(dead, 0.0, rows))
    table = jnp.concatenate(tables, axis=0)
    values = [jnp.broadcast_to(table[:, k : k + 1], (48, 128)) for k in range(NBR)]
    near = [table[:, NBR + n : NBR + n + 1] - rank * 512.0 for n in range(NB)]
    total = jnp.zeros((144, 256), F32)
    for chunk in range(4):
        cell = (lanes((48, 128)) + 128 * chunk).astype(F32)
        hits = [cell == near[n] for n in range(NB)]
        for j in range(NC):
            weight = jnp.where(hits[0], values[j], 0.0)
            for n in range(1, NB):
                weight = weight + jnp.where(hits[n], values[n * NC + j], 0.0)
            w0 = weight.astype(BF16)
            rest = weight - w0.astype(F32)
            w1 = rest.astype(BF16)
            w2 = (rest - w1.astype(F32)).astype(BF16)
            stacked = jnp.concatenate([w0, w1, w2], axis=0)
            total = total + jnp.dot(
                stacked,
                u_ref[j, 128 * chunk : 128 * chunk + 128, :],
                preferred_element_type=F32,
            )
    rows = total[0:48, :] + (total[48:96, :] + total[96:144, :])
    rows = jnp.concatenate([rows, jnp.zeros((80, 256), F32)], axis=0)
    lane = lanes((1, 128))
    extra = jnp.where(lane == LOW_CNT, low_ref[0:1, CNT : CNT + 1], 0.0)
    extra = extra + jnp.where(lane == OWN_CNT, own_ref[0:1, CNT : CNT + 1], 0.0)
    extra = extra + jnp.where(lane == RANK, rank, 0.0)
    cols = rows.T + extra
    for z in range(16):
        out_ref[z, :, :] = cols[16 * z : 16 * z + 16, :]


def sample(low, own, high, trial):
    return pl.pallas_call(
        sample_kernel,
        out_shape=jax.ShapeDtypeStruct((16, 16, 128), F32),
        name="sample",
    )(low, own, high, trial)


def merge_kernel(g_ref, b_ref, out_ref):
    total = g_ref[0, 0:32, :]
    for p in range(1, 8):
        total = total + g_ref[p, 0:32, :]
    lane = lanes((1, 128))
    counts = jnp.zeros((1, 128), F32)
    for p in range(8):
        counts = counts + jnp.where(lane == PLANE_CNT + p, g_ref[p, 32:33, :], 0.0)
    for z in range(16):
        out_ref[z, 0:32, :] = total
        out_ref[z, 32:48, :] = b_ref[z, :, :] + counts


def merge(g_parts, columns):
    return pl.pallas_call(
        merge_kernel,
        out_shape=jax.ShapeDtypeStruct((16, 48, 128), F32),
        name="merge",
    )(g_parts, columns)


def fold_kernel(x_ref, s_ref, out_ref):
    total = x_ref[0, 0:32, :]
    for z in range(1, 16):
        total = total + x_ref[z, 0:32, :]
    info = x_ref[:, 32, :]
    lane = lanes((16, 128))

    def column(k):
        return jnp.sum(jnp.where(lane == k, info, 0.0), axis=1, keepdims=True)

    rank = column(RANK)
    place = rank - 8.0 * jnp.floor(rank * 0.125)
    is_count = (lane >= PLANE_CNT) & (lane < PLANE_CNT + 8)
    counts = jnp.where(is_count, info, 0.0)
    before = lax.broadcasted_iota(jnp.int32, (16, 16), 1) < lax.broadcasted_iota(
        jnp.int32, (16, 16), 0
    )
    lower = jnp.dot(before.astype(F32), counts, preferred_element_type=F32)
    ahead = (lane - PLANE_CNT).astype(F32) < place
    lower = lower + jnp.where(ahead, counts, 0.0)
    offset = jnp.sum(lower, axis=1, keepdims=True)
    shift = jnp.where(lane < 16, -column(LOW_CNT), jnp.where(lane < 32, 0.0, column(OWN_CNT)))
    ids = offset + shift + (lane % 16).astype(F32)
    ids = jnp.where(lane < 48, ids, -1.0)
    mode = lax.broadcasted_iota(jnp.int32, (512, 128), 0).astype(F32)
    slots = lanes((16, 128)) < 48
    full = jnp.zeros((32, 512), F32)
    for z in range(16):
        hot = jnp.where(mode == ids[z : z + 1, :], 1.0, 0.0).astype(BF16)
        cols = jnp.where(slots, x_ref[z, 32:48, :], 0.0)
        high = cols.astype(BF16)
        low = (cols - high.astype(F32)).astype(BF16)
        both = jnp.concatenate([high, low], axis=0)
        full = full + lax.dot_general(
            both, hot, (((1,), (1,)), ((), ())), preferred_element_type=F32
        )
    sampled = full[0:16, :] + full[16:32, :]
    c = lax.dot_general(
        sampled,
        s_ref[...],
        (((1,), (1,)), ((), ())),
        precision=lax.Precision.HIGHEST,
        preferred_element_type=F32,
    )
    blank = jnp.zeros((6, 128), F32)
    for p in range(8):
        mine = jnp.concatenate([c[2 * p : 2 * p + 2, :], blank], axis=0)
        for m in range(4):
            out_ref[4 * p + m, 0:8, :] = total[8 * m : 8 * m + 8, :]
            out_ref[4 * p + m, 8:16, :] = mine


def fold(parts, inverse):
    return pl.pallas_call(
        fold_kernel,
        out_shape=jax.ShapeDtypeStruct((32, 16, 128), F32),
        name="fold",
    )(parts, inverse)


def finish_kernel(x_ref, out_ref):
    for j in range(2):
        c = []
        for m in range(4):
            total = x_ref[m, 8 + j : 9 + j, :]
            for p in range(1, 8):
                total = total + x_ref[4 * p + m, 8 + j : 9 + j, :]
            c.append(total)
        for p in range(8):
            acc = x_ref[4 * p, 0:8, :] * c[0]
            for m in range(1, 4):
                acc = acc + x_ref[4 * p + m, 0:8, :] * c[m]
            out_ref[8 * p : 8 * p + 8, j : j + 1] = jnp.sum(acc, axis=1, keepdims=True)


def finish(parts):
    return pl.pallas_call(
        finish_kernel,
        out_shape=jax.ShapeDtypeStruct((64, 2), F32),
        name="finish",
    )(parts)


def shards(test_basis, deim_basis, trial_basis, jacobian, neighbours, counts, sample_inverse):
    slots = neighbours.shape[0]
    own = jnp.concatenate(
        [
            jacobian.reshape(slots, NB * NC),
            neighbours.astype(F32),
            jnp.broadcast_to(counts.astype(F32)[None, :], (slots, 1)),
            jnp.zeros((slots, 128 - NB * NC - NB - 1), F32),
        ],
        axis=1,
    )
    groups = lax.axis_size(ROWS)
    up = [(i, i + 1) for i in range(groups - 1)]
    down = [(i + 1, i) for i in range(groups - 1)]
    low = lax.ppermute(own, ROWS, up)
    high = lax.ppermute(own, ROWS, down)
    g_part = project(test_basis.swapaxes(0, 1), deim_basis.swapaxes(0, 1), own)
    g_plane = lax.all_to_all(g_part, PLANE, 0, 0, tiled=True)
    columns = sample(low, own, high, trial_basis.swapaxes(0, 1))
    parts = lax.all_to_all(merge(g_plane, columns), "z", 0, 0, tiled=True)
    pieces = lax.all_to_all(fold(parts, sample_inverse), CUBE, 0, 0, tiled=True)
    return finish(pieces)


def solution(mesh):
    split = Mesh(mesh.devices.reshape(16, 4, 2, 4), ("z", "x", "c", "y"))
    placed = (
        P(ROWS, None, None),
        P(ROWS, None, "y"),
        P(ROWS, None, None),
        P(ROWS, None, None),
        P(ROWS, None),
        P(ROWS),
        P("y", None),
    )
    return jax.shard_map(
        shards, mesh=split, in_specs=placed, out_specs=P("y", ROWS), check_vma=False
    )
```

time: 193 us -> 91.8 us (0.48)
  waiting for transfers between devices: 48.4 us -> 0.76 us
  starting transfers between devices: 42.9 us -> 15.7 us
  local copies, waits for them, and re-layouts: 25.7 us -> 3.71 us
  between operations: 15.6 us -> 0.7 us
  Pallas kernels: 0 us -> 14.2 us
  blocking collectives: 46.3 us -> 54.6 us
  matrix products: 7.5 us -> 0 us
  other arithmetic: 5.42 us -> 1.37 us
    all_to_all x5 -> x1, waiting for transfers between devices: 48.4 us -> 0.01 us  [shards(): g_plane = lax.all_to_all(g_part, PLANE, 0, 0, tiled=True)]
    all_to_all x2, blocking collectives: 13.6 us -> 54.6 us  [the longest x1 28.3 us: shards(): pieces = lax.all_to_all(fold(parts, sample_inverse), CUBE, 0, 0, tiled=True)]
    unnamed x3 -> x0, blocking collectives: 32.8 us -> none
    all_to_all x5 -> x1, starting transfers between devices: 32.8 us -> 10.2 us  [shards(): g_plane = lax.all_to_all(g_part, PLANE, 0, 0, tiled=True)]
    pallas_call x0 -> x5, Pallas kernels: none -> 14.2 us  [the longest x1 4.5 us: project(): pl.pallas_call(project_kernel, grid=(NC,), in_specs=[pl.BlockSpec((1, 512...]
    unnamed x21 -> x9, local copies, waits for them, and re-layouts: 11 us -> 2 us
    dot_general x4 -> x0, matrix products: 7.5 us -> none  [the longest x1 3.96 us: shards(): lax.dot_general(selector, arrived, (((0,), (0,)), ((), ())), precision=la...]
    gather x2 -> x0, local copies, waits for them, and re-layouts: 5.45 us -> none  [shards(): picked = trial_basis[local].astype(jnp.float32)]
  transfers between devices with their start and end apart: 7 -> 3, of which waited for: 5 -> 1; matrix products, arithmetic and copies ran while one was open for 11% -> 0% of each run, Pallas kernels for 0% -> 3%
where the time goes in v1:
time: 91.8 us; the launch traced here: 91.1 us
  blocking collectives  54.6 us (59%)
  starting transfers between devices  15.7 us (17%)
  Pallas kernels  14.2 us (15%)
  local copies, waits for them, and re-layouts  3.71 us (4%)
  other arithmetic  1.37 us (1%)
    all_to_all x1, blocking collectives, shards(): pieces = lax.all_to_all(fold(parts, sample_inverse), CUBE, 0, 0, tiled=True)  28.3 us
    all_to_all x1, blocking collectives, shards(): parts = lax.all_to_all(merge(g_plane, columns), 'z', 0, 0, tiled=True)  26.4 us
    all_to_all x1, starting transfers between devices, shards(): g_plane = lax.all_to_all(g_part, PLANE, 0, 0, tiled=True)  10.2 us
    pallas_call x1, Pallas kernels, project(): pl.pallas_call(project_kernel, grid=(NC,), in_specs=[pl.BlockSpec((1, 512...  4.5 us
    ppermute x1, starting transfers between devices, shards(): low = lax.ppermute(own, ROWS, up)  3.53 us
    pallas_call x1, Pallas kernels, fold(): pl.pallas_call(fold_kernel, out_shape=jax.ShapeDtypeStruct((32, 16, 128),...  3.18 us
    pallas_call x1, Pallas kernels, sample(): pl.pallas_call(sample_kernel, out_shape=jax.ShapeDtypeStruct((16, 16, 128...  3.13 us
    ppermute x1, starting transfers between devices, shards(): high = lax.ppermute(own, ROWS, down)  2.02 us
  transfers between devices with their start and end apart: 3, of which 1 were waited for; matrix products, arithmetic and copies ran while one was open for 0% of the time, Pallas kernels for 3%

profile of v1, /device:TPU:1, one launch (start us, length us, event | category | flops | bytes accessed | tf_op | source)
XLA Modules:
  0.0 91.1 jit_solution(13119644137226738207)
XLA Ops:
  0.7 0.1 pad.2.clone
  0.7 0.1 pad.3.clone
  0.8 0.7 convert_element_type.6
  1.5 0.1 copy.17
  1.6 0.7 copy.15
  2.3 0.1 copy.16
  2.4 0.7 maximum_maximum_fusion.table_ref.own_ref
  3.1 0.0 copy-start.1
  3.1 4.5 %project.1 = f32[8,40,128]{2,1,0:T(8,128)} custom-call(bf16[5,512,256]{2,1,0:T(8,128)(2,1)} %bitcast.7, bf16[5,512,128]{2,1,0:T(8,128)(2,1)} %bitcast.8, f32[16,128]{1,0:T(8,128)} %maximum_maximum_fusion.table_ref.own_ref), custom_call_target="tpu_custom_call" | custom-call | tf_op jit(solution)/shard_map/project/pallas_call | solution.py:53
  7.6 10.2 %all-to-all-start = ((f32[8,40,128]{2,1,0:T(8,128)}), f32[8,40,128]{2,1,0:T(8,128)S(1)}, u32[]{:S(2)}, u32[]{:S(2)}) async-start(f32[8,40,128]{2,1,0:T(8,128)} %project.1), calls=%async_computation | async-start | bytes 327680 | tf_op jit(solution)/shard_map/all_to_all | solution.py:238
  17.7 0.0 copy-done.1
  17.7 2.0 %collective-permute-start.1 = (f32[16,128]{1,0:T(8,128)S(1)}, f32[16,128]{1,0:T(8,128)S(1)}, u32[]{:S(2)}, u32[]{:S(2)}) collective-permute-start(f32[16,128]{1,0:T(8,128)S(1)} %copy-done.1), channel_id=1, source_target_pairs={{4,0},{8,4},{12,8},{16,12},{20,16},{24,20},{28,24},{32,28},{36,32}... | collective-permute-start | bytes 24584 | tf_op jit(solution)/shard_map/ppermute | solution.py:236
  19.8 3.5 %collective-permute-start = (f32[16,128]{1,0:T(8,128)S(1)}, f32[16,128]{1,0:T(8,128)S(1)}, u32[]{:S(2)}, u32[]{:S(2)}) collective-permute-start(f32[16,128]{1,0:T(8,128)S(1)} %copy-done.1), channel_id=1, source_target_pairs={{0,4},{4,8},{8,12},{12,16},{16,20},{20,24},{24,28},{28,32},{32,36}... | collective-permute-start | bytes 24584 | tf_op jit(solution)/shard_map/ppermute | solution.py:235
  23.3 0.0 collective-permute-done.1.high_ref
  23.3 0.0 copy-start.2
  23.3 0.8 collective-permute-done.low_ref
  24.1 0.0 copy-start.3
  24.1 0.0 copy-done.2
  24.1 0.6 copy-done.3
  24.7 3.1 %sample.1.b_ref = f32[16,16,128]{2,1,0:T(8,128)} custom-call(f32[16,128]{1,0:T(8,128)} %copy-done.3, f32[16,128]{1,0:T(8,128)} %maximum_maximum_fusion.table_ref.own_ref, f32[16,128]{1,0:T(8,128)} %copy-done.2, bf16[5,512,256]{2,1,0:T(8,128)(2,1)} %bitcast.6), custom_call_target="tpu_custom_call" | custom-call | tf_op jit(solution)/shard_map/sample/pallas_call | solution.py:110
  27.8 0.0 all-to-all-done.g_ref
  27.8 0.0 copy-start
  27.8 0.7 copy-done
  28.5 1.8 %merge.1 = f32[16,48,128]{2,1,0:T(8,128)} custom-call(f32[8,40,128]{2,1,0:T(8,128)} %copy-done, f32[16,16,128]{2,1,0:T(8,128)} %sample.1.b_ref), custom_call_target="tpu_custom_call" | custom-call | tf_op jit(solution)/shard_map/merge/pallas_call | solution.py:131
  30.2 26.4 %all_to_all.15.x_ref = f32[16,48,128]{2,1,0:T(8,128)} all-to-all(f32[16,48,128]{2,1,0:T(8,128)} %merge.1), channel_id=1, replica_groups=mesh['z'=16,'x'=4,'c'=2,'y'=4] {'z'}, dimensions={0} | all-to-all | bytes 786432 | tf_op jit(solution)/shard_map/all_to_all | solution.py:240
  56.6 3.2 %fold.1 = f32[32,16,128]{2,1,0:T(8,128)} custom-call(f32[16,48,128]{2,1,0:T(8,128)} %all_to_all.15.x_ref, f32[128,512]{1,0:T(8,128)} %s_ref.1), custom_call_target="tpu_custom_call" | custom-call | tf_op jit(solution)/shard_map/fold/pallas_call | solution.py:191
  59.8 28.3 %all_to_all.16.x_ref = f32[32,16,128]{2,1,0:T(8,128)} all-to-all(f32[32,16,128]{2,1,0:T(8,128)} %fold.1), channel_id=1, replica_groups=mesh['z'=16,'x'=4,'c'=2,'y'=4] {'x','c','y'}, dimensions={0} | all-to-all | bytes 524288 | tf_op jit(solution)/shard_map/all_to_all | solution.py:241
  88.0 1.7 %finish.1 = f32[64,2]{1,0:T(8,128)} custom-call(f32[32,16,128]{2,1,0:T(8,128)} %all_to_all.16.x_ref), custom_call_target="tpu_custom_call" | custom-call | tf_op jit(solution)/shard_map/finish/pallas_call | solution.py:214
  89.7 1.4 %copy.18 = f32[64,2]{0,1:T(2,128)} copy(f32[64,2]{1,0:T(8,128)} %finish.1) | data formatting | bytes 1024 | tf_op jit(solution)/shard_map/finish/pallas_call | solution.py:214
  (2 shorter events, 0.0 us)
Async XLA Ops:
  3.1 14.7 %copy-start.1 = (f32[16,128]{1,0:T(8,128)S(1)}, f32[16,128]{1,0:T(8,128)}, u32[]{:S(2)}) copy-start(f32[16,128]{1,0:T(8,128)} %maximum_maximum_fusion.table_ref.own_ref) | copy-start | bytes 24580
  7.6 20.2 %all-to-all-start = ((f32[8,40,128]{2,1,0:T(8,128)}), f32[8,40,128]{2,1,0:T(8,128)S(1)}, u32[]{:S(2)}, u32[]{:S(2)}) async-start(f32[8,40,128]{2,1,0:T(8,128)} %project.1), calls=%async_computation | async-start | bytes 327680 | tf_op jit(solution)/shard_map/all_to_all | solution.py:238
  17.7 5.6 %collective-permute-start.1 = (f32[16,128]{1,0:T(8,128)S(1)}, f32[16,128]{1,0:T(8,128)S(1)}, u32[]{:S(2)}, u32[]{:S(2)}) collective-permute-start(f32[16,128]{1,0:T(8,128)S(1)} %copy-done.1), channel_id=1, source_target_pairs={{4,0},{8,4},{12,8},{16,12},{20,16},{24,20},{28,24},{32,28},{36,32}... | collective-permute-start | bytes 24584 | tf_op jit(solution)/shard_map/ppermute | solution.py:236
  19.8 4.3 %collective-permute-start = (f32[16,128]{1,0:T(8,128)S(1)}, f32[16,128]{1,0:T(8,128)S(1)}, u32[]{:S(2)}, u32[]{:S(2)}) collective-permute-start(f32[16,128]{1,0:T(8,128)S(1)} %copy-done.1), channel_id=1, source_target_pairs={{0,4},{4,8},{8,12},{12,16},{16,20},{20,24},{24,28},{28,32},{32,36}... | collective-permute-start | bytes 24584 | tf_op jit(solution)/shard_map/ppermute | solution.py:235
  23.3 0.8 copy-start.2
  24.1 0.6 copy-start.3
  27.8 0.7 copy-start

commit v2 on v1

v2 whole, which is shorter than its diff:
```python
import jax
import jax.numpy as jnp
from jax import lax
from jax.experimental import pallas as pl
from jax.experimental.pallas import tpu as pltpu
from jax.sharding import Mesh
from jax.sharding import PartitionSpec as P

ROWS = ("z", "x", "c")
PLANE = ("x", "c")
CUBE = ("x", "c", "y")
F32 = jnp.float32
BF16 = jnp.bfloat16
NC, NB = 5, 7
NBR, CNT = 40, 47
PLANE_CNT, LOW_CNT, OWN_CNT, RANK, G_EXP, B_EXP = 96, 104, 105, 106, 107, 108
TOP = 32000.0
FINE = 65536.0


def whole(shape):
    return pl.BlockSpec(shape, lambda *_: (0,) * len(shape))


def lanes(shape):
    return lax.broadcasted_iota(jnp.int32, shape, len(shape) - 1)


def exponent(x):
    top = jnp.max(jnp.abs(x), axis=(0, 1), keepdims=True)
    return jnp.floor(-jnp.log2(jnp.maximum(top, 1e-30)))


def nearest(x):
    return jnp.floor(x + 0.5)


def to_i16(x):
    return x.astype(jnp.int32).astype(jnp.int16)


def from_i16(x):
    return x.astype(jnp.int32).astype(F32)


def table_kernel(jac_ref, nbr_ref, count_ref, out_ref):
    blank = jnp.zeros((1, 16), F32)
    rows = []
    for j in range(NC):
        rows += [jac_ref[j], blank]
    count = jnp.full((1, 16), count_ref[0].astype(F32))
    rows += [nbr_ref[...].astype(F32), count]
    table = jnp.concatenate(rows + [jnp.zeros((80, 16), F32)], axis=0)
    table = jnp.concatenate([table, jnp.zeros((128, 112), F32)], axis=1)
    out_ref[...] = table.T[0:16, :]


def make_table(jac, nbr, counts):
    return pl.pallas_call(
        table_kernel,
        in_specs=[
            pl.BlockSpec(memory_space=pltpu.VMEM),
            pl.BlockSpec(memory_space=pltpu.VMEM),
            pl.BlockSpec(memory_space=pltpu.SMEM),
        ],
        out_shape=jax.ShapeDtypeStruct((16, 128), F32),
        name="table",
    )(jac, nbr, counts)


def project_kernel(v_ref, d_ref, count_ref, out_ref, acc_ref):
    step = pl.program_id(0)
    part = lax.dot_general(
        d_ref[0], v_ref[0], (((0,), (0,)), ((), ())), preferred_element_type=F32
    )

    @pl.when(step == 0)
    def _():
        acc_ref[...] = part

    @pl.when(step > 0)
    def _():
        acc_ref[...] += part

    @pl.when(step == NC - 1)
    def _():
        g = acc_ref[...].T
        count = jnp.full((8, 128), count_ref[0].astype(F32))
        for p in range(8):
            for m in range(4):
                row = 64 * m + 8 * p
                out_ref[p, 8 * m : 8 * m + 8, :] = g[row : row + 8, :]
            out_ref[p, 32:40, :] = count


def project(test, deim, counts):
    return pl.pallas_call(
        project_kernel,
        grid=(NC,),
        in_specs=[
            pl.BlockSpec((1, 512, 256), lambda j: (j, 0, 0)),
            pl.BlockSpec((1, 512, 128), lambda j: (j, 0, 0)),
            pl.BlockSpec(memory_space=pltpu.SMEM),
        ],
        out_specs=whole((8, 40, 128)),
        out_shape=jax.ShapeDtypeStruct((8, 40, 128), F32),
        scratch_shapes=[pltpu.VMEM((128, 256), F32)],
        name="project",
        cost_estimate=pl.CostEstimate(
            flops=2 * 2560 * 256 * 128, bytes_accessed=2 * 2560 * 384, transcendentals=0
        ),
    )(test, deim, counts)


def sample_kernel(low_ref, own_ref, high_ref, u_ref, out_ref):
    rank = jnp.floor(own_ref[0:1, NBR : NBR + 1] * (1.0 / 512.0))
    slot = lax.broadcasted_iota(jnp.int32, (16, 128), 0).astype(F32)
    entry = lanes((16, 128)) < NBR
    tables = []
    for ref in (low_ref, own_ref, high_ref):
        rows = ref[...]
        dead = entry & (slot >= rows[:, CNT : CNT + 1])
        tables.append(jnp.where(dead, 0.0, rows))
    table = jnp.concatenate(tables, axis=0)
    near = [table[:, NBR + n : NBR + n + 1] - rank * 512.0 for n in range(NB)]
    total = jnp.zeros((144, 256), F32)
    values = [jnp.broadcast_to(table[:, k : k + 1], (48, 128)) for k in range(NBR)]
    for chunk in range(4):
        cell = (lanes((48, 128)) + 128 * chunk).astype(F32)
        hits = [cell == near[n] for n in range(NB)]
        for j in range(NC):
            weight = jnp.where(hits[0], values[8 * j], 0.0)
            for n in range(1, NB):
                weight = weight + jnp.where(hits[n], values[8 * j + n], 0.0)
            w0 = weight.astype(BF16)
            rest = weight - w0.astype(F32)
            w1 = rest.astype(BF16)
            w2 = (rest - w1.astype(F32)).astype(BF16)
            stacked = jnp.concatenate([w0, w1, w2], axis=0)
            total = total + jnp.dot(
                stacked,
                u_ref[j, 128 * chunk : 128 * chunk + 128, :],
                preferred_element_type=F32,
            )
    rows = total[0:48, :] + (total[48:96, :] + total[96:144, :])
    exp = exponent(rows)
    rows = rows * (jnp.exp2(exp) * TOP)
    coarse = nearest(rows)
    fine = jnp.clip(nearest((rows - coarse) * FINE), -32767.0, 32767.0)
    rows = jnp.concatenate([coarse, fine, jnp.zeros((32, 256), F32)], axis=0)
    lane = lanes((1, 128))
    extra = jnp.where(lane == LOW_CNT, low_ref[0:1, CNT : CNT + 1], 0.0)
    extra = extra + jnp.where(lane == OWN_CNT, own_ref[0:1, CNT : CNT + 1], 0.0)
    extra = extra + jnp.where(lane == RANK, rank, 0.0)
    extra = extra + jnp.where(lane == B_EXP, exp, 0.0)
    cols = rows.T + extra
    for z in range(16):
        out_ref[z, :, :] = cols[16 * z : 16 * z + 16, :]


def sample(low, own, high, trial):
    return pl.pallas_call(
        sample_kernel,
        out_shape=jax.ShapeDtypeStruct((16, 16, 128), F32),
        name="sample",
    )(low, own, high, trial)


def merge_kernel(g_ref, b_ref, out_ref):
    total = g_ref[0, 0:32, :]
    for p in range(1, 8):
        total = total + g_ref[p, 0:32, :]
    exp = exponent(total)
    share = jnp.abs(total * jnp.exp2(exp))
    code = nearest(jnp.sqrt(jnp.sqrt(share)) * TOP)
    code = to_i16(jnp.where(total < 0.0, -code, code))
    lane = lanes((1, 128))
    extra = jnp.where(lane == G_EXP, exp, 0.0)
    for p in range(8):
        extra = extra + jnp.where(lane == PLANE_CNT + p, g_ref[p, 32:33, :], 0.0)
    for z in range(16):
        out_ref[z, 0:32, :] = code
        out_ref[z, 32:48, :] = to_i16(b_ref[z, :, :] + extra)


def merge(g_parts, columns):
    return pl.pallas_call(
        merge_kernel,
        out_shape=jax.ShapeDtypeStruct((16, 48, 128), jnp.int16),
        name="merge",
    )(g_parts, columns)


def fold_kernel(x_ref, s_ref, out_ref):
    blocks = [from_i16(x_ref[z, 32:48, :]) for z in range(16)]
    info = jnp.concatenate([block[0:1, :] for block in blocks], axis=0)
    lane = lanes((16, 128))

    def column(k):
        return jnp.sum(jnp.where(lane == k, info, 0.0), axis=1, keepdims=True)

    g_scale = jnp.exp2(-column(G_EXP))
    b_scale = jnp.exp2(-column(B_EXP)) * (1.0 / TOP)
    total = jnp.zeros((32, 128), F32)
    for z in range(16):
        root = from_i16(x_ref[z, 0:32, :]) * (1.0 / TOP)
        square = root * root
        total = total + square * square * jnp.where(root < 0.0, -1.0, 1.0) * g_scale[z : z + 1, :]
    rank = column(RANK)
    place = rank - 8.0 * jnp.floor(rank * 0.125)
    is_count = (lane >= PLANE_CNT) & (lane < PLANE_CNT + 8)
    counts = jnp.where(is_count, info, 0.0)
    before = lax.broadcasted_iota(jnp.int32, (16, 16), 1) < lax.broadcasted_iota(
        jnp.int32, (16, 16), 0
    )
    lower = jnp.dot(before.astype(F32), counts, preferred_element_type=F32)
    ahead = (lane - PLANE_CNT).astype(F32) < place
    lower = lower + jnp.where(ahead, counts, 0.0)
    offset = jnp.sum(lower, axis=1, keepdims=True)
    slot = jnp.where(lane < 48, lane, lane - 48)
    shift = jnp.where(slot < 16, -column(LOW_CNT), jnp.where(slot < 32, 0.0, column(OWN_CNT)))
    ids = offset + shift + (lane % 16).astype(F32)
    ids = jnp.where(lane < 96, ids, -1.0)
    unit = jnp.where(lane < 48, 1.0, jnp.where(lane < 96, 1.0 / FINE, 0.0))
    mode = lax.broadcasted_iota(jnp.int32, (512, 128), 0).astype(F32)
    sampled = jnp.zeros((16, 512), F32)
    for z in range(16):
        hot = jnp.where(mode == ids[z : z + 1, :], 1.0, 0.0).astype(BF16)
        cols = blocks[z] * unit
        high = cols.astype(BF16)
        rest = (cols - high.astype(F32)).astype(BF16)
        part = lax.dot_general(
            jnp.concatenate([high, rest], axis=0),
            hot,
            (((1,), (1,)), ((), ())),
            preferred_element_type=F32,
        )
        sampled = sampled + (part[0:16, :] + part[16:32, :]) * b_scale[z : z + 1, :]
    c = lax.dot_general(
        sampled,
        s_ref[...],
        (((1,), (1,)), ((), ())),
        precision=lax.Precision.HIGHEST,
        preferred_element_type=F32,
    )
    g_pairs = total.reshape(16, 2, 128)
    c_pairs = c.reshape(8, 2, 128)
    for p in range(8):
        for m in range(4):
            at = 5 * (4 * p + m)
            out_ref[at : at + 4] = g_pairs[4 * m : 4 * m + 4]
            out_ref[at + 4] = c_pairs[p]


def fold(parts, inverse):
    return pl.pallas_call(
        fold_kernel,
        out_shape=jax.ShapeDtypeStruct((160, 2, 128), F32),
        name="fold",
    )(parts, inverse)


def finish_kernel(x_ref, out_ref):
    result = jnp.zeros((2, 64), F32)
    for m in range(4):
        rows = [x_ref[5 * (4 * p + m) : 5 * (4 * p + m) + 4].reshape(8, 128) for p in range(8)]
        c = x_ref[5 * m + 4]
        for p in range(1, 8):
            c = c + x_ref[5 * (4 * p + m) + 4]
        result = result + lax.dot_general(
            c,
            jnp.concatenate(rows, axis=0),
            (((1,), (1,)), ((), ())),
            precision=lax.Precision.HIGHEST,
            preferred_element_type=F32,
        )
    out_ref[...] = result


def finish(parts):
    return pl.pallas_call(
        finish_kernel,
        out_shape=jax.ShapeDtypeStruct((2, 64), F32),
        name="finish",
    )(parts)


def shards(test_basis, deim_basis, trial_basis, jacobian, neighbours, counts, sample_inverse):
    own = make_table(jacobian.transpose(2, 1, 0), neighbours.T, counts)
    groups = lax.axis_size(ROWS)
    up = [(i, i + 1) for i in range(groups - 1)]
    down = [(i + 1, i) for i in range(groups - 1)]
    low = lax.ppermute(own, ROWS, up)
    high = lax.ppermute(own, ROWS, down)
    g_part = project(test_basis.swapaxes(0, 1), deim_basis.swapaxes(0, 1), counts)
    g_part, low, high = lax.optimization_barrier((g_part, low, high))
    g_plane = lax.all_to_all(g_part, PLANE, 0, 0, tiled=True)
    columns = sample(low, own, high, trial_basis.swapaxes(0, 1))
    parts = lax.all_to_all(merge(g_plane, columns), "z", 0, 0, tiled=True)
    pieces = lax.all_to_all(fold(parts, sample_inverse), CUBE, 0, 0, tiled=True)
    return finish(pieces).T


def solution(mesh):
    split = Mesh(mesh.devices.reshape(16, 4, 2, 4), ("z", "x", "c", "y"))
    placed = (
        P(ROWS, None, None),
        P(ROWS, None, "y"),
        P(ROWS, None, None),
        P(ROWS, None, None),
        P(ROWS, None),
        P(ROWS),
        P("y", None),
    )
    return jax.shard_map(
        shards, mesh=split, in_specs=placed, out_specs=P("y", ROWS), check_vma=False
    )
```

time: 91.8 us -> 78.5 us (0.86)
  blocking collectives: 54.6 us -> 43.8 us
  local copies, waits for them, and re-layouts: 3.71 us -> 0.68 us
  Pallas kernels: 14.2 us -> 16 us
  waiting for transfers between devices: 0.76 us -> 2.29 us
  other arithmetic: 1.37 us -> 0 us
  starting transfers between devices: 15.7 us -> 14.5 us
    all_to_all x1, blocking collectives: 28.3 us -> 18.3 us  [shards(): pieces = lax.all_to_all(fold(parts, sample_inverse), CUBE, 0, 0, tiled=True)]
    ppermute x1, starting transfers between devices: 2.02 us -> 8.77 us  [shards(): high = lax.ppermute(own, ROWS, down)]
    all_to_all x1, starting transfers between devices: 10.2 us -> 3.79 us  [shards(): g_plane = lax.all_to_all(g_part, PLANE, 0, 0, tiled=True)]
    all_to_all x1, waiting for transfers between devices: 0.01 us -> 2.29 us  [shards(): g_plane = lax.all_to_all(g_part, PLANE, 0, 0, tiled=True)]
    ppermute x1, starting transfers between devices: 3.53 us -> 1.92 us  [shards(): low = lax.ppermute(own, ROWS, up)]
    pallas_call x2 -> x3, Pallas kernels: 4.84 us -> 6.34 us  [the longest x1 3.14 us: fold(): pl.pallas_call(fold_kernel, out_shape=jax.ShapeDtypeStruct((160, 2, 128),...]
    pallas_call x1 -> x0, local copies, waits for them, and re-layouts: 1.39 us -> none  [finish(): pl.pallas_call(finish_kernel, out_shape=jax.ShapeDtypeStruct((64, 2), F32...]
    unnamed x9 -> x6, local copies, waits for them, and re-layouts: 2 us -> 0.68 us
  transfers between devices with their start and end apart: 3 -> 3, of which waited for: 1 -> 1; matrix products, arithmetic and copies ran while one was open for 0% -> 0% of each run, Pallas kernels for 3% -> 10%
where the time goes in v2:
time: 78.5 us; the launch traced here: 77.9 us
  blocking collectives  43.8 us (56%)
  Pallas kernels  16 us (20%)
  starting transfers between devices  14.5 us (18%)
  waiting for transfers between devices  2.29 us (3%)
    all_to_all x1, blocking collectives, shards(): parts = lax.all_to_all(merge(g_plane, columns), 'z', 0, 0, tiled=True)  25.5 us
    all_to_all x1, blocking collectives, shards(): pieces = lax.all_to_all(fold(parts, sample_inverse), CUBE, 0, 0, tiled=True)  18.3 us
    ppermute x1, starting transfers between devices, shards(): high = lax.ppermute(own, ROWS, down)  8.77 us
    pallas_call x1, Pallas kernels, project(): pl.pallas_call(project_kernel, grid=(NC,), in_specs=[pl.BlockSpec((1, 512...  4.48 us
    all_to_all x1, starting transfers between devices, shards(): g_plane = lax.all_to_all(g_part, PLANE, 0, 0, tiled=True)  3.79 us
    pallas_call x1, Pallas kernels, sample(): pl.pallas_call(sample_kernel, out_shape=jax.ShapeDtypeStruct((16, 16, 128...  3.3 us
    pallas_call x1, Pallas kernels, fold(): pl.pallas_call(fold_kernel, out_shape=jax.ShapeDtypeStruct((160, 2, 128),...  3.14 us
    all_to_all x1, waiting for transfers between devices, shards(): g_plane = lax.all_to_all(g_part, PLANE, 0, 0, tiled=True)  2.29 us
  transfers between devices with their start and end apart: 3, of which 1 were waited for; matrix products, arithmetic and copies ran while one was open for 0% of the time, Pallas kernels for 10%

profile of v2, /device:TPU:1, one launch (start us, length us, event | category | flops | bytes accessed | tf_op | source)
XLA Modules:
  0.0 77.9 jit_solution(15814711092533033179)
XLA Ops:
  0.7 1.4 %table.1.own_ref = f32[16,128]{1,0:T(8,128)} custom-call(f32[5,7,16]{2,1,0:T(8,128)} %bitcast.9, s32[7,16]{1,0:T(8,128)} %bitcast.10, s32[1]{0:T(128)S(6)} %copy.8.count_ref), custom_call_target="tpu_custom_call" | custom-call | tf_op jit(solution)/shard_map/table/pallas_call | solution.py:59
  2.0 8.8 %collective-permute-start.1 = (f32[16,128]{1,0:T(8,128)}, f32[16,128]{1,0:T(8,128)S(1)}, u32[]{:S(2)}, u32[]{:S(2)}) collective-permute-start(f32[16,128]{1,0:T(8,128)} %table.1.own_ref), channel_id=1, source_target_pairs={{4,0},{8,4},{12,8},{16,12},{20,16},{24,20},{28,24},{32,28},{36,32}... | collective-permute-start | bytes 24584 | tf_op jit(solution)/shard_map/ppermute | solution.py:294
  10.8 1.9 %collective-permute-start = (f32[16,128]{1,0:T(8,128)}, f32[16,128]{1,0:T(8,128)S(1)}, u32[]{:S(2)}, u32[]{:S(2)}) collective-permute-start(f32[16,128]{1,0:T(8,128)} %table.1.own_ref), channel_id=1, source_target_pairs={{0,4},{4,8},{8,12},{12,16},{16,20},{20,24},{24,28},{28,32},{32,36}... | collective-permute-start | bytes 24584 | tf_op jit(solution)/shard_map/ppermute | solution.py:293
  12.8 4.5 %project.1 = f32[8,40,128]{2,1,0:T(8,128)} custom-call(bf16[5,512,256]{2,1,0:T(8,128)(2,1)} %bitcast.6, bf16[5,512,128]{2,1,0:T(8,128)(2,1)} %bitcast.8, s32[1]{0:T(128)S(6)} %copy.8.count_ref), custom_call_target="tpu_custom_call" | custom-call | flops 167772160 | bytes 1966080 | tf_op jit(solution)/shard_map/project/pallas_call | solution.py:97
  17.2 0.0 collective-permute-done.1.high_ref
  17.2 0.0 copy-start.1
  17.2 0.0 collective-permute-done.low_ref
  17.2 0.0 copy-start.2
  17.3 3.8 %all-to-all-start = ((f32[8,40,128]{2,1,0:T(8,128)}), f32[8,40,128]{2,1,0:T(8,128)S(1)}, u32[]{:S(2)}, u32[]{:S(2)}) async-start(f32[8,40,128]{2,1,0:T(8,128)} %project.1), calls=%async_computation | async-start | bytes 327680 | tf_op jit(solution)/shard_map/all_to_all | solution.py:297
  21.0 0.0 copy-done.1
  21.0 0.0 copy-done.2
  21.1 3.3 %sample.1.b_ref = f32[16,16,128]{2,1,0:T(8,128)} custom-call(f32[16,128]{1,0:T(8,128)} %copy-done.2, f32[16,128]{1,0:T(8,128)} %table.1.own_ref, f32[16,128]{1,0:T(8,128)} %copy-done.1, bf16[5,512,256]{2,1,0:T(8,128)(2,1)} %bitcast.7), custom_call_target="tpu_custom_call" | custom-call | tf_op jit(solution)/shard_map/sample/pallas_call | solution.py:162
  24.4 2.3 %all-to-all-done.g_ref = f32[8,40,128]{2,1,0:T(8,128)S(1)} async-done(((f32[8,40,128]{2,1,0:T(8,128)}), f32[8,40,128]{2,1,0:T(8,128)S(1)}, u32[]{:S(2)}, u32[]{:S(2)}) %all-to-all-start) | async-done | bytes 163872 | tf_op jit(solution)/shard_map/all_to_all | solution.py:297
  26.6 0.0 copy-start
  26.6 0.7 copy-done
  27.3 1.8 %merge.1 = s16[16,48,128]{2,1,0:T(8,128)(2,1)} custom-call(f32[8,40,128]{2,1,0:T(8,128)} %copy-done, f32[16,16,128]{2,1,0:T(8,128)} %sample.1.b_ref), custom_call_target="tpu_custom_call" | custom-call | tf_op jit(solution)/shard_map/merge/pallas_call | solution.py:187
  29.2 25.5 %all_to_all.15.x_ref = s16[16,48,128]{2,1,0:T(8,128)(2,1)} all-to-all(s16[16,48,128]{2,1,0:T(8,128)(2,1)} %merge.1), channel_id=1, replica_groups=mesh['z'=16,'x'=4,'c'=2,'y'=4] {'z'}, dimensions={0} | all-to-all | bytes 393216 | tf_op jit(solution)/shard_map/all_to_all | solution.py:299
  54.7 3.1 %fold.1 = f32[160,2,128]{2,1,0:T(2,128)} custom-call(s16[16,48,128]{2,1,0:T(8,128)(2,1)} %all_to_all.15.x_ref, f32[128,512]{1,0:T(8,128)} %s_ref.1), custom_call_target="tpu_custom_call" | custom-call | tf_op jit(solution)/shard_map/fold/pallas_call | solution.py:256
  57.8 18.3 %all_to_all.16.x_ref = f32[160,2,128]{2,1,0:T(2,128)} all-to-all(f32[160,2,128]{2,1,0:T(2,128)} %fold.1), channel_id=1, replica_groups=mesh['z'=16,'x'=4,'c'=2,'y'=4] {'x','c','y'}, dimensions={0} | all-to-all | bytes 327680 | tf_op jit(solution)/shard_map/all_to_all | solution.py:300
  76.1 1.8 %finish.1 = f32[2,64]{1,0:T(2,128)} custom-call(f32[160,2,128]{2,1,0:T(2,128)} %all_to_all.16.x_ref), custom_call_target="tpu_custom_call" | custom-call | tf_op jit(solution)/shard_map/finish/pallas_call | solution.py:281
Async XLA Ops:
  2.0 15.2 %collective-permute-start.1 = (f32[16,128]{1,0:T(8,128)}, f32[16,128]{1,0:T(8,128)S(1)}, u32[]{:S(2)}, u32[]{:S(2)}) collective-permute-start(f32[16,128]{1,0:T(8,128)} %table.1.own_ref), channel_id=1, source_target_pairs={{4,0},{8,4},{12,8},{16,12},{20,16},{24,20},{28,24},{32,28},{36,32}... | collective-permute-start | bytes 24584 | tf_op jit(solution)/shard_map/ppermute | solution.py:294
  10.8 6.4 %collective-permute-start = (f32[16,128]{1,0:T(8,128)}, f32[16,128]{1,0:T(8,128)S(1)}, u32[]{:S(2)}, u32[]{:S(2)}) collective-permute-start(f32[16,128]{1,0:T(8,128)} %table.1.own_ref), channel_id=1, source_target_pairs={{0,4},{4,8},{8,12},{12,16},{16,20},{20,24},{24,28},{28,32},{32,36}... | collective-permute-start | bytes 24584 | tf_op jit(solution)/shard_map/ppermute | solution.py:293
  17.2 3.8 %copy-start.1 = (f32[16,128]{1,0:T(8,128)}, f32[16,128]{1,0:T(8,128)S(1)}, u32[]{:S(2)}) copy-start(f32[16,128]{1,0:T(8,128)S(1)} %collective-permute-done.1.high_ref) | copy-start | bytes 24580
  17.2 3.8 %copy-start.2 = (f32[16,128]{1,0:T(8,128)}, f32[16,128]{1,0:T(8,128)S(1)}, u32[]{:S(2)}) copy-start(f32[16,128]{1,0:T(8,128)S(1)} %collective-permute-done.low_ref) | copy-start | bytes 24580
  17.3 9.4 %all-to-all-start = ((f32[8,40,128]{2,1,0:T(8,128)}), f32[8,40,128]{2,1,0:T(8,128)S(1)}, u32[]{:S(2)}, u32[]{:S(2)}) async-start(f32[8,40,128]{2,1,0:T(8,128)} %project.1), calls=%async_computation | async-start | bytes 327680 | tf_op jit(solution)/shard_map/all_to_all | solution.py:297
  26.6 0.7 copy-start

commit v3 on v2

--- a/solution.py
+++ b/solution.py
@@ -18,8 +18,9 @@
 FINE = 65536.0
 
 
-def whole(shape):
-    return pl.BlockSpec(shape, lambda *_: (0,) * len(shape))
+VMEM = pl.BlockSpec(memory_space=pltpu.VMEM)
+SMEM = pl.BlockSpec(memory_space=pltpu.SMEM)
+PARAMS = pltpu.CompilerParams(vmem_limit_bytes=12 * 1024 * 1024)
 
 
 def lanes(shape):
@@ -58,53 +59,36 @@
 def make_table(jac, nbr, counts):
     return pl.pallas_call(
         table_kernel,
-        in_specs=[
-            pl.BlockSpec(memory_space=pltpu.VMEM),
-            pl.BlockSpec(memory_space=pltpu.VMEM),
-            pl.BlockSpec(memory_space=pltpu.SMEM),
-        ],
+        in_specs=[VMEM, VMEM, SMEM],
         out_shape=jax.ShapeDtypeStruct((16, 128), F32),
+        out_specs=VMEM,
+        compiler_params=PARAMS,
         name="table",
     )(jac, nbr, counts)
 
 
-def project_kernel(v_ref, d_ref, count_ref, out_ref, acc_ref):
-    step = pl.program_id(0)
-    part = lax.dot_general(
-        d_ref[0], v_ref[0], (((0,), (0,)), ((), ())), preferred_element_type=F32
-    )
-
-    @pl.when(step == 0)
-    def _():
-        acc_ref[...] = part
-
-    @pl.when(step > 0)
-    def _():
-        acc_ref[...] += part
-
-    @pl.when(step == NC - 1)
-    def _():
-        g = acc_ref[...].T
-        count = jnp.full((8, 128), count_ref[0].astype(F32))
-        for p in range(8):
-            for m in range(4):
-                row = 64 * m + 8 * p
-                out_ref[p, 8 * m : 8 * m + 8, :] = g[row : row + 8, :]
-            out_ref[p, 32:40, :] = count
+def project_kernel(v_ref, d_ref, count_ref, out_ref):
+    acc = jnp.zeros((128, 256), F32)
+    for j in range(NC):
+        acc = acc + lax.dot_general(
+            d_ref[j], v_ref[j], (((0,), (0,)), ((), ())), preferred_element_type=F32
+        )
+    g = acc.T
+    count = jnp.full((8, 128), count_ref[0].astype(F32))
+    for p in range(8):
+        for m in range(4):
+            row = 64 * m + 8 * p
+            out_ref[p, 8 * m : 8 * m + 8, :] = g[row : row + 8, :]
+        out_ref[p, 32:40, :] = count
 
 
 def project(test, deim, counts):
     return pl.pallas_call(
         project_kernel,
-        grid=(NC,),
-        in_specs=[
-            pl.BlockSpec((1, 512, 256), lambda j: (j, 0, 0)),
-            pl.BlockSpec((1, 512, 128), lambda j: (j, 0, 0)),
-            pl.BlockSpec(memory_space=pltpu.SMEM),
-        ],
-        out_specs=whole((8, 40, 128)),
+        in_specs=[VMEM, VMEM, SMEM],
+        out_specs=VMEM,
         out_shape=jax.ShapeDtypeStruct((8, 40, 128), F32),
-        scratch_shapes=[pltpu.VMEM((128, 256), F32)],
+        compiler_params=PARAMS,
         name="project",
         cost_estimate=pl.CostEstimate(
             flops=2 * 2560 * 256 * 128, bytes_accessed=2 * 2560 * 384, transcendentals=0
@@ -162,6 +146,9 @@
     return pl.pallas_call(
         sample_kernel,
         out_shape=jax.ShapeDtypeStruct((16, 16, 128), F32),
+        in_specs=[VMEM] * 4,
+        out_specs=VMEM,
+        compiler_params=PARAMS,
         name="sample",
     )(low, own, high, trial)
 
@@ -187,6 +174,9 @@
     return pl.pallas_call(
         merge_kernel,
         out_shape=jax.ShapeDtypeStruct((16, 48, 128), jnp.int16),
+        in_specs=[VMEM] * 2,
+        out_specs=VMEM,
+        compiler_params=PARAMS,
         name="merge",
     )(g_parts, columns)
 
@@ -256,6 +246,9 @@
     return pl.pallas_call(
         fold_kernel,
         out_shape=jax.ShapeDtypeStruct((160, 2, 128), F32),
+        in_specs=[VMEM] * 2,
+        out_specs=VMEM,
+        compiler_params=PARAMS,
         name="fold",
     )(parts, inverse)
 
@@ -281,6 +274,9 @@
     return pl.pallas_call(
         finish_kernel,
         out_shape=jax.ShapeDtypeStruct((2, 64), F32),
+        in_specs=[VMEM] * 1,
+        out_specs=VMEM,
+        compiler_params=PARAMS,
         name="finish",
     )(parts)
 

time: 78.5 us -> 72.5 us (0.924)
  Pallas kernels: 16 us -> 4.92 us
  local copies, waits for them, and re-layouts: 0.68 us -> 3.81 us
  waiting for transfers between devices: 2.29 us -> 4.34 us
    pallas_call x2, Pallas kernels: 5.87 us -> 1.17 us  [the longest x1 1.11 us: project(): pl.pallas_call(project_kernel, in_specs=[VMEM, VMEM, SMEM], out_specs=VME...]
    unnamed x6 -> x12, local copies, waits for them, and re-layouts: 0.68 us -> 3.81 us
    pallas_call x1, Pallas kernels: 3.3 us -> 1.25 us  [sample(): pl.pallas_call(sample_kernel, out_shape=jax.ShapeDtypeStruct((16, 16, 128...]
    all_to_all x1, waiting for transfers between devices: 2.29 us -> 4.34 us  [shards(): g_plane = lax.all_to_all(g_part, PLANE, 0, 0, tiled=True)]
    pallas_call x1, Pallas kernels: 3.14 us -> 1.42 us  [fold(): pl.pallas_call(fold_kernel, out_shape=jax.ShapeDtypeStruct((160, 2, 128),...]
    pallas_call x1, Pallas kernels: 1.84 us -> 0.18 us  [merge(): pl.pallas_call(merge_kernel, out_shape=jax.ShapeDtypeStruct((16, 48, 128)...]
    pallas_call x1, Pallas kernels: 1.8 us -> 0.89 us  [finish(): pl.pallas_call(finish_kernel, out_shape=jax.ShapeDtypeStruct((2, 64), F32...]
  transfers between devices with their start and end apart: 3 -> 3, of which waited for: 1 -> 1; matrix products, arithmetic and copies ran while one was open for 0% -> 0% of each run, Pallas kernels for 10% -> 3%
where the time goes in v3:
time: 72.5 us; the launch traced here: 72 us
  blocking collectives  43.6 us (60%)
  starting transfers between devices  14.6 us (20%)
  Pallas kernels  4.92 us (7%)
  waiting for transfers between devices  4.34 us (6%)
  local copies, waits for them, and re-layouts  3.81 us (5%)
    all_to_all x1, blocking collectives, shards(): parts = lax.all_to_all(merge(g_plane, columns), 'z', 0, 0, tiled=True)  25.7 us
    all_to_all x1, blocking collectives, shards(): pieces = lax.all_to_all(fold(parts, sample_inverse), CUBE, 0, 0, tiled=True)  18 us
    ppermute x1, starting transfers between devices, shards(): high = lax.ppermute(own, ROWS, down)  8.78 us
    all_to_all x1, waiting for transfers between devices, shards(): g_plane = lax.all_to_all(g_part, PLANE, 0, 0, tiled=True)  4.34 us
    all_to_all x1, starting transfers between devices, shards(): g_plane = lax.all_to_all(g_part, PLANE, 0, 0, tiled=True)  3.92 us
    unnamed x12, local copies, waits for them, and re-layouts  3.81 us
    ppermute x1, starting transfers between devices, shards(): low = lax.ppermute(own, ROWS, up)  1.92 us
  transfers between devices with their start and end apart: 3, of which 1 were waited for; matrix products, arithmetic and copies ran while one was open for 0% of the time, Pallas kernels for 3%

profile of v3, /device:TPU:1, one launch (start us, length us, event | category | flops | bytes accessed | tf_op | source)
XLA Modules:
  0.0 72.0 jit_solution(4642341834304196215)
XLA Ops:
  0.7 0.0 copy-start.4
  0.7 0.7 copy-done.4
  1.4 0.0 copy-start.5
  1.4 0.7 copy-done.5
  2.1 0.1 table.1.own_ref
  2.1 8.8 %collective-permute-start.1 = (f32[16,128]{1,0:T(8,128)S(1)}, f32[16,128]{1,0:T(8,128)S(1)}, u32[]{:S(2)}, u32[]{:S(2)}) collective-permute-start(f32[16,128]{1,0:T(8,128)S(1)} %table.1.own_ref), channel_id=1, source_target_pairs={{4,0},{8,4},{12,8},{16,12},{20,16},{24,20},{28,24},{32,28},{36,32}... | collective-permute-start | bytes 24584 | tf_op jit(solution)/shard_map/ppermute | solution.py:290
  10.9 1.9 %collective-permute-start = (f32[16,128]{1,0:T(8,128)S(1)}, f32[16,128]{1,0:T(8,128)S(1)}, u32[]{:S(2)}, u32[]{:S(2)}) collective-permute-start(f32[16,128]{1,0:T(8,128)S(1)} %table.1.own_ref), channel_id=1, source_target_pairs={{0,4},{4,8},{8,12},{12,16},{16,20},{20,24},{24,28},{28,32},{32,36}... | collective-permute-start | bytes 24584 | tf_op jit(solution)/shard_map/ppermute | solution.py:289
  12.9 0.0 copy-start
  12.9 1.3 %copy-done = bf16[512,5,256]{2,0,1:T(8,128)(2,1)S(1)} copy-done((bf16[512,5,256]{2,0,1:T(8,128)(2,1)S(1)}, bf16[512,5,256]{2,0,1:T(8,128)(2,1)}, u32[]{:S(2)}) %copy-start) | copy-done | bytes 1310744
  14.2 0.0 copy-start.2
  14.2 1.1 %copy-done.2 = bf16[512,5,128]{2,0,1:T(8,128)(2,1)S(1)} copy-done((bf16[512,5,128]{2,0,1:T(8,128)(2,1)S(1)}, bf16[512,5,128]{2,0,1:T(8,128)(2,1)}, u32[]{:S(2)}) %copy-start.2) | copy-done | bytes 655384
  15.3 0.0 copy-start.1
  15.3 1.1 %project.1 = f32[8,40,128]{2,1,0:T(8,128)} custom-call(bf16[5,512,256]{2,1,0:T(8,128)(2,1)S(1)} %bitcast.6, bf16[5,512,128]{2,1,0:T(8,128)(2,1)S(1)} %bitcast.8, s32[1]{0:T(128)S(6)} %copy.8.count_ref), custom_call_target="tpu_custom_call" | custom-call | flops 167772160 | bytes 1966080 | tf_op jit(solution)/shard_map/project/pallas_call | solution.py:86
  16.4 0.0 copy-start.3
  16.4 0.0 collective-permute-done.1.high_ref
  16.4 0.0 collective-permute-done.low_ref
  16.4 3.9 %all-to-all-start = ((f32[8,40,128]{2,1,0:T(8,128)}), f32[8,40,128]{2,1,0:T(8,128)S(1)}, u32[]{:S(2)}, u32[]{:S(2)}) async-start(f32[8,40,128]{2,1,0:T(8,128)} %project.1), calls=%async_computation | async-start | bytes 327680 | tf_op jit(solution)/shard_map/all_to_all | solution.py:293
  20.3 0.0 copy-done.1
  20.3 1.3 %sample.1.b_ref = f32[16,16,128]{2,1,0:T(8,128)S(1)} custom-call(f32[16,128]{1,0:T(8,128)S(1)} %collective-permute-done.low_ref, f32[16,128]{1,0:T(8,128)S(1)} %table.1.own_ref, f32[16,128]{1,0:T(8,128)S(1)} %collective-permute-done.1.high_ref, bf16[5,512,256]{2,1,0:T(8,128)(2,1)S(1)} %bitcast.7), custom_call_target="tpu_custom_call" | custom-call | tf_op jit(solution)/shard_map/sample/pallas_call | solution.py:146
  21.6 4.3 %all-to-all-done.g_ref = f32[8,40,128]{2,1,0:T(8,128)S(1)} async-done(((f32[8,40,128]{2,1,0:T(8,128)}), f32[8,40,128]{2,1,0:T(8,128)S(1)}, u32[]{:S(2)}, u32[]{:S(2)}) %all-to-all-start) | async-done | bytes 163872 | tf_op jit(solution)/shard_map/all_to_all | solution.py:293
  25.9 0.2 merge.1
  26.1 25.7 %all_to_all.15.x_ref = s16[16,48,128]{2,1,0:T(8,128)(2,1)S(1)} all-to-all(s16[16,48,128]{2,1,0:T(8,128)(2,1)S(1)} %merge.1), channel_id=1, replica_groups=mesh['z'=16,'x'=4,'c'=2,'y'=4] {'z'}, dimensions={0} | all-to-all | bytes 393216 | tf_op jit(solution)/shard_map/all_to_all | solution.py:295
  51.7 0.0 copy-done.3
  51.8 1.4 %fold.1 = f32[160,2,128]{2,1,0:T(2,128)S(1)} custom-call(s16[16,48,128]{2,1,0:T(8,128)(2,1)S(1)} %all_to_all.15.x_ref, f32[128,512]{1,0:T(8,128)S(1)} %copy-done.3), custom_call_target="tpu_custom_call" | custom-call | tf_op jit(solution)/shard_map/fold/pallas_call | solution.py:246
  53.2 18.0 %all_to_all.16.x_ref = f32[160,2,128]{2,1,0:T(2,128)S(1)} all-to-all(f32[160,2,128]{2,1,0:T(2,128)S(1)} %fold.1), channel_id=1, replica_groups=mesh['z'=16,'x'=4,'c'=2,'y'=4] {'x','c','y'}, dimensions={0} | all-to-all | bytes 327680 | tf_op jit(solution)/shard_map/all_to_all | solution.py:296
  71.1 0.9 %finish.1 = f32[2,64]{1,0:T(2,128)} custom-call(f32[160,2,128]{2,1,0:T(2,128)S(1)} %all_to_all.16.x_ref), custom_call_target="tpu_custom_call" | custom-call | tf_op jit(solution)/shard_map/finish/pallas_call | solution.py:274
Async XLA Ops:
  0.7 0.7 %copy-start.4 = (f32[16,7,5]{0,1,2:T(8,128)S(1)}, f32[16,7,5]{0,1,2:T(8,128)}, u32[]{:S(2)}) copy-start(f32[16,7,5]{0,1,2:T(8,128)} %param.10) | copy-start | bytes 6724
  1.4 0.7 copy-start.5
  2.1 14.2 %collective-permute-start.1 = (f32[16,128]{1,0:T(8,128)S(1)}, f32[16,128]{1,0:T(8,128)S(1)}, u32[]{:S(2)}, u32[]{:S(2)}) collective-permute-start(f32[16,128]{1,0:T(8,128)S(1)} %table.1.own_ref), channel_id=1, source_target_pairs={{4,0},{8,4},{12,8},{16,12},{20,16},{24,20},{28,24},{32,28},{36,32}... | collective-permute-start | bytes 24584 | tf_op jit(solution)/shard_map/ppermute | solution.py:290
  10.9 5.5 %collective-permute-start = (f32[16,128]{1,0:T(8,128)S(1)}, f32[16,128]{1,0:T(8,128)S(1)}, u32[]{:S(2)}, u32[]{:S(2)}) collective-permute-start(f32[16,128]{1,0:T(8,128)S(1)} %table.1.own_ref), channel_id=1, source_target_pairs={{0,4},{4,8},{8,12},{12,16},{16,20},{20,24},{24,28},{28,32},{32,36}... | collective-permute-start | bytes 24584 | tf_op jit(solution)/shard_map/ppermute | solution.py:289
  12.9 1.3 %copy-start = (bf16[512,5,256]{2,0,1:T(8,128)(2,1)S(1)}, bf16[512,5,256]{2,0,1:T(8,128)(2,1)}, u32[]{:S(2)}) copy-start(bf16[512,5,256]{2,0,1:T(8,128)(2,1)} %param.7) | copy-start | bytes 3932164
  14.2 1.1 %copy-start.2 = (bf16[512,5,128]{2,0,1:T(8,128)(2,1)S(1)}, bf16[512,5,128]{2,0,1:T(8,128)(2,1)}, u32[]{:S(2)}) copy-start(bf16[512,5,128]{2,0,1:T(8,128)(2,1)} %param.8) | copy-start | bytes 1966084
  15.3 5.0 %copy-start.1 = (bf16[512,5,256]{2,0,1:T(8,128)(2,1)S(1)}, bf16[512,5,256]{2,0,1:T(8,128)(2,1)}, u32[]{:S(2)}) copy-start(bf16[512,5,256]{2,0,1:T(8,128)(2,1)} %param.9) | copy-start | bytes 3932164
  16.4 35.4 %copy-start.3 = (f32[128,512]{1,0:T(8,128)S(1)}, f32[128,512]{1,0:T(8,128)}, u32[]{:S(2)}) copy-start(f32[128,512]{1,0:T(8,128)} %s_ref.1) | copy-start | bytes 786436
  16.4 9.5 %all-to-all-start = ((f32[8,40,128]{2,1,0:T(8,128)}), f32[8,40,128]{2,1,0:T(8,128)S(1)}, u32[]{:S(2)}, u32[]{:S(2)}) async-start(f32[8,40,128]{2,1,0:T(8,128)} %project.1), calls=%async_computation | async-start | bytes 327680 | tf_op jit(solution)/shard_map/all_to_all | solution.py:293

commit v4 on v3

v4 whole, which is shorter than its diff:
```python
import jax
import jax.numpy as jnp
from jax import lax
from jax.experimental import pallas as pl
from jax.experimental.pallas import tpu as pltpu
from jax.sharding import Mesh
from jax.sharding import PartitionSpec as P

ROWS = ("z", "x", "c")
PLANE = ("x", "c")
CUBE = ("x", "c", "y")
F32 = jnp.float32
BF16 = jnp.bfloat16
NC, NB = 5, 7
NBR, CNT = 40, 47
PLANE_CNT, LOW_CNT, OWN_CNT, RANK, G_EXP, B_EXP = 96, 104, 105, 106, 107, 108
TOP = 32000.0


VMEM = pl.BlockSpec(memory_space=pltpu.VMEM)
HBM = pl.BlockSpec(memory_space=pltpu.HBM)
SMEM = pl.BlockSpec(memory_space=pltpu.SMEM)
PARAMS = pltpu.CompilerParams(vmem_limit_bytes=12 * 1024 * 1024)


def lanes(shape):
    return lax.broadcasted_iota(jnp.int32, shape, len(shape) - 1)


def exponent(x):
    top = jnp.max(jnp.abs(x), axis=(0, 1), keepdims=True)
    return jnp.floor(-jnp.log2(jnp.maximum(top, 1e-30)))


def coded(x, exp):
    code = jnp.floor(jnp.sqrt(jnp.sqrt(jnp.abs(x * jnp.exp2(exp)))) * TOP + 0.5)
    return jnp.where(x < 0.0, -code, code)


def decoded(code):
    root = code * (1.0 / TOP)
    square = root * root
    return square * square * jnp.where(code < 0.0, -1.0, 1.0)


def to_i16(x):
    return x.astype(jnp.int32).astype(jnp.int16)


def from_i16(x):
    return x.astype(jnp.int32).astype(F32)


def prepare_kernel(
    v_hbm, d_hbm, jac_hbm, nbr_hbm, count_ref, g_ref, table_ref, v_ref, d_ref, jac_ref, nbr_ref, sems
):
    small = [
        pltpu.make_async_copy(jac_hbm, jac_ref, sems.at[2 * NC]),
        pltpu.make_async_copy(nbr_hbm, nbr_ref, sems.at[2 * NC + 1]),
    ]
    v_copies = [
        pltpu.make_async_copy(v_hbm.at[j], v_ref.at[j], sems.at[j]) for j in range(NC)
    ]
    d_copies = [
        pltpu.make_async_copy(d_hbm.at[j], d_ref.at[j], sems.at[NC + j]) for j in range(NC)
    ]
    for j in range(NC):
        v_copies[j].start()
        d_copies[j].start()
    for copy in small:
        copy.start()
    acc = jnp.zeros((128, 256), F32)
    for j in range(NC):
        v_copies[j].wait()
        d_copies[j].wait()
        acc = acc + lax.dot_general(
            d_ref[j], v_ref[j], (((0,), (0,)), ((), ())), preferred_element_type=F32
        )
    for copy in small:
        copy.wait()
    blank = jnp.zeros((1, 16), F32)
    rows = []
    for j in range(NC):
        rows += [jac_ref[j], blank]
    count = count_ref[0].astype(F32)
    rows += [nbr_ref[...].astype(F32), jnp.full((1, 16), count)]
    table = jnp.concatenate(rows + [jnp.zeros((80, 16), F32)], axis=0)
    table = jnp.concatenate([table, jnp.zeros((128, 112), F32)], axis=1)
    table_ref[...] = table.T[0:16, :]
    g = acc.T
    for p in range(8):
        for m in range(4):
            row = 64 * m + 8 * p
            g_ref[p, 8 * m : 8 * m + 8, :] = g[row : row + 8, :]
        g_ref[p, 32:40, :] = jnp.full((8, 128), count)


def prepare(test, deim, jac, nbr, counts):
    return pl.pallas_call(
        prepare_kernel,
        in_specs=[HBM, HBM, HBM, HBM, SMEM],
        out_specs=[VMEM, VMEM],
        out_shape=[
            jax.ShapeDtypeStruct((8, 40, 128), F32),
            jax.ShapeDtypeStruct((16, 128), F32),
        ],
        scratch_shapes=[
            pltpu.VMEM(test.shape, BF16),
            pltpu.VMEM(deim.shape, BF16),
            pltpu.VMEM((NC, NB, 16), F32),
            pltpu.VMEM((NB, 16), jnp.int32),
            pltpu.SemaphoreType.DMA((2 * NC + 2,)),
        ],
        name="prepare",
    )(test, deim, jac, nbr, counts)


def sample_kernel(own_ref, chip_ref, core_ref, u_ref, out_ref):
    rank = jnp.floor(own_ref[0:1, NBR : NBR + 1] * (1.0 / 512.0))
    slot = lax.broadcasted_iota(jnp.int32, (16, 128), 0).astype(F32)
    entry = lanes((16, 128)) < NBR
    first = rank == 2.0 * jnp.floor(rank * 0.5)
    chip, core = chip_ref[...], core_ref[...]
    low = jnp.where(first, chip, core)
    tables = []
    for rows in (low, own_ref[...], jnp.where(first, core, chip)):
        dead = entry & (slot >= rows[:, CNT : CNT + 1])
        tables.append(jnp.where(dead, 0.0, rows))
    table = jnp.concatenate(tables, axis=0)
    near = [table[:, NBR + n : NBR + n + 1] - rank * 512.0 for n in range(NB)]
    total = jnp.zeros((144, 256), F32)
    values = [jnp.broadcast_to(table[:, k : k + 1], (48, 128)) for k in range(NBR)]
    for chunk in range(4):
        cell = (lanes((48, 128)) + 128 * chunk).astype(F32)
        hits = [cell == near[n] for n in range(NB)]
        for j in range(NC):
            weight = jnp.where(hits[0], values[8 * j], 0.0)
            for n in range(1, NB):
                weight = weight + jnp.where(hits[n], values[8 * j + n], 0.0)
            w0 = weight.astype(BF16)
            rest = weight - w0.astype(F32)
            w1 = rest.astype(BF16)
            w2 = (rest - w1.astype(F32)).astype(BF16)
            stacked = jnp.concatenate([w0, w1, w2], axis=0)
            total = total + jnp.dot(
                stacked,
                u_ref[j, 128 * chunk : 128 * chunk + 128, :],
                preferred_element_type=F32,
            )
    rows = total[0:48, :] + (total[48:96, :] + total[96:144, :])
    exp = exponent(rows)
    rows = jnp.concatenate([coded(rows, exp), jnp.zeros((80, 256), F32)], axis=0)
    lane = lanes((1, 128))
    extra = jnp.where(lane == LOW_CNT, low[0:1, CNT : CNT + 1], 0.0)
    extra = extra + jnp.where(lane == OWN_CNT, own_ref[0:1, CNT : CNT + 1], 0.0)
    extra = extra + jnp.where(lane == RANK, rank, 0.0)
    extra = extra + jnp.where(lane == B_EXP, exp, 0.0)
    cols = rows.T
    for z in range(16):
        left = cols[16 * z : 16 * z + 8, :]
        right = pltpu.roll(cols[16 * z + 8 : 16 * z + 16, :], 48, 1)
        out_ref[z, :, :] = left + right + extra


def sample(own, chip, core, trial):
    return pl.pallas_call(
        sample_kernel,
        out_shape=jax.ShapeDtypeStruct((16, 8, 128), F32),
        in_specs=[VMEM] * 4,
        out_specs=VMEM,
        compiler_params=PARAMS,
        name="sample",
    )(own, chip, core, trial)


def merge_kernel(g_ref, b_ref, out_ref):
    total = g_ref[0, 0:32, :]
    for p in range(1, 8):
        total = total + g_ref[p, 0:32, :]
    exp = exponent(total)
    code = coded(total, exp)
    lane = lanes((1, 128))
    extra = jnp.where(lane == G_EXP, exp, 0.0)
    for p in range(8):
        extra = extra + jnp.where(lane == PLANE_CNT + p, g_ref[p, 32:33, :], 0.0)
    for z in range(16):
        out_ref[z] = to_i16(jnp.concatenate([code, b_ref[z] + extra], axis=0))


def merge(g_parts, columns):
    return pl.pallas_call(
        merge_kernel,
        out_shape=jax.ShapeDtypeStruct((16, 40, 128), jnp.int16),
        in_specs=[VMEM] * 2,
        out_specs=VMEM,
        compiler_params=PARAMS,
        name="merge",
    )(g_parts, columns)


def fold_kernel(x_ref, s_ref, out_ref):
    blocks = [from_i16(x_ref[z]) for z in range(16)]
    info = jnp.concatenate([block[32:33, :] for block in blocks], axis=0)
    lane = lanes((16, 128))

    def column(k):
        return jnp.sum(jnp.where(lane == k, info, 0.0), axis=1, keepdims=True)

    g_scale = jnp.exp2(-column(G_EXP))
    b_scale = jnp.exp2(-column(B_EXP))
    total = jnp.zeros((32, 128), F32)
    for z in range(16):
        total = total + decoded(blocks[z][0:32, :]) * g_scale[z : z + 1, :]
    rank = column(RANK)
    place = rank - 8.0 * jnp.floor(rank * 0.125)
    is_count = (lane >= PLANE_CNT) & (lane < PLANE_CNT + 8)
    counts = jnp.where(is_count, info, 0.0)
    before = lax.broadcasted_iota(jnp.int32, (16, 16), 1) < lax.broadcasted_iota(
        jnp.int32, (16, 16), 0
    )
    lower = jnp.dot(before.astype(F32), counts, preferred_element_type=F32)
    ahead = (lane - PLANE_CNT).astype(F32) < place
    lower = lower + jnp.where(ahead, counts, 0.0)
    offset = jnp.sum(lower, axis=1, keepdims=True)
    shift = jnp.where(lane < 16, -column(LOW_CNT), jnp.where(lane < 32, 0.0, column(OWN_CNT)))
    ids = jnp.where(lane < 48, offset + shift + (lane % 16).astype(F32), -1.0)
    slots = lane < 48
    mode = lax.broadcasted_iota(jnp.int32, (512, 128), 0).astype(F32)
    sampled = jnp.zeros((16, 512), F32)
    for z in range(16):
        hot = jnp.where(mode == ids[z : z + 1, :], 1.0, 0.0).astype(BF16)
        both = decoded(blocks[z][32:40, :])
        both = jnp.concatenate([both, pltpu.roll(both, 80, 1)], axis=0)
        cols = jnp.where(slots, both, 0.0)
        high = cols.astype(BF16)
        rest = (cols - high.astype(F32)).astype(BF16)
        part = lax.dot_general(
            jnp.concatenate([high, rest], axis=0),
            hot,
            (((1,), (1,)), ((), ())),
            preferred_element_type=F32,
        )
        sampled = sampled + (part[0:16, :] + part[16:32, :]) * b_scale[z : z + 1, :]
    c = lax.dot_general(
        sampled,
        s_ref[...],
        (((1,), (1,)), ((), ())),
        precision=lax.Precision.HIGHEST,
        preferred_element_type=F32,
    )
    g_pairs = total.reshape(16, 2, 128)
    c_pairs = c.reshape(8, 2, 128)
    for p in range(8):
        for m in range(4):
            at = 5 * (4 * p + m)
            out_ref[at : at + 4] = g_pairs[4 * m : 4 * m + 4]
            out_ref[at + 4] = c_pairs[p]


def fold(parts, inverse):
    return pl.pallas_call(
        fold_kernel,
        out_shape=jax.ShapeDtypeStruct((160, 2, 128), F32),
        in_specs=[VMEM] * 2,
        out_specs=VMEM,
        compiler_params=PARAMS,
        name="fold",
    )(parts, inverse)


def finish_kernel(x_ref, out_ref):
    result = jnp.zeros((2, 64), F32)
    for m in range(4):
        rows = [x_ref[5 * (4 * p + m) : 5 * (4 * p + m) + 4].reshape(8, 128) for p in range(8)]
        c = x_ref[5 * m + 4]
        for p in range(1, 8):
            c = c + x_ref[5 * (4 * p + m) + 4]
        result = result + lax.dot_general(
            c,
            jnp.concatenate(rows, axis=0),
            (((1,), (1,)), ((), ())),
            precision=lax.Precision.HIGHEST,
            preferred_element_type=F32,
        )
    out_ref[...] = result


def finish(parts):
    return pl.pallas_call(
        finish_kernel,
        out_shape=jax.ShapeDtypeStruct((2, 64), F32),
        in_specs=[VMEM] * 1,
        out_specs=VMEM,
        compiler_params=PARAMS,
        name="finish",
    )(parts)


def shards(test_basis, deim_basis, trial_basis, jacobian, neighbours, counts, sample_inverse):
    g_part, own = prepare(
        test_basis.swapaxes(0, 1),
        deim_basis.swapaxes(0, 1),
        jacobian.transpose(2, 1, 0),
        neighbours.T,
        counts,
    )
    groups = lax.axis_size(ROWS)
    across = [(i, i + 1) for i in range(1, groups - 1, 2)]
    across += [(target, source) for source, target in across]
    inside = [(i, i ^ 1) for i in range(groups)]
    chip = lax.ppermute(own, ROWS, across)
    core = lax.ppermute(own, ROWS, inside)
    g_plane = lax.all_to_all(g_part, PLANE, 0, 0, tiled=True)
    columns = sample(own, chip, core, trial_basis.swapaxes(0, 1))
    parts = lax.all_to_all(merge(g_plane, columns), "z", 0, 0, tiled=True)
    pieces = lax.all_to_all(fold(parts, sample_inverse), CUBE, 0, 0, tiled=True)
    return finish(pieces).T


def solution(mesh):
    split = Mesh(mesh.devices.reshape(16, 4, 2, 4), ("z", "x", "c", "y"))
    placed = (
        P(ROWS, None, None),
        P(ROWS, None, "y"),
        P(ROWS, None, None),
        P(ROWS, None, None),
        P(ROWS, None),
        P(ROWS),
        P("y", None),
    )
    return jax.shard_map(
        shards, mesh=split, in_specs=placed, out_specs=P("y", ROWS), check_vma=False
    )
```

time: 72.5 us -> 68 us (0.938)
  local copies, waits for them, and re-layouts: 3.81 us -> 0.71 us
  waiting for transfers between devices: 4.34 us -> 1.59 us
  Pallas kernels: 4.92 us -> 6.71 us
  blocking collectives: 43.6 us -> 41.9 us
  starting transfers between devices: 14.6 us -> 15.9 us
    all_to_all x1, starting transfers between devices: 3.92 us -> 10.3 us  [shards(): g_plane = lax.all_to_all(g_part, PLANE, 0, 0, tiled=True)]
    ppermute x2, starting transfers between devices: 10.7 us -> 5.59 us  [the longest x1 3.58 us: shards(): chip = lax.ppermute(own, ROWS, across)]
    all_to_all x1, waiting for transfers between devices: 4.34 us -> 0.01 us  [shards(): g_plane = lax.all_to_all(g_part, PLANE, 0, 0, tiled=True)]
    all_to_all x1, blocking collectives: 25.7 us -> 22.4 us  [shards(): parts = lax.all_to_all(merge(g_plane, columns), 'z', 0, 0, tiled=True)]
    unnamed x12 -> x6, local copies, waits for them, and re-layouts: 3.81 us -> 0.71 us
    pallas_call x4 -> x3, Pallas kernels: 2.61 us -> 4.41 us  [the longest x1 2.77 us: prepare(): pl.pallas_call(prepare_kernel, in_specs=[HBM, HBM, HBM, HBM, SMEM], out_s...]
    ppermute x2, waiting for transfers between devices: 0.01 us -> 1.59 us  [the longest x1 1.58 us: shards(): chip = lax.ppermute(own, ROWS, across)]
    all_to_all x1, blocking collectives: 18 us -> 19.4 us  [shards(): pieces = lax.all_to_all(fold(parts, sample_inverse), CUBE, 0, 0, tiled=True)]
  transfers between devices with their start and end apart: 3 -> 3, of which waited for: 1 -> 1; matrix products, arithmetic and copies ran while one was open for 0% -> 0% of each run, Pallas kernels for 3% -> 2%
where the time goes in v4:
time: 68 us; the launch traced here: 67.6 us
  blocking collectives  41.9 us (62%)
  starting transfers between devices  15.9 us (23%)
  Pallas kernels  6.71 us (10%)
  waiting for transfers between devices  1.59 us (2%)
  between operations  0.83 us (1%)
  local copies, waits for them, and re-layouts  0.71 us (1%)
    all_to_all x1, blocking collectives, shards(): parts = lax.all_to_all(merge(g_plane, columns), 'z', 0, 0, tiled=True)  22.4 us
    all_to_all x1, blocking collectives, shards(): pieces = lax.all_to_all(fold(parts, sample_inverse), CUBE, 0, 0, tiled=True)  19.4 us
    all_to_all x1, starting transfers between devices, shards(): g_plane = lax.all_to_all(g_part, PLANE, 0, 0, tiled=True)  10.3 us
    ppermute x1, starting transfers between devices, shards(): chip = lax.ppermute(own, ROWS, across)  3.58 us
    pallas_call x1, Pallas kernels, prepare(): pl.pallas_call(prepare_kernel, in_specs=[HBM, HBM, HBM, HBM, SMEM], out_s...  2.77 us
    ppermute x1, starting transfers between devices, shards(): core = lax.ppermute(own, ROWS, inside)  2.01 us
    ppermute x1, waiting for transfers between devices, shards(): chip = lax.ppermute(own, ROWS, across)  1.58 us
    pallas_call x1, Pallas kernels, sample(): pl.pallas_call(sample_kernel, out_shape=jax.ShapeDtypeStruct((16, 8, 128)...  1.46 us
  transfers between devices with their start and end apart: 3, of which 1 were waited for; matrix products, arithmetic and copies ran while one was open for 0% of the time, Pallas kernels for 2%

profile of v4, /device:TPU:1, one launch (start us, length us, event | category | flops | bytes accessed | tf_op | source)
XLA Modules:
  0.0 67.6 jit_solution(2882766762997401168)
XLA Ops:
  0.0 0.0 copy-start
  0.8 2.8 %prepare.1 = (f32[8,40,128]{2,1,0:T(8,128)}, f32[16,128]{1,0:T(8,128)}) custom-call(bf16[5,512,256]{2,1,0:T(8,128)(2,1)} %bitcast.7, bf16[5,512,128]{2,1,0:T(8,128)(2,1)} %bitcast.8, f32[5,7,16]{2,1,0:T(8,128)} %bitcast.9, s32[7,16]{1,0:T(8,128)} %bitcast.10, s32[1]{0:T(128)S(6)} %copy.8.count_ref), custom_call_target="tpu_custom_call" | custom-call | tf_op jit(solution)/shard_map/prepare/pallas_call | solution.py:99
  3.5 0.0 copy-start.1
  3.5 10.3 %all-to-all-start = ((f32[8,40,128]{2,1,0:T(8,128)}), f32[8,40,128]{2,1,0:T(8,128)S(1)}, u32[]{:S(2)}, u32[]{:S(2)}) async-start(f32[8,40,128]{2,1,0:T(8,128)} %get-tuple-element.7), calls=%async_computation | async-start | bytes 327680 | tf_op jit(solution)/shard_map/all_to_all | solution.py:313
  13.8 2.0 %collective-permute-start.1 = (f32[16,128]{1,0:T(8,128)}, f32[16,128]{1,0:T(8,128)S(1)}, u32[]{:S(2)}, u32[]{:S(2)}) collective-permute-start(f32[16,128]{1,0:T(8,128)} %get-tuple-element.8.own_ref), channel_id=1, source_target_pairs={{0,4},{4,0},{8,12},{12,8},{16,20},{20,16},{24,28},{28,24},{32,36},... | collective-permute-start | bytes 24584 | tf_op jit(solution)/shard_map/ppermute | solution.py:312
  15.9 3.6 %collective-permute-start = (f32[16,128]{1,0:T(8,128)}, f32[16,128]{1,0:T(8,128)S(1)}, u32[]{:S(2)}, u32[]{:S(2)}) collective-permute-start(f32[16,128]{1,0:T(8,128)} %get-tuple-element.8.own_ref), channel_id=1, source_target_pairs={{4,8},{12,16},{20,24},{28,32},{36,40},{44,48},{52,56},{60,64},{68,... | collective-permute-start | bytes 24584 | tf_op jit(solution)/shard_map/ppermute | solution.py:311
  19.5 0.0 collective-permute-done.1.core_ref
  19.5 1.6 %collective-permute-done.chip_ref = f32[16,128]{1,0:T(8,128)S(1)} collective-permute-done((f32[16,128]{1,0:T(8,128)}, f32[16,128]{1,0:T(8,128)S(1)}, u32[]{:S(2)}, u32[]{:S(2)}) %collective-permute-start) | collective-permute-done | bytes 8224 | tf_op jit(solution)/shard_map/ppermute | solution.py:311
  21.1 0.0 copy-done
  21.1 0.0 copy-start.2
  21.1 0.7 %copy-done.2 = f32[16,128]{1,0:T(8,128)S(1)} copy-done((f32[16,128]{1,0:T(8,128)S(1)}, f32[16,128]{1,0:T(8,128)}, u32[]{:S(2)}) %copy-start.2) | copy-done | bytes 8216
  21.8 1.5 %sample.1.b_ref = f32[16,8,128]{2,1,0:T(8,128)S(1)} custom-call(f32[16,128]{1,0:T(8,128)S(1)} %copy-done.2, f32[16,128]{1,0:T(8,128)S(1)} %collective-permute-done.chip_ref, f32[16,128]{1,0:T(8,128)S(1)} %collective-permute-done.1.core_ref, bf16[5,512,256]{2,1,0:T(8,128)(2,1)S(1)} %bitcast.6), custom_call_target="tpu_custom_call" | custom-call | tf_op jit(solution)/shard_map/sample/pallas_call | solution.py:166
  23.2 0.0 all-to-all-done.g_ref
  23.2 0.2 merge.1
  23.4 22.4 %all_to_all.15.x_ref = s16[16,40,128]{2,1,0:T(8,128)(2,1)S(1)} all-to-all(s16[16,40,128]{2,1,0:T(8,128)(2,1)S(1)} %merge.1), channel_id=1, replica_groups=mesh['z'=16,'x'=4,'c'=2,'y'=4] {'z'}, dimensions={0} | all-to-all | bytes 327680 | tf_op jit(solution)/shard_map/all_to_all | solution.py:315
  45.9 0.0 copy-done.1
  45.9 1.4 %fold.1 = f32[160,2,128]{2,1,0:T(2,128)S(1)} custom-call(s16[16,40,128]{2,1,0:T(8,128)(2,1)S(1)} %all_to_all.15.x_ref, f32[128,512]{1,0:T(8,128)S(1)} %copy-done.1), custom_call_target="tpu_custom_call" | custom-call | tf_op jit(solution)/shard_map/fold/pallas_call | solution.py:261
  47.3 19.4 %all_to_all.16.x_ref = f32[160,2,128]{2,1,0:T(2,128)S(1)} all-to-all(f32[160,2,128]{2,1,0:T(2,128)S(1)} %fold.1), channel_id=1, replica_groups=mesh['z'=16,'x'=4,'c'=2,'y'=4] {'x','c','y'}, dimensions={0} | all-to-all | bytes 327680 | tf_op jit(solution)/shard_map/all_to_all | solution.py:316
  66.7 0.9 %finish.1 = f32[2,64]{1,0:T(2,128)} custom-call(f32[160,2,128]{2,1,0:T(2,128)S(1)} %all_to_all.16.x_ref), custom_call_target="tpu_custom_call" | custom-call | tf_op jit(solution)/shard_map/finish/pallas_call | solution.py:289
Async XLA Ops:
  0.0 21.1 %copy-start = (bf16[512,5,256]{2,0,1:T(8,128)(2,1)S(1)}, bf16[512,5,256]{2,0,1:T(8,128)(2,1)}, u32[]{:S(2)}) copy-start(bf16[512,5,256]{2,0,1:T(8,128)(2,1)} %param.9) | copy-start | bytes 3932164
  3.5 42.3 %copy-start.1 = (f32[128,512]{1,0:T(8,128)S(1)}, f32[128,512]{1,0:T(8,128)}, u32[]{:S(2)}) copy-start(f32[128,512]{1,0:T(8,128)} %s_ref.1) | copy-start | bytes 786436
  3.5 19.7 %all-to-all-start = ((f32[8,40,128]{2,1,0:T(8,128)}), f32[8,40,128]{2,1,0:T(8,128)S(1)}, u32[]{:S(2)}, u32[]{:S(2)}) async-start(f32[8,40,128]{2,1,0:T(8,128)} %get-tuple-element.7), calls=%async_computation | async-start | bytes 327680 | tf_op jit(solution)/shard_map/all_to_all | solution.py:313
  13.8 5.6 %collective-permute-start.1 = (f32[16,128]{1,0:T(8,128)}, f32[16,128]{1,0:T(8,128)S(1)}, u32[]{:S(2)}, u32[]{:S(2)}) collective-permute-start(f32[16,128]{1,0:T(8,128)} %get-tuple-element.8.own_ref), channel_id=1, source_target_pairs={{0,4},{4,0},{8,12},{12,8},{16,20},{20,16},{24,28},{28,24},{32,36},... | collective-permute-start | bytes 24584 | tf_op jit(solution)/shard_map/ppermute | solution.py:312
  15.9 5.2 %collective-permute-start = (f32[16,128]{1,0:T(8,128)}, f32[16,128]{1,0:T(8,128)S(1)}, u32[]{:S(2)}, u32[]{:S(2)}) collective-permute-start(f32[16,128]{1,0:T(8,128)} %get-tuple-element.8.own_ref), channel_id=1, source_target_pairs={{4,8},{12,16},{20,24},{28,32},{36,40},{44,48},{52,56},{60,64},{68,... | collective-permute-start | bytes 24584 | tf_op jit(solution)/shard_map/ppermute | solution.py:311
  21.1 0.7 %copy-start.2 = (f32[16,128]{1,0:T(8,128)S(1)}, f32[16,128]{1,0:T(8,128)}, u32[]{:S(2)}) copy-start(f32[16,128]{1,0:T(8,128)} %get-tuple-element.8.own_ref) | copy-start | bytes 24580

commit v5 on v4

v5 whole, which is shorter than its diff:
```python
import jax
import jax.numpy as jnp
from jax import lax
from jax.experimental import pallas as pl
from jax.experimental.pallas import tpu as pltpu
from jax.sharding import Mesh
from jax.sharding import PartitionSpec as P

ROWS = ("zh", "zl", "x", "c")
GROUP = ("zl", "x", "c")
CUBE = ("zl", "x", "c", "y")
F32 = jnp.float32
BF16 = jnp.bfloat16
NC, NB = 5, 7
NBR, CNT = 40, 47
GROUP_CNT, LOW_CNT, OWN_CNT, RANK, G_EXP, B_EXP = 96, 112, 113, 114, 115, 116
TOP = 32000.0


VMEM = pl.BlockSpec(memory_space=pltpu.VMEM)
HBM = pl.BlockSpec(memory_space=pltpu.HBM)
PARAMS = pltpu.CompilerParams(vmem_limit_bytes=12 * 1024 * 1024)


def lanes(shape):
    return lax.broadcasted_iota(jnp.int32, shape, len(shape) - 1)


def exponent(x):
    top = jnp.max(jnp.abs(x), axis=(0, 1), keepdims=True)
    return jnp.floor(-jnp.log2(jnp.maximum(top, 1e-30)))


def coded(x, exp):
    code = jnp.floor(jnp.sqrt(jnp.sqrt(jnp.abs(x * jnp.exp2(exp)))) * TOP + 0.5)
    return jnp.where(x < 0.0, -code, code)


def decoded(code):
    root = code * (1.0 / TOP)
    square = root * root
    return square * square * jnp.where(code < 0.0, -1.0, 1.0)


def to_i16(x):
    return x.astype(jnp.int32).astype(jnp.int16)


def from_i16(x):
    return x.astype(jnp.int32).astype(F32)


def table_of(jac_ref, nbr_ref, count):
    blank = jnp.zeros((1, 16), F32)
    rows = []
    for j in range(NC):
        rows += [jac_ref[j], blank]
    rows += [nbr_ref[...].astype(F32), jnp.broadcast_to(count, (1, 16))]
    table = jnp.concatenate(rows + [jnp.zeros((80, 16), F32)], axis=0)
    table = jnp.concatenate([table, jnp.zeros((128, 112), F32)], axis=1)
    return table.T[0:16, :]


def prepare_kernel(
    v_hbm,
    d_hbm,
    jac_hbm,
    nbr_hbm,
    count_hbm,
    g_ref,
    table_ref,
    v_ref,
    d_ref,
    jac_ref,
    nbr_ref,
    count_ref,
    sems,
):
    small = [
        pltpu.make_async_copy(jac_hbm, jac_ref, sems.at[2 * NC]),
        pltpu.make_async_copy(nbr_hbm, nbr_ref, sems.at[2 * NC + 1]),
        pltpu.make_async_copy(count_hbm, count_ref, sems.at[2 * NC + 2]),
    ]
    v_copies = [
        pltpu.make_async_copy(v_hbm.at[j], v_ref.at[j], sems.at[j]) for j in range(NC)
    ]
    d_copies = [
        pltpu.make_async_copy(d_hbm.at[j], d_ref.at[j], sems.at[NC + j]) for j in range(NC)
    ]
    for copy in small:
        copy.start()
    for j in range(NC):
        v_copies[j].start()
        d_copies[j].start()
    for copy in small:
        copy.wait()
    count = count_ref[0, 0].astype(F32)
    table_ref[...] = table_of(jac_ref, nbr_ref, count)
    acc = jnp.zeros((128, 256), F32)
    for j in range(NC):
        v_copies[j].wait()
        d_copies[j].wait()
        acc = acc + lax.dot_general(
            d_ref[j], v_ref[j], (((0,), (0,)), ((), ())), preferred_element_type=F32
        )
    pairs = acc.T.reshape(128, 2, 128)
    for p in range(16):
        for m in range(4):
            at = 32 * m + 2 * p
            g_ref[9 * p + 2 * m : 9 * p + 2 * m + 2] = pairs[at : at + 2]
        g_ref[9 * p + 8] = jnp.full((2, 128), count)


def prepare(test, deim, jac, nbr, counts):
    return pl.pallas_call(
        prepare_kernel,
        in_specs=[HBM, HBM, HBM, HBM, HBM],
        out_specs=[VMEM, VMEM],
        out_shape=[
            jax.ShapeDtypeStruct((144, 2, 128), F32),
            jax.ShapeDtypeStruct((16, 128), F32),
        ],
        scratch_shapes=[
            pltpu.VMEM(test.shape, BF16),
            pltpu.VMEM(deim.shape, BF16),
            pltpu.VMEM((NC, NB, 16), F32),
            pltpu.VMEM((NB, 16), jnp.int32),
            pltpu.SMEM((1, 1), jnp.int32),
            pltpu.SemaphoreType.DMA((2 * NC + 3,)),
        ],
        name="prepare",
    )(test, deim, jac, nbr, counts)


def sample_kernel(jac_ref, nbr_ref, count_ref, chip_ref, core_ref, u_ref, out_ref):
    own = table_of(jac_ref, nbr_ref, count_ref[...].astype(F32))
    rank = jnp.floor(own[0:1, NBR : NBR + 1] * (1.0 / 512.0))
    slot = lax.broadcasted_iota(jnp.int32, (16, 128), 0).astype(F32)
    entry = lanes((16, 128)) < NBR
    first = rank == 2.0 * jnp.floor(rank * 0.5)
    chip, core = chip_ref[...], core_ref[...]
    low = jnp.where(first, chip, core)
    tables = []
    for rows in (low, own, jnp.where(first, core, chip)):
        dead = entry & (slot >= rows[:, CNT : CNT + 1])
        tables.append(jnp.where(dead, 0.0, rows))
    table = jnp.concatenate(tables, axis=0)
    near = [table[:, NBR + n : NBR + n + 1] - rank * 512.0 for n in range(NB)]
    total = jnp.zeros((96, 256), F32)
    values = [jnp.broadcast_to(table[:, k : k + 1], (48, 128)) for k in range(NBR)]
    for chunk in range(4):
        cell = (lanes((48, 128)) + 128 * chunk).astype(F32)
        hits = [cell == near[n] for n in range(NB)]
        for j in range(NC):
            weight = jnp.where(hits[0], values[8 * j], 0.0)
            for n in range(1, NB):
                weight = weight + jnp.where(hits[n], values[8 * j + n], 0.0)
            high = weight.astype(BF16)
            rest = (weight - high.astype(F32)).astype(BF16)
            total = total + jnp.dot(
                jnp.concatenate([high, rest], axis=0),
                u_ref[j, 128 * chunk : 128 * chunk + 128, :],
                preferred_element_type=F32,
            )
    rows = total[0:48, :] + total[48:96, :]
    exp = exponent(rows)
    rows = jnp.concatenate([coded(rows, exp), jnp.zeros((80, 256), F32)], axis=0)
    lane = lanes((1, 128))
    extra = jnp.where(lane == LOW_CNT, low[0:1, CNT : CNT + 1], 0.0)
    extra = extra + jnp.where(lane == OWN_CNT, own[0:1, CNT : CNT + 1], 0.0)
    extra = extra + jnp.where(lane == RANK, rank, 0.0)
    extra = extra + jnp.where(lane == B_EXP, exp, 0.0)
    cols = rows.T
    for z in range(8):
        left = cols[32 * z : 32 * z + 16, :]
        right = pltpu.roll(cols[32 * z + 16 : 32 * z + 32, :], 48, 1)
        out_ref[z, :, :] = left + right + extra


def sample(jac, nbr, counts, chip, core, trial):
    return pl.pallas_call(
        sample_kernel,
        out_shape=jax.ShapeDtypeStruct((8, 16, 128), F32),
        in_specs=[VMEM] * 6,
        out_specs=VMEM,
        compiler_params=PARAMS,
        name="sample",
    )(jac, nbr, counts, chip, core, trial)


def merge_kernel(g_ref, b_ref, out_ref):
    total = g_ref[0:8]
    for p in range(1, 16):
        total = total + g_ref[9 * p : 9 * p + 8]
    total = total.reshape(16, 128)
    exp = exponent(total)
    code = coded(total, exp)
    lane = lanes((1, 128))
    extra = jnp.where(lane == G_EXP, exp, 0.0)
    for p in range(16):
        extra = extra + jnp.where(lane == GROUP_CNT + p, g_ref[9 * p + 8][0:1, :], 0.0)
    for z in range(8):
        out_ref[z] = to_i16(jnp.concatenate([code, b_ref[z] + extra], axis=0))


def merge(g_parts, columns):
    return pl.pallas_call(
        merge_kernel,
        out_shape=jax.ShapeDtypeStruct((8, 32, 128), jnp.int16),
        in_specs=[VMEM] * 2,
        out_specs=VMEM,
        compiler_params=PARAMS,
        name="merge",
    )(g_parts, columns)


def fold_kernel(x_ref, s_ref, out_ref):
    blocks = [from_i16(x_ref[z]) for z in range(8)]
    info = jnp.concatenate([block[16:17, :] for block in blocks], axis=0)
    lane = lanes((8, 128))

    def column(k):
        return jnp.sum(jnp.where(lane == k, info, 0.0), axis=1, keepdims=True)

    g_scale = jnp.exp2(-column(G_EXP))
    b_scale = jnp.exp2(-column(B_EXP))
    total = jnp.zeros((16, 128), F32)
    for z in range(8):
        total = total + decoded(blocks[z][0:16, :]) * g_scale[z : z + 1, :]
    rank = column(RANK)
    place = rank - 16.0 * jnp.floor(rank * 0.0625)
    is_count = (lane >= GROUP_CNT) & (lane < GROUP_CNT + 16)
    counts = jnp.where(is_count, info, 0.0)
    before = lax.broadcasted_iota(jnp.int32, (8, 8), 1) < lax.broadcasted_iota(
        jnp.int32, (8, 8), 0
    )
    lower = jnp.dot(before.astype(F32), counts, preferred_element_type=F32)
    ahead = (lane - GROUP_CNT).astype(F32) < place
    lower = lower + jnp.where(ahead, counts, 0.0)
    offset = jnp.sum(lower, axis=1, keepdims=True)
    shift = jnp.where(lane < 16, -column(LOW_CNT), jnp.where(lane < 32, 0.0, column(OWN_CNT)))
    ids = jnp.where(lane < 48, offset + shift + (lane % 16).astype(F32), -1.0)
    slots = lanes((1, 128)) < 48
    mode = lax.broadcasted_iota(jnp.int32, (512, 128), 0).astype(F32)
    sampled = jnp.zeros((32, 512), F32)
    for z in range(8):
        hot = jnp.where(mode == ids[z : z + 1, :], 1.0, 0.0).astype(BF16)
        both = decoded(blocks[z][16:32, :])
        both = jnp.concatenate([both, pltpu.roll(both, 80, 1)], axis=0)
        cols = jnp.where(slots, both, 0.0)
        high = cols.astype(BF16)
        rest = (cols - high.astype(F32)).astype(BF16)
        part = lax.dot_general(
            jnp.concatenate([high, rest], axis=0),
            hot,
            (((1,), (1,)), ((), ())),
            preferred_element_type=F32,
        )
        sampled = sampled + (part[0:32, :] + part[32:64, :]) * b_scale[z : z + 1, :]
    c = lax.dot_general(
        sampled,
        s_ref[...],
        (((1,), (1,)), ((), ())),
        precision=lax.Precision.HIGHEST,
        preferred_element_type=F32,
    )
    g_pairs = total.reshape(8, 2, 128)
    c_pairs = c.reshape(16, 2, 128)
    for p in range(16):
        for m in range(4):
            at = 3 * (4 * p + m)
            out_ref[at : at + 2] = g_pairs[2 * m : 2 * m + 2]
            out_ref[at + 2] = c_pairs[p]


def fold(parts, inverse):
    return pl.pallas_call(
        fold_kernel,
        out_shape=jax.ShapeDtypeStruct((192, 2, 128), F32),
        in_specs=[VMEM] * 2,
        out_specs=VMEM,
        compiler_params=PARAMS,
        name="fold",
    )(parts, inverse)


def finish_kernel(x_ref, out_ref):
    result = jnp.zeros((2, 64), F32)
    for m in range(4):
        rows = [x_ref[3 * (4 * p + m) : 3 * (4 * p + m) + 2] for p in range(16)]
        c = x_ref[3 * m + 2]
        for p in range(1, 16):
            c = c + x_ref[3 * (4 * p + m) + 2]
        result = result + lax.dot_general(
            c,
            jnp.concatenate(rows, axis=0).reshape(64, 128),
            (((1,), (1,)), ((), ())),
            precision=lax.Precision.HIGHEST,
            preferred_element_type=F32,
        )
    out_ref[...] = result


def finish(parts):
    return pl.pallas_call(
        finish_kernel,
        out_shape=jax.ShapeDtypeStruct((2, 64), F32),
        in_specs=[VMEM] * 1,
        out_specs=VMEM,
        compiler_params=PARAMS,
        name="finish",
    )(parts)


def shards(test_basis, deim_basis, trial_basis, jacobian, neighbours, counts, sample_inverse):
    jac, nbr, count = jacobian.transpose(2, 1, 0), neighbours.T, counts.reshape(1, 1)
    g_part, own = prepare(test_basis.swapaxes(0, 1), deim_basis.swapaxes(0, 1), jac, nbr, count)
    groups = lax.axis_size(ROWS)
    across = [(i, i + 1) for i in range(1, groups - 1, 2)]
    across += [(target, source) for source, target in across]
    inside = [(i, i ^ 1) for i in range(groups)]
    core = lax.ppermute(own, ROWS, inside)
    chip = lax.ppermute(own, ROWS, across)
    g_group = lax.all_to_all(g_part, GROUP, 0, 0, tiled=True)
    columns = sample(jac, nbr, count, chip, core, trial_basis.swapaxes(0, 1))
    parts = lax.all_to_all(merge(g_group, columns), "zh", 0, 0, tiled=True)
    pieces = lax.all_to_all(fold(parts, sample_inverse), CUBE, 0, 0, tiled=True)
    return finish(pieces).T


def solution(mesh):
    split = Mesh(mesh.devices.reshape(8, 2, 4, 2, 4), ("zh", "zl", "x", "c", "y"))
    placed = (
        P(ROWS, None, None),
        P(ROWS, None, "y"),
        P(ROWS, None, None),
        P(ROWS, None, None),
        P(ROWS, None),
        P(ROWS),
        P("y", None),
    )
    return jax.shard_map(
        shards, mesh=split, in_specs=placed, out_specs=P("y", ROWS), check_vma=False
    )
```

time: 68 us -> 68.2 us (level)
  blocking collectives: 41.9 us -> 42.8 us
  local copies, waits for them, and re-layouts: 0.71 us -> 0.02 us
    unnamed x6 -> x8, local copies, waits for them, and re-layouts: 0.71 us -> 0.02 us
where the time goes in v5:
time: 68.2 us; the launch traced here: 67.9 us
  blocking collectives  42.8 us (63%)
  starting transfers between devices  15.9 us (23%)
  Pallas kernels  6.62 us (10%)
  waiting for transfers between devices  1.7 us (2%)
  between operations  0.83 us (1%)
    all_to_all x1, blocking collectives, shards(): parts = lax.all_to_all(merge(g_group, columns), 'zh', 0, 0, tiled=True)  22.9 us
    all_to_all x1, blocking collectives, shards(): pieces = lax.all_to_all(fold(parts, sample_inverse), CUBE, 0, 0, tiled=True)  19.9 us
    all_to_all x1, starting transfers between devices, shards(): g_group = lax.all_to_all(g_part, GROUP, 0, 0, tiled=True)  10.3 us
    ppermute x1, starting transfers between devices, shards(): chip = lax.ppermute(own, ROWS, across)  3.46 us
    pallas_call x1, Pallas kernels, prepare(): pl.pallas_call(prepare_kernel, in_specs=[HBM, HBM, HBM, HBM, HBM], out_sp...  2.76 us
    ppermute x1, starting transfers between devices, shards(): core = lax.ppermute(own, ROWS, inside)  2.13 us
    ppermute x1, waiting for transfers between devices, shards(): chip = lax.ppermute(own, ROWS, across)  1.7 us
    pallas_call x1, Pallas kernels, sample(): pl.pallas_call(sample_kernel, out_shape=jax.ShapeDtypeStruct((8, 16, 128)...  1.6 us
  transfers between devices with their start and end apart: 3, of which 1 were waited for; matrix products, arithmetic and copies ran while one was open for 0% of the time, Pallas kernels for 2%

profile of v5, /device:TPU:1, one launch (start us, length us, event | category | flops | bytes accessed | tf_op | source)
XLA Modules:
  0.0 67.9 jit_solution(10424196120467441345)
XLA Ops:
  0.0 0.0 copy-start.3
  0.0 0.0 copy-start.2
  0.0 0.0 copy-start
  0.8 2.8 %prepare.1 = (f32[144,2,128]{2,1,0:T(2,128)}, f32[16,128]{1,0:T(8,128)}) custom-call(bf16[5,512,256]{2,1,0:T(8,128)(2,1)} %bitcast.14, bf16[5,512,128]{2,1,0:T(8,128)(2,1)} %bitcast.15, f32[5,7,16]{2,1,0:T(8,128)} %bitcast.10, s32[7,16]{1,0:T(8,128)} %bitcast.12, s32[1,1]{1,0:T(1,128)} %bitcast.7.count_hbm), custom_call_target="tpu_custom_call" | custom-call | tf_op jit(solution)/shard_map/prepare/pallas_call | solution.py:115
  3.5 0.0 copy-start.1
  3.5 10.3 %all-to-all-start = ((f32[144,2,128]{2,1,0:T(2,128)}), f32[144,2,128]{2,1,0:T(2,128)S(1)}, u32[]{:S(2)}, u32[]{:S(2)}) async-start(f32[144,2,128]{2,1,0:T(2,128)} %get-tuple-element.7), calls=%async_computation | async-start | bytes 294912 | tf_op jit(solution)/shard_map/all_to_all | solution.py:324
  13.9 2.1 %collective-permute-start.1 = (f32[16,128]{1,0:T(8,128)}, f32[16,128]{1,0:T(8,128)S(1)}, u32[]{:S(2)}, u32[]{:S(2)}) collective-permute-start(f32[16,128]{1,0:T(8,128)} %get-tuple-element.8), channel_id=1, source_target_pairs={{0,4},{4,0},{8,12},{12,8},{16,20},{20,16},{24,28},{28,24},{32,36},... | collective-permute-start | bytes 24584 | tf_op jit(solution)/shard_map/ppermute | solution.py:322
  16.0 3.5 %collective-permute-start = (f32[16,128]{1,0:T(8,128)}, f32[16,128]{1,0:T(8,128)S(1)}, u32[]{:S(2)}, u32[]{:S(2)}) collective-permute-start(f32[16,128]{1,0:T(8,128)} %get-tuple-element.8), channel_id=1, source_target_pairs={{4,8},{12,16},{20,24},{28,32},{36,40},{44,48},{52,56},{60,64},{68,... | collective-permute-start | bytes 24584 | tf_op jit(solution)/shard_map/ppermute | solution.py:323
  19.5 0.0 collective-permute-done.1.core_ref
  19.5 1.7 %collective-permute-done.chip_ref = f32[16,128]{1,0:T(8,128)S(1)} collective-permute-done((f32[16,128]{1,0:T(8,128)}, f32[16,128]{1,0:T(8,128)S(1)}, u32[]{:S(2)}, u32[]{:S(2)}) %collective-permute-start) | collective-permute-done | bytes 8224 | tf_op jit(solution)/shard_map/ppermute | solution.py:323
  21.2 0.0 copy-done.3
  21.2 0.0 copy-done.2
  21.2 0.0 copy-done
  21.2 1.6 %sample.1.b_ref = f32[8,16,128]{2,1,0:T(8,128)S(1)} custom-call(f32[5,7,16]{2,1,0:T(8,128)S(1)} %bitcast.11, s32[7,16]{1,0:T(8,128)S(1)} %bitcast.13, s32[1,1]{1,0:T(1,128)} %bitcast.8.count_ref, f32[16,128]{1,0:T(8,128)S(1)} %collective-permute-done.chip_ref, f32[16,128]{1,0:T(8,128)S(1)} %collective-permute-done.1.core_ref, bf16[5,512,256]{2,1,0:T(8,128)(2,1)S(1)} %bitcast.9), custom_call_target="tpu_custom_call" | custom-call | tf_op jit(solution)/shard_map/sample/pallas_call | solution.py:181
  22.8 0.0 all-to-all-done.g_ref
  22.8 0.2 merge.1
  23.0 22.9 %all_to_all.15.x_ref = s16[8,32,128]{2,1,0:T(8,128)(2,1)S(1)} all-to-all(s16[8,32,128]{2,1,0:T(8,128)(2,1)S(1)} %merge.1), channel_id=1, replica_groups=mesh['zh'=8,'zl'=2,'x'=4,'c'=2,'y'=4] {'zh'}, dimensions={0} | all-to-all | bytes 131072 | tf_op jit(solution)/shard_map/all_to_all | solution.py:326
  45.9 0.0 copy-done.1
  45.9 1.2 %fold.1 = f32[192,2,128]{2,1,0:T(2,128)S(1)} custom-call(s16[8,32,128]{2,1,0:T(8,128)(2,1)S(1)} %all_to_all.15.x_ref, f32[128,512]{1,0:T(8,128)S(1)} %copy-done.1), custom_call_target="tpu_custom_call" | custom-call | tf_op jit(solution)/shard_map/fold/pallas_call | solution.py:277
  47.1 19.9 %all_to_all.16.x_ref = f32[192,2,128]{2,1,0:T(2,128)S(1)} all-to-all(f32[192,2,128]{2,1,0:T(2,128)S(1)} %fold.1), channel_id=1, replica_groups=mesh['zh'=8,'zl'=2,'x'=4,'c'=2,'y'=4] {'zl','x','c','y'}, dimensions={0} | all-to-all | bytes 393216 | tf_op jit(solution)/shard_map/all_to_all | solution.py:327
  67.0 0.9 %finish.1 = f32[2,64]{1,0:T(2,128)} custom-call(f32[192,2,128]{2,1,0:T(2,128)S(1)} %all_to_all.16.x_ref), custom_call_target="tpu_custom_call" | custom-call | tf_op jit(solution)/shard_map/finish/pallas_call | solution.py:305
Async XLA Ops:
  0.0 21.2 %copy-start.3 = (s32[16,7]{0,1:T(8,128)S(1)}, s32[16,7]{0,1:T(8,128)}, u32[]{:S(2)}) copy-start(s32[16,7]{0,1:T(8,128)} %param.11) | copy-start | bytes 1348
  0.0 21.2 %copy-start.2 = (f32[16,7,5]{0,1,2:T(8,128)S(1)}, f32[16,7,5]{0,1,2:T(8,128)}, u32[]{:S(2)}) copy-start(f32[16,7,5]{0,1,2:T(8,128)} %param.10) | copy-start | bytes 6724
  0.0 21.2 %copy-start = (bf16[512,5,256]{2,0,1:T(8,128)(2,1)S(1)}, bf16[512,5,256]{2,0,1:T(8,128)(2,1)}, u32[]{:S(2)}) copy-start(bf16[512,5,256]{2,0,1:T(8,128)(2,1)} %param.9) | copy-start | bytes 3932164
  3.5 42.4 %copy-start.1 = (f32[128,512]{1,0:T(8,128)S(1)}, f32[128,512]{1,0:T(8,128)}, u32[]{:S(2)}) copy-start(f32[128,512]{1,0:T(8,128)} %s_ref.1) | copy-start | bytes 786436
  3.5 19.3 %all-to-all-start = ((f32[144,2,128]{2,1,0:T(2,128)}), f32[144,2,128]{2,1,0:T(2,128)S(1)}, u32[]{:S(2)}, u32[]{:S(2)}) async-start(f32[144,2,128]{2,1,0:T(2,128)} %get-tuple-element.7), calls=%async_computation | async-start | bytes 294912 | tf_op jit(solution)/shard_map/all_to_all | solution.py:324
  13.9 5.6 %collective-permute-start.1 = (f32[16,128]{1,0:T(8,128)}, f32[16,128]{1,0:T(8,128)S(1)}, u32[]{:S(2)}, u32[]{:S(2)}) collective-permute-start(f32[16,128]{1,0:T(8,128)} %get-tuple-element.8), channel_id=1, source_target_pairs={{0,4},{4,0},{8,12},{12,8},{16,20},{20,16},{24,28},{28,24},{32,36},... | collective-permute-start | bytes 24584 | tf_op jit(solution)/shard_map/ppermute | solution.py:322
  16.0 5.2 %collective-permute-start = (f32[16,128]{1,0:T(8,128)}, f32[16,128]{1,0:T(8,128)S(1)}, u32[]{:S(2)}, u32[]{:S(2)}) collective-permute-start(f32[16,128]{1,0:T(8,128)} %get-tuple-element.8), channel_id=1, source_target_pairs={{4,8},{12,16},{20,24},{28,32},{36,40},{44,48},{52,56},{60,64},{68,... | collective-permute-start | bytes 24584 | tf_op jit(solution)/shard_map/ppermute | solution.py:323

commit v6 on v5

--- a/solution.py
+++ b/solution.py
@@ -132,7 +132,7 @@
     )(test, deim, jac, nbr, counts)
 
 
-def sample_kernel(jac_ref, nbr_ref, count_ref, chip_ref, core_ref, u_ref, out_ref):
+def sample_kernel(jac_ref, nbr_ref, count_ref, core_ref, chip_ref, u_ref, out_ref):
     own = table_of(jac_ref, nbr_ref, count_ref[...].astype(F32))
     rank = jnp.floor(own[0:1, NBR : NBR + 1] * (1.0 / 512.0))
     slot = lax.broadcasted_iota(jnp.int32, (16, 128), 0).astype(F32)
@@ -148,20 +148,21 @@
     near = [table[:, NBR + n : NBR + n + 1] - rank * 512.0 for n in range(NB)]
     total = jnp.zeros((96, 256), F32)
     values = [jnp.broadcast_to(table[:, k : k + 1], (48, 128)) for k in range(NBR)]
-    for chunk in range(4):
-        cell = (lanes((48, 128)) + 128 * chunk).astype(F32)
-        hits = [cell == near[n] for n in range(NB)]
-        for j in range(NC):
-            weight = jnp.where(hits[0], values[8 * j], 0.0)
+    cell = lanes((48, 128)).astype(F32)
+    hits = [[cell + 128.0 * part == near[n] for n in range(NB)] for part in range(4)]
+    for j in range(NC):
+        weights = []
+        for part in range(4):
+            weight = jnp.where(hits[part][0], values[8 * j], 0.0)
             for n in range(1, NB):
-                weight = weight + jnp.where(hits[n], values[8 * j + n], 0.0)
-            high = weight.astype(BF16)
-            rest = (weight - high.astype(F32)).astype(BF16)
-            total = total + jnp.dot(
-                jnp.concatenate([high, rest], axis=0),
-                u_ref[j, 128 * chunk : 128 * chunk + 128, :],
-                preferred_element_type=F32,
-            )
+                weight = weight + jnp.where(hits[part][n], values[8 * j + n], 0.0)
+            weights.append(weight)
+        weight = jnp.concatenate(weights, axis=1)
+        high = weight.astype(BF16)
+        rest = (weight - high.astype(F32)).astype(BF16)
+        total = total + jnp.dot(
+            jnp.concatenate([high, rest], axis=0), u_ref[j], preferred_element_type=F32
+        )
     rows = total[0:48, :] + total[48:96, :]
     exp = exponent(rows)
     rows = jnp.concatenate([coded(rows, exp), jnp.zeros((80, 256), F32)], axis=0)
@@ -177,7 +178,7 @@
         out_ref[z, :, :] = left + right + extra
 
 
-def sample(jac, nbr, counts, chip, core, trial):
+def sample(jac, nbr, counts, core, chip, trial):
     return pl.pallas_call(
         sample_kernel,
         out_shape=jax.ShapeDtypeStruct((8, 16, 128), F32),
@@ -185,7 +186,7 @@
         out_specs=VMEM,
         compiler_params=PARAMS,
         name="sample",
-    )(jac, nbr, counts, chip, core, trial)
+    )(jac, nbr, counts, core, chip, trial)
 
 
 def merge_kernel(g_ref, b_ref, out_ref):
@@ -322,7 +323,7 @@
     core = lax.ppermute(own, ROWS, inside)
     chip = lax.ppermute(own, ROWS, across)
     g_group = lax.all_to_all(g_part, GROUP, 0, 0, tiled=True)
-    columns = sample(jac, nbr, count, chip, core, trial_basis.swapaxes(0, 1))
+    columns = sample(jac, nbr, count, core, chip, trial_basis.swapaxes(0, 1))
     parts = lax.all_to_all(merge(g_group, columns), "zh", 0, 0, tiled=True)
     pieces = lax.all_to_all(fold(parts, sample_inverse), CUBE, 0, 0, tiled=True)
     return finish(pieces).T

time: 68.2 us -> 66.9 us (0.981)
  blocking collectives: 42.8 us -> 42.1 us
    all_to_all x1, blocking collectives: 19.9 us -> 17.8 us  [shards(): pieces = lax.all_to_all(fold(parts, sample_inverse), CUBE, 0, 0, tiled=True)]
    ppermute x1, waiting for transfers between devices: 1.7 us -> 0.01 us  [shards(): chip = lax.ppermute(own, ROWS, across)]
    all_to_all x1, blocking collectives: 22.9 us -> 24.3 us  [shards(): parts = lax.all_to_all(merge(g_group, columns), 'zh', 0, 0, tiled=True)]
    ppermute x1, waiting for transfers between devices: 0.01 us -> 1.34 us  [shards(): core = lax.ppermute(own, ROWS, inside)]
where the time goes in v6:
time: 66.9 us; the launch traced here: 66.6 us
  blocking collectives  42.1 us (63%)
  starting transfers between devices  15.8 us (24%)
  Pallas kernels  6.5 us (10%)
  waiting for transfers between devices  1.34 us (2%)
  between operations  0.84 us (1%)
    all_to_all x1, blocking collectives, shards(): parts = lax.all_to_all(merge(g_group, columns), 'zh', 0, 0, tiled=True)  24.3 us
    all_to_all x1, blocking collectives, shards(): pieces = lax.all_to_all(fold(parts, sample_inverse), CUBE, 0, 0, tiled=True)  17.8 us
    all_to_all x1, starting transfers between devices, shards(): g_group = lax.all_to_all(g_part, GROUP, 0, 0, tiled=True)  10.3 us
    ppermute x1, starting transfers between devices, shards(): chip = lax.ppermute(own, ROWS, across)  3.53 us
    pallas_call x1, Pallas kernels, prepare(): pl.pallas_call(prepare_kernel, in_specs=[HBM, HBM, HBM, HBM, HBM], out_sp...  2.76 us
    ppermute x1, starting transfers between devices, shards(): core = lax.ppermute(own, ROWS, inside)  1.92 us
    pallas_call x1, Pallas kernels, sample(): pl.pallas_call(sample_kernel, out_shape=jax.ShapeDtypeStruct((8, 16, 128)...  1.48 us
  transfers between devices with their start and end apart: 3, of which 1 were waited for; matrix products, arithmetic and copies ran while one was open for 0% of the time, Pallas kernels for 2%

profile of v6, /device:TPU:1, one launch (start us, length us, event | category | flops | bytes accessed | tf_op | source)
XLA Modules:
  0.0 66.6 jit_solution(8727533806118381766)
XLA Ops:
  0.0 0.0 copy-start.3
  0.0 0.0 copy-start.2
  0.0 0.0 copy-start
  0.8 2.8 %prepare.1 = (f32[144,2,128]{2,1,0:T(2,128)}, f32[16,128]{1,0:T(8,128)}) custom-call(bf16[5,512,256]{2,1,0:T(8,128)(2,1)} %bitcast.14, bf16[5,512,128]{2,1,0:T(8,128)(2,1)} %bitcast.15, f32[5,7,16]{2,1,0:T(8,128)} %bitcast.10, s32[7,16]{1,0:T(8,128)} %bitcast.12, s32[1,1]{1,0:T(1,128)} %bitcast.7.count_hbm), custom_call_target="tpu_custom_call" | custom-call | tf_op jit(solution)/shard_map/prepare/pallas_call | solution.py:115
  3.5 0.0 copy-start.1
  3.5 10.3 %all-to-all-start = ((f32[144,2,128]{2,1,0:T(2,128)}), f32[144,2,128]{2,1,0:T(2,128)S(1)}, u32[]{:S(2)}, u32[]{:S(2)}) async-start(f32[144,2,128]{2,1,0:T(2,128)} %get-tuple-element.7), calls=%async_computation | async-start | bytes 294912 | tf_op jit(solution)/shard_map/all_to_all | solution.py:325
  13.9 3.5 %collective-permute-start.1 = (f32[16,128]{1,0:T(8,128)}, f32[16,128]{1,0:T(8,128)S(1)}, u32[]{:S(2)}, u32[]{:S(2)}) collective-permute-start(f32[16,128]{1,0:T(8,128)} %get-tuple-element.8), channel_id=1, source_target_pairs={{4,8},{12,16},{20,24},{28,32},{36,40},{44,48},{52,56},{60,64},{68,... | collective-permute-start | bytes 24584 | tf_op jit(solution)/shard_map/ppermute | solution.py:324
  17.4 1.9 %collective-permute-start = (f32[16,128]{1,0:T(8,128)}, f32[16,128]{1,0:T(8,128)S(1)}, u32[]{:S(2)}, u32[]{:S(2)}) collective-permute-start(f32[16,128]{1,0:T(8,128)} %get-tuple-element.8), channel_id=1, source_target_pairs={{0,4},{4,0},{8,12},{12,8},{16,20},{20,16},{24,28},{28,24},{32,36},... | collective-permute-start | bytes 24584 | tf_op jit(solution)/shard_map/ppermute | solution.py:323
  19.3 0.0 collective-permute-done.1.chip_ref
  19.3 1.3 %collective-permute-done.core_ref = f32[16,128]{1,0:T(8,128)S(1)} collective-permute-done((f32[16,128]{1,0:T(8,128)}, f32[16,128]{1,0:T(8,128)S(1)}, u32[]{:S(2)}, u32[]{:S(2)}) %collective-permute-start) | collective-permute-done | bytes 8224 | tf_op jit(solution)/shard_map/ppermute | solution.py:323
  20.7 0.0 copy-done.3
  20.7 0.0 copy-done.2
  20.7 0.0 copy-done
  20.7 1.5 %sample.1.b_ref = f32[8,16,128]{2,1,0:T(8,128)S(1)} custom-call(f32[5,7,16]{2,1,0:T(8,128)S(1)} %bitcast.11, s32[7,16]{1,0:T(8,128)S(1)} %bitcast.13, s32[1,1]{1,0:T(1,128)} %bitcast.8.count_ref, f32[16,128]{1,0:T(8,128)S(1)} %collective-permute-done.core_ref, f32[16,128]{1,0:T(8,128)S(1)} %collective-permute-done.1.chip_ref, bf16[5,512,256]{2,1,0:T(8,128)(2,1)S(1)} %bitcast.9), custom_call_target="tpu_custom_call" | custom-call | tf_op jit(solution)/shard_map/sample/pallas_call | solution.py:182
  22.2 0.0 all-to-all-done.g_ref
  22.2 0.2 merge.1
  22.4 24.3 %all_to_all.15.x_ref = s16[8,32,128]{2,1,0:T(8,128)(2,1)S(1)} all-to-all(s16[8,32,128]{2,1,0:T(8,128)(2,1)S(1)} %merge.1), channel_id=1, replica_groups=mesh['zh'=8,'zl'=2,'x'=4,'c'=2,'y'=4] {'zh'}, dimensions={0} | all-to-all | bytes 131072 | tf_op jit(solution)/shard_map/all_to_all | solution.py:327
  46.8 0.0 copy-done.1
  46.8 1.2 %fold.1 = f32[192,2,128]{2,1,0:T(2,128)S(1)} custom-call(s16[8,32,128]{2,1,0:T(8,128)(2,1)S(1)} %all_to_all.15.x_ref, f32[128,512]{1,0:T(8,128)S(1)} %copy-done.1), custom_call_target="tpu_custom_call" | custom-call | tf_op jit(solution)/shard_map/fold/pallas_call | solution.py:278
  47.9 17.8 %all_to_all.16.x_ref = f32[192,2,128]{2,1,0:T(2,128)S(1)} all-to-all(f32[192,2,128]{2,1,0:T(2,128)S(1)} %fold.1), channel_id=1, replica_groups=mesh['zh'=8,'zl'=2,'x'=4,'c'=2,'y'=4] {'zl','x','c','y'}, dimensions={0} | all-to-all | bytes 393216 | tf_op jit(solution)/shard_map/all_to_all | solution.py:328
  65.7 0.9 %finish.1 = f32[2,64]{1,0:T(2,128)} custom-call(f32[192,2,128]{2,1,0:T(2,128)S(1)} %all_to_all.16.x_ref), custom_call_target="tpu_custom_call" | custom-call | tf_op jit(solution)/shard_map/finish/pallas_call | solution.py:306
Async XLA Ops:
  0.0 20.7 %copy-start.3 = (s32[16,7]{0,1:T(8,128)S(1)}, s32[16,7]{0,1:T(8,128)}, u32[]{:S(2)}) copy-start(s32[16,7]{0,1:T(8,128)} %param.11) | copy-start | bytes 1348
  0.0 20.7 %copy-start.2 = (f32[16,7,5]{0,1,2:T(8,128)S(1)}, f32[16,7,5]{0,1,2:T(8,128)}, u32[]{:S(2)}) copy-start(f32[16,7,5]{0,1,2:T(8,128)} %param.10) | copy-start | bytes 6724
  0.0 20.7 %copy-start = (bf16[512,5,256]{2,0,1:T(8,128)(2,1)S(1)}, bf16[512,5,256]{2,0,1:T(8,128)(2,1)}, u32[]{:S(2)}) copy-start(bf16[512,5,256]{2,0,1:T(8,128)(2,1)} %param.9) | copy-start | bytes 3932164
  3.5 43.2 %copy-start.1 = (f32[128,512]{1,0:T(8,128)S(1)}, f32[128,512]{1,0:T(8,128)}, u32[]{:S(2)}) copy-start(f32[128,512]{1,0:T(8,128)} %s_ref.1) | copy-start | bytes 786436
  3.5 18.6 %all-to-all-start = ((f32[144,2,128]{2,1,0:T(2,128)}), f32[144,2,128]{2,1,0:T(2,128)S(1)}, u32[]{:S(2)}, u32[]{:S(2)}) async-start(f32[144,2,128]{2,1,0:T(2,128)} %get-tuple-element.7), calls=%async_computation | async-start | bytes 294912 | tf_op jit(solution)/shard_map/all_to_all | solution.py:325
  13.9 5.5 %collective-permute-start.1 = (f32[16,128]{1,0:T(8,128)}, f32[16,128]{1,0:T(8,128)S(1)}, u32[]{:S(2)}, u32[]{:S(2)}) collective-permute-start(f32[16,128]{1,0:T(8,128)} %get-tuple-element.8), channel_id=1, source_target_pairs={{4,8},{12,16},{20,24},{28,32},{36,40},{44,48},{52,56},{60,64},{68,... | collective-permute-start | bytes 24584 | tf_op jit(solution)/shard_map/ppermute | solution.py:324
  17.4 3.3 %collective-permute-start = (f32[16,128]{1,0:T(8,128)}, f32[16,128]{1,0:T(8,128)S(1)}, u32[]{:S(2)}, u32[]{:S(2)}) collective-permute-start(f32[16,128]{1,0:T(8,128)} %get-tuple-element.8), channel_id=1, source_target_pairs={{0,4},{4,0},{8,12},{12,8},{16,20},{20,16},{24,28},{28,24},{32,36},... | collective-permute-start | bytes 24584 | tf_op jit(solution)/shard_map/ppermute | solution.py:323

commit v7 on v6

--- a/solution.py
+++ b/solution.py
@@ -13,7 +13,7 @@
 BF16 = jnp.bfloat16
 NC, NB = 5, 7
 NBR, CNT = 40, 47
-GROUP_CNT, LOW_CNT, OWN_CNT, RANK, G_EXP, B_EXP = 96, 112, 113, 114, 115, 116
+LOW_CNT, OWN_CNT, RANK, G_EXP, B_EXP, GROUP_CNT = 96, 97, 98, 99, 100, 112
 TOP = 32000.0
 
 
@@ -95,7 +95,11 @@
     for copy in small:
         copy.wait()
     count = count_ref[0, 0].astype(F32)
-    table_ref[...] = table_of(jac_ref, nbr_ref, count)
+    table = table_of(jac_ref, nbr_ref, count)
+    table_ref[...] = table
+    packed = table[0:8, :] + pltpu.roll(table[8:16, :], 64, 1)
+    packed = packed + jnp.where(lanes((8, 128)) >= GROUP_CNT, count, 0.0)
+    packed = packed.reshape(4, 2, 128)
     acc = jnp.zeros((128, 256), F32)
     for j in range(NC):
         v_copies[j].wait()
@@ -107,8 +111,8 @@
     for p in range(16):
         for m in range(4):
             at = 32 * m + 2 * p
-            g_ref[9 * p + 2 * m : 9 * p + 2 * m + 2] = pairs[at : at + 2]
-        g_ref[9 * p + 8] = jnp.full((2, 128), count)
+            g_ref[12 * p + 2 * m : 12 * p + 2 * m + 2] = pairs[at : at + 2]
+        g_ref[12 * p + 8 : 12 * p + 12] = packed
 
 
 def prepare(test, deim, jac, nbr, counts):
@@ -117,7 +121,7 @@
         in_specs=[HBM, HBM, HBM, HBM, HBM],
         out_specs=[VMEM, VMEM],
         out_shape=[
-            jax.ShapeDtypeStruct((144, 2, 128), F32),
+            jax.ShapeDtypeStruct((192, 2, 128), F32),
             jax.ShapeDtypeStruct((16, 128), F32),
         ],
         scratch_shapes=[
@@ -132,87 +136,82 @@
     )(test, deim, jac, nbr, counts)
 
 
-def sample_kernel(jac_ref, nbr_ref, count_ref, core_ref, chip_ref, u_ref, out_ref):
-    own = table_of(jac_ref, nbr_ref, count_ref[...].astype(F32))
-    rank = jnp.floor(own[0:1, NBR : NBR + 1] * (1.0 / 512.0))
+def sample_kernel(x_ref, nbr_ref, edge_ref, u_ref, out_ref):
+    rank = jnp.floor(nbr_ref[0:1, 0:1].astype(F32) * (1.0 / 512.0))
+    place = rank - 16.0 * jnp.floor(rank * 0.0625)
+    lane = lanes((1, 128))
+    total = jnp.zeros((8, 2, 128), F32)
+    blank = jnp.zeros((4, 2, 128), F32)
+    near = [blank, blank, blank]
+    extra = jnp.zeros((1, 128), F32)
+    for p in range(16):
+        total = total + x_ref[12 * p : 12 * p + 8]
+        packed = x_ref[12 * p + 8 : 12 * p + 12]
+        near = [
+            near[k] + jnp.where((place == p + 1 - k)[None], packed, 0.0) for k in range(3)
+        ]
+        extra = extra + jnp.where(lane == GROUP_CNT + p, packed[0, 0:1, :], 0.0)
+    total = total.reshape(16, 128)
     slot = lax.broadcasted_iota(jnp.int32, (16, 128), 0).astype(F32)
     entry = lanes((16, 128)) < NBR
-    first = rank == 2.0 * jnp.floor(rank * 0.5)
-    chip, core = chip_ref[...], core_ref[...]
-    low = jnp.where(first, chip, core)
     tables = []
-    for rows in (low, own, jnp.where(first, core, chip)):
+    for k, edge in ((0, 0.0), (1, None), (2, 15.0)):
+        rows = near[k].reshape(8, 128)
+        rows = jnp.concatenate([rows, pltpu.roll(rows, 64, 1)], axis=0)
+        if edge is not None:
+            rows = jnp.where(place == edge, edge_ref[...], rows)
+        extra = extra + jnp.where(lane == LOW_CNT + k, rows[0:1, CNT : CNT + 1], 0.0) * (k < 2)
         dead = entry & (slot >= rows[:, CNT : CNT + 1])
         tables.append(jnp.where(dead, 0.0, rows))
-    table = jnp.concatenate(tables, axis=0)
-    near = [table[:, NBR + n : NBR + n + 1] - rank * 512.0 for n in range(NB)]
-    total = jnp.zeros((96, 256), F32)
-    values = [jnp.broadcast_to(table[:, k : k + 1], (48, 128)) for k in range(NBR)]
-    cell = lanes((48, 128)).astype(F32)
-    hits = [[cell + 128.0 * part == near[n] for n in range(NB)] for part in range(4)]
+    cell = lanes((16, 128)).astype(F32) + rank * 512.0
+    zero = jnp.zeros((16, 128), F32)
+
+    def weights(table, part, j):
+        at = cell + 128.0 * part
+        weight = zero
+        for n in range(NB):
+            hit = at == table[:, NBR + n : NBR + n + 1]
+            weight = weight + jnp.where(hit, table[:, 8 * j + n : 8 * j + n + 1], 0.0)
+        return weight
+
+    low, own, high = tables
+    sums = jnp.zeros((96, 256), F32)
     for j in range(NC):
-        weights = []
-        for part in range(4):
-            weight = jnp.where(hits[part][0], values[8 * j], 0.0)
-            for n in range(1, NB):
-                weight = weight + jnp.where(hits[part][n], values[8 * j + n], 0.0)
-            weights.append(weight)
-        weight = jnp.concatenate(weights, axis=1)
-        high = weight.astype(BF16)
-        rest = (weight - high.astype(F32)).astype(BF16)
-        total = total + jnp.dot(
-            jnp.concatenate([high, rest], axis=0), u_ref[j], preferred_element_type=F32
-        )
-    rows = total[0:48, :] + total[48:96, :]
-    exp = exponent(rows)
-    rows = jnp.concatenate([coded(rows, exp), jnp.zeros((80, 256), F32)], axis=0)
-    lane = lanes((1, 128))
-    extra = jnp.where(lane == LOW_CNT, low[0:1, CNT : CNT + 1], 0.0)
-    extra = extra + jnp.where(lane == OWN_CNT, own[0:1, CNT : CNT + 1], 0.0)
+        weight = jnp.concatenate(
+            [
+                jnp.concatenate([weights(low, 0, j), zero, zero, zero], axis=1),
+                jnp.concatenate([weights(own, part, j) for part in range(4)], axis=1),
+                jnp.concatenate([zero, zero, zero, weights(high, 3, j)], axis=1),
+            ],
+            axis=0,
+        )
+        upper = weight.astype(BF16)
+        rest = (weight - upper.astype(F32)).astype(BF16)
+        sums = sums + jnp.dot(
+            jnp.concatenate([upper, rest], axis=0), u_ref[j], preferred_element_type=F32
+        )
+    rows = sums[0:48, :] + sums[48:96, :]
+    b_exp, g_exp = exponent(rows), exponent(total)
+    rows = jnp.concatenate([coded(rows, b_exp), jnp.zeros((80, 256), F32)], axis=0)
     extra = extra + jnp.where(lane == RANK, rank, 0.0)
-    extra = extra + jnp.where(lane == B_EXP, exp, 0.0)
+    extra = extra + jnp.where(lane == B_EXP, b_exp, 0.0) + jnp.where(lane == G_EXP, g_exp, 0.0)
     cols = rows.T
+    code = coded(total, g_exp)
     for z in range(8):
         left = cols[32 * z : 32 * z + 16, :]
         right = pltpu.roll(cols[32 * z + 16 : 32 * z + 32, :], 48, 1)
-        out_ref[z, :, :] = left + right + extra
-
-
-def sample(jac, nbr, counts, core, chip, trial):
+        out_ref[z] = to_i16(jnp.concatenate([code, left + right + extra], axis=0))
+
+
+def sample(g_parts, nbr, edge, trial):
     return pl.pallas_call(
         sample_kernel,
-        out_shape=jax.ShapeDtypeStruct((8, 16, 128), F32),
-        in_specs=[VMEM] * 6,
+        out_shape=jax.ShapeDtypeStruct((8, 32, 128), jnp.int16),
+        in_specs=[VMEM] * 4,
         out_specs=VMEM,
         compiler_params=PARAMS,
         name="sample",
-    )(jac, nbr, counts, core, chip, trial)
-
-
-def merge_kernel(g_ref, b_ref, out_ref):
-    total = g_ref[0:8]
-    for p in range(1, 16):
-        total = total + g_ref[9 * p : 9 * p + 8]
-    total = total.reshape(16, 128)
-    exp = exponent(total)
-    code = coded(total, exp)
-    lane = lanes((1, 128))
-    extra = jnp.where(lane == G_EXP, exp, 0.0)
-    for p in range(16):
-        extra = extra + jnp.where(lane == GROUP_CNT + p, g_ref[9 * p + 8][0:1, :], 0.0)
-    for z in range(8):
-        out_ref[z] = to_i16(jnp.concatenate([code, b_ref[z] + extra], axis=0))
-
-
-def merge(g_parts, columns):
-    return pl.pallas_call(
-        merge_kernel,
-        out_shape=jax.ShapeDtypeStruct((8, 32, 128), jnp.int16),
-        in_specs=[VMEM] * 2,
-        out_specs=VMEM,
-        compiler_params=PARAMS,
-        name="merge",
-    )(g_parts, columns)
+    )(g_parts, nbr, edge, trial)
 
 
 def fold_kernel(x_ref, s_ref, out_ref):
@@ -316,15 +315,13 @@
 def shards(test_basis, deim_basis, trial_basis, jacobian, neighbours, counts, sample_inverse):
     jac, nbr, count = jacobian.transpose(2, 1, 0), neighbours.T, counts.reshape(1, 1)
     g_part, own = prepare(test_basis.swapaxes(0, 1), deim_basis.swapaxes(0, 1), jac, nbr, count)
-    groups = lax.axis_size(ROWS)
-    across = [(i, i + 1) for i in range(1, groups - 1, 2)]
+    groups, group = lax.axis_size(ROWS), lax.axis_size(GROUP)
+    across = [(i - 1, i) for i in range(group, groups, group)]
     across += [(target, source) for source, target in across]
-    inside = [(i, i ^ 1) for i in range(groups)]
-    core = lax.ppermute(own, ROWS, inside)
-    chip = lax.ppermute(own, ROWS, across)
+    edge = lax.ppermute(own, ROWS, across)
     g_group = lax.all_to_all(g_part, GROUP, 0, 0, tiled=True)
-    columns = sample(jac, nbr, count, core, chip, trial_basis.swapaxes(0, 1))
-    parts = lax.all_to_all(merge(g_group, columns), "zh", 0, 0, tiled=True)
+    sent = sample(g_group, nbr, edge, trial_basis.swapaxes(0, 1))
+    parts = lax.all_to_all(sent, "zh", 0, 0, tiled=True)
     pieces = lax.all_to_all(fold(parts, sample_inverse), CUBE, 0, 0, tiled=True)
     return finish(pieces).T
 

time: 66.9 us -> 65.2 us (0.975)
  starting transfers between devices: 15.8 us -> 11 us
  waiting for transfers between devices: 1.34 us -> 6.08 us
  blocking collectives: 42.1 us -> 40.9 us
    all_to_all x1, waiting for transfers between devices: 0.01 us -> 6.07 us  [shards(): g_group = lax.all_to_all(g_part, GROUP, 0, 0, tiled=True)]
    ppermute x2 -> x1, starting transfers between devices: 5.45 us -> 0.65 us  [shards(): edge = lax.ppermute(own, ROWS, across)]
    all_to_all x1, blocking collectives: 24.3 us -> 22.7 us  [shards(): parts = lax.all_to_all(sent, 'zh', 0, 0, tiled=True)]
    ppermute x2 -> x1, waiting for transfers between devices: 1.34 us -> 0.01 us  [shards(): edge = lax.ppermute(own, ROWS, across)]
    pallas_call x2 -> x1, Pallas kernels: 1.68 us -> 1.22 us  [sample(): pl.pallas_call(sample_kernel, out_shape=jax.ShapeDtypeStruct((8, 32, 128)...]
  transfers between devices with their start and end apart: 3 -> 2, of which waited for: 1 -> 1; matrix products, arithmetic and copies ran while one was open for 0% -> 0% of each run, Pallas kernels for 2% -> 0%
where the time goes in v7:
time: 65.2 us; the launch traced here: 64.9 us
  blocking collectives  40.9 us (63%)
  starting transfers between devices  11 us (17%)
  waiting for transfers between devices  6.08 us (9%)
  Pallas kernels  6.07 us (9%)
  between operations  0.8 us (1%)
    all_to_all x1, blocking collectives, shards(): parts = lax.all_to_all(sent, 'zh', 0, 0, tiled=True)  22.7 us
    all_to_all x1, blocking collectives, shards(): pieces = lax.all_to_all(fold(parts, sample_inverse), CUBE, 0, 0, tiled=True)  18.3 us
    all_to_all x1, starting transfers between devices, shards(): g_group = lax.all_to_all(g_part, GROUP, 0, 0, tiled=True)  10.3 us
    all_to_all x1, waiting for transfers between devices, shards(): g_group = lax.all_to_all(g_part, GROUP, 0, 0, tiled=True)  6.07 us
    pallas_call x1, Pallas kernels, prepare(): pl.pallas_call(prepare_kernel, in_specs=[HBM, HBM, HBM, HBM, HBM], out_sp...  2.8 us
  transfers between devices with their start and end apart: 2, of which 1 were waited for; matrix products, arithmetic and copies ran while one was open for 0% of the time, Pallas kernels for 0%

profile of v7, /device:TPU:1, one launch (start us, length us, event | category | flops | bytes accessed | tf_op | source)
XLA Modules:
  0.0 64.9 jit_solution(8123140263356246285)
XLA Ops:
  0.0 0.0 copy-start.2
  0.0 0.0 copy-start
  0.8 2.8 %prepare.1 = (f32[192,2,128]{2,1,0:T(2,128)}, f32[16,128]{1,0:T(8,128)}) custom-call(bf16[5,512,256]{2,1,0:T(8,128)(2,1)} %bitcast.11, bf16[5,512,128]{2,1,0:T(8,128)(2,1)} %bitcast.12, f32[5,7,16]{2,1,0:T(8,128)} %bitcast.13, s32[7,16]{1,0:T(8,128)} %bitcast.9, s32[1,1]{1,0:T(1,128)} %bitcast.7.count_hbm), custom_call_target="tpu_custom_call" | custom-call | tf_op jit(solution)/shard_map/prepare/pallas_call | solution.py:119
  3.6 0.0 copy-start.1
  3.6 10.3 %all-to-all-start = ((f32[192,2,128]{2,1,0:T(2,128)}), f32[192,2,128]{2,1,0:T(2,128)S(1)}, u32[]{:S(2)}, u32[]{:S(2)}) async-start(f32[192,2,128]{2,1,0:T(2,128)} %get-tuple-element.7), calls=%async_computation | async-start | bytes 393216 | tf_op jit(solution)/shard_map/all_to_all | solution.py:322
  13.9 0.6 %collective-permute-start = (f32[16,128]{1,0:T(8,128)}, f32[16,128]{1,0:T(8,128)S(1)}, u32[]{:S(2)}, u32[]{:S(2)}) collective-permute-start(f32[16,128]{1,0:T(8,128)} %get-tuple-element.8), channel_id=1, source_target_pairs={{60,64},{124,128},{188,192},{252,256},{316,320},{380,384},{444,448... | collective-permute-start | bytes 24584 | tf_op jit(solution)/shard_map/ppermute | solution.py:321
  14.6 0.0 collective-permute-done.edge_ref
  14.6 6.1 %all-to-all-done.x_ref = f32[192,2,128]{2,1,0:T(2,128)S(1)} async-done(((f32[192,2,128]{2,1,0:T(2,128)}), f32[192,2,128]{2,1,0:T(2,128)S(1)}, u32[]{:S(2)}, u32[]{:S(2)}) %all-to-all-start) | async-done | bytes 196640 | tf_op jit(solution)/shard_map/all_to_all | solution.py:322
  20.7 0.0 copy-done.2
  20.7 0.0 copy-done
  20.7 1.2 %sample.1 = s16[8,32,128]{2,1,0:T(8,128)(2,1)S(1)} custom-call(f32[192,2,128]{2,1,0:T(2,128)S(1)} %all-to-all-done.x_ref, s32[7,16]{1,0:T(8,128)S(1)} %bitcast.10, f32[16,128]{1,0:T(8,128)S(1)} %collective-permute-done.edge_ref, bf16[5,512,256]{2,1,0:T(8,128)(2,1)S(1)} %bitcast.8), custom_call_target="tpu_custom_call" | custom-call | tf_op jit(solution)/shard_map/sample/pallas_call | solution.py:207
  21.9 22.7 %all_to_all.15.x_ref = s16[8,32,128]{2,1,0:T(8,128)(2,1)S(1)} all-to-all(s16[8,32,128]{2,1,0:T(8,128)(2,1)S(1)} %sample.1), channel_id=1, replica_groups=mesh['zh'=8,'zl'=2,'x'=4,'c'=2,'y'=4] {'zh'}, dimensions={0} | all-to-all | bytes 131072 | tf_op jit(solution)/shard_map/all_to_all | solution.py:324
  44.5 0.0 copy-done.1
  44.6 1.2 %fold.1 = f32[192,2,128]{2,1,0:T(2,128)S(1)} custom-call(s16[8,32,128]{2,1,0:T(8,128)(2,1)S(1)} %all_to_all.15.x_ref, f32[128,512]{1,0:T(8,128)S(1)} %copy-done.1), custom_call_target="tpu_custom_call" | custom-call | tf_op jit(solution)/shard_map/fold/pallas_call | solution.py:277
  45.7 18.3 %all_to_all.16.x_ref = f32[192,2,128]{2,1,0:T(2,128)S(1)} all-to-all(f32[192,2,128]{2,1,0:T(2,128)S(1)} %fold.1), channel_id=1, replica_groups=mesh['zh'=8,'zl'=2,'x'=4,'c'=2,'y'=4] {'zl','x','c','y'}, dimensions={0} | all-to-all | bytes 393216 | tf_op jit(solution)/shard_map/all_to_all | solution.py:325
  64.0 0.9 %finish.1 = f32[2,64]{1,0:T(2,128)} custom-call(f32[192,2,128]{2,1,0:T(2,128)S(1)} %all_to_all.16.x_ref), custom_call_target="tpu_custom_call" | custom-call | tf_op jit(solution)/shard_map/finish/pallas_call | solution.py:305
Async XLA Ops:
  0.0 20.7 %copy-start.2 = (s32[16,7]{0,1:T(8,128)S(1)}, s32[16,7]{0,1:T(8,128)}, u32[]{:S(2)}) copy-start(s32[16,7]{0,1:T(8,128)} %param.11) | copy-start | bytes 1348
  0.0 20.7 %copy-start = (bf16[512,5,256]{2,0,1:T(8,128)(2,1)S(1)}, bf16[512,5,256]{2,0,1:T(8,128)(2,1)}, u32[]{:S(2)}) copy-start(bf16[512,5,256]{2,0,1:T(8,128)(2,1)} %param.9) | copy-start | bytes 3932164
  3.6 41.0 %copy-start.1 = (f32[128,512]{1,0:T(8,128)S(1)}, f32[128,512]{1,0:T(8,128)}, u32[]{:S(2)}) copy-start(f32[128,512]{1,0:T(8,128)} %s_ref.1) | copy-start | bytes 786436
  3.6 17.1 %all-to-all-start = ((f32[192,2,128]{2,1,0:T(2,128)}), f32[192,2,128]{2,1,0:T(2,128)S(1)}, u32[]{:S(2)}, u32[]{:S(2)}) async-start(f32[192,2,128]{2,1,0:T(2,128)} %get-tuple-element.7), calls=%async_computation | async-start | bytes 393216 | tf_op jit(solution)/shard_map/all_to_all | solution.py:322
  13.9 0.7 %collective-permute-start = (f32[16,128]{1,0:T(8,128)}, f32[16,128]{1,0:T(8,128)S(1)}, u32[]{:S(2)}, u32[]{:S(2)}) collective-permute-start(f32[16,128]{1,0:T(8,128)} %get-tuple-element.8), channel_id=1, source_target_pairs={{60,64},{124,128},{188,192},{252,256},{316,320},{380,384},{444,448... | collective-permute-start | bytes 24584 | tf_op jit(solution)/shard_map/ppermute | solution.py:321

commit v8 on v7

--- a/solution.py
+++ b/solution.py
@@ -136,7 +136,57 @@
     )(test, deim, jac, nbr, counts)
 
 
-def sample_kernel(x_ref, nbr_ref, edge_ref, u_ref, out_ref):
+def halves(x):
+    upper = x.astype(BF16)
+    return upper, (x - upper.astype(F32)).astype(BF16)
+
+
+def alive(rows):
+    slot = lax.broadcasted_iota(jnp.int32, (16, 128), 0).astype(F32)
+    dead = (lanes((16, 128)) < NBR) & (slot >= rows[:, CNT : CNT + 1])
+    return jnp.where(dead, 0.0, rows)
+
+
+def weights(table, cell, j):
+    weight = jnp.zeros((16, 128), F32)
+    for n in range(NB):
+        hit = cell == table[:, NBR + n : NBR + n + 1]
+        weight = weight + jnp.where(hit, table[:, 8 * j + n : 8 * j + n + 1], 0.0)
+    return weight
+
+
+def own_kernel(table_ref, u_ref, s_ref, sums_ref, upper_ref, rest_ref):
+    table = table_ref[...]
+    rank = jnp.floor(table[0:1, NBR : NBR + 1] * (1.0 / 512.0))
+    own = alive(table)
+    cell = lanes((16, 128)).astype(F32) + rank * 512.0
+    sums = jnp.zeros((32, 256), F32)
+    for j in range(NC):
+        parts = [weights(own, cell + 128.0 * part, j) for part in range(4)]
+        pieces = halves(jnp.concatenate(parts, axis=1))
+        sums = sums + jnp.dot(
+            jnp.concatenate(pieces, axis=0), u_ref[j], preferred_element_type=F32
+        )
+    sums_ref[...] = sums[0:16, :] + sums[16:32, :]
+    upper_ref[...], rest_ref[...] = halves(s_ref[...])
+
+
+def own_part(table, trial, inverse):
+    return pl.pallas_call(
+        own_kernel,
+        out_shape=[
+            jax.ShapeDtypeStruct((16, 256), F32),
+            jax.ShapeDtypeStruct(inverse.shape, BF16),
+            jax.ShapeDtypeStruct(inverse.shape, BF16),
+        ],
+        in_specs=[VMEM] * 3,
+        out_specs=[VMEM] * 3,
+        compiler_params=PARAMS,
+        name="own_part",
+    )(table, trial, inverse)
+
+
+def sample_kernel(x_ref, nbr_ref, edge_ref, own_ref, u_ref, out_ref):
     rank = jnp.floor(nbr_ref[0:1, 0:1].astype(F32) * (1.0 / 512.0))
     place = rank - 16.0 * jnp.floor(rank * 0.0625)
     lane = lanes((1, 128))
@@ -152,45 +202,30 @@
         ]
         extra = extra + jnp.where(lane == GROUP_CNT + p, packed[0, 0:1, :], 0.0)
     total = total.reshape(16, 128)
-    slot = lax.broadcasted_iota(jnp.int32, (16, 128), 0).astype(F32)
-    entry = lanes((16, 128)) < NBR
     tables = []
     for k, edge in ((0, 0.0), (1, None), (2, 15.0)):
         rows = near[k].reshape(8, 128)
         rows = jnp.concatenate([rows, pltpu.roll(rows, 64, 1)], axis=0)
         if edge is not None:
             rows = jnp.where(place == edge, edge_ref[...], rows)
-        extra = extra + jnp.where(lane == LOW_CNT + k, rows[0:1, CNT : CNT + 1], 0.0) * (k < 2)
-        dead = entry & (slot >= rows[:, CNT : CNT + 1])
-        tables.append(jnp.where(dead, 0.0, rows))
+        if k < 2:
+            extra = extra + jnp.where(lane == LOW_CNT + k, rows[0:1, CNT : CNT + 1], 0.0)
+        tables.append(alive(rows))
     cell = lanes((16, 128)).astype(F32) + rank * 512.0
-    zero = jnp.zeros((16, 128), F32)
-
-    def weights(table, part, j):
-        at = cell + 128.0 * part
-        weight = zero
-        for n in range(NB):
-            hit = at == table[:, NBR + n : NBR + n + 1]
-            weight = weight + jnp.where(hit, table[:, 8 * j + n : 8 * j + n + 1], 0.0)
-        return weight
-
-    low, own, high = tables
-    sums = jnp.zeros((96, 256), F32)
-    for j in range(NC):
-        weight = jnp.concatenate(
-            [
-                jnp.concatenate([weights(low, 0, j), zero, zero, zero], axis=1),
-                jnp.concatenate([weights(own, part, j) for part in range(4)], axis=1),
-                jnp.concatenate([zero, zero, zero, weights(high, 3, j)], axis=1),
-            ],
-            axis=0,
-        )
-        upper = weight.astype(BF16)
-        rest = (weight - upper.astype(F32)).astype(BF16)
-        sums = sums + jnp.dot(
-            jnp.concatenate([upper, rest], axis=0), u_ref[j], preferred_element_type=F32
-        )
-    rows = sums[0:48, :] + sums[48:96, :]
+    low = jnp.zeros((32, 256), F32)
+    high = jnp.zeros((32, 256), F32)
+    for j in range(NC):
+        pieces = halves(weights(tables[0], cell, j))
+        low = low + jnp.dot(
+            jnp.concatenate(pieces, axis=0), u_ref[j, 0:128, :], preferred_element_type=F32
+        )
+        pieces = halves(weights(tables[2], cell + 384.0, j))
+        high = high + jnp.dot(
+            jnp.concatenate(pieces, axis=0), u_ref[j, 384:512, :], preferred_element_type=F32
+        )
+    rows = jnp.concatenate(
+        [low[0:16, :] + low[16:32, :], own_ref[...], high[0:16, :] + high[16:32, :]], axis=0
+    )
     b_exp, g_exp = exponent(rows), exponent(total)
     rows = jnp.concatenate([coded(rows, b_exp), jnp.zeros((80, 256), F32)], axis=0)
     extra = extra + jnp.where(lane == RANK, rank, 0.0)
@@ -203,18 +238,18 @@
         out_ref[z] = to_i16(jnp.concatenate([code, left + right + extra], axis=0))
 
 
-def sample(g_parts, nbr, edge, trial):
+def sample(g_parts, nbr, edge, own, trial):
     return pl.pallas_call(
         sample_kernel,
         out_shape=jax.ShapeDtypeStruct((8, 32, 128), jnp.int16),
-        in_specs=[VMEM] * 4,
+        in_specs=[VMEM] * 5,
         out_specs=VMEM,
         compiler_params=PARAMS,
         name="sample",
-    )(g_parts, nbr, edge, trial)
-
-
-def fold_kernel(x_ref, s_ref, out_ref):
+    )(g_parts, nbr, edge, own, trial)
+
+
+def fold_kernel(x_ref, upper_ref, rest_ref, out_ref):
     blocks = [from_i16(x_ref[z]) for z in range(8)]
     info = jnp.concatenate([block[16:17, :] for block in blocks], axis=0)
     lane = lanes((8, 128))
@@ -240,29 +275,34 @@
     offset = jnp.sum(lower, axis=1, keepdims=True)
     shift = jnp.where(lane < 16, -column(LOW_CNT), jnp.where(lane < 32, 0.0, column(OWN_CNT)))
     ids = jnp.where(lane < 48, offset + shift + (lane % 16).astype(F32), -1.0)
-    slots = lanes((1, 128)) < 48
+    at = lanes((1, 128))
     mode = lax.broadcasted_iota(jnp.int32, (512, 128), 0).astype(F32)
-    sampled = jnp.zeros((32, 512), F32)
-    for z in range(8):
-        hot = jnp.where(mode == ids[z : z + 1, :], 1.0, 0.0).astype(BF16)
-        both = decoded(blocks[z][16:32, :])
-        both = jnp.concatenate([both, pltpu.roll(both, 80, 1)], axis=0)
-        cols = jnp.where(slots, both, 0.0)
-        high = cols.astype(BF16)
-        rest = (cols - high.astype(F32)).astype(BF16)
-        part = lax.dot_general(
-            jnp.concatenate([high, rest], axis=0),
+    sampled = jnp.zeros((64, 512), F32)
+    for z in range(0, 8, 2):
+        here, there = (
+            decoded(blocks[k][16:32, :]) * b_scale[k : k + 1, :] for k in (z, z + 1)
+        )
+        first = jnp.where(at < 48, here, jnp.where(at < 96, pltpu.roll(there, 48, 1), 0.0))
+        second = jnp.where(at < 48, pltpu.roll(here, 80, 1), jnp.where(at < 96, there, 0.0))
+        row = jnp.where(at < 48, ids[z : z + 1, :], pltpu.roll(ids[z + 1 : z + 2, :], 48, 1))
+        hot = jnp.where(mode == row, 1.0, 0.0).astype(BF16)
+        pieces = halves(jnp.concatenate([first, second], axis=0))
+        sampled = sampled + lax.dot_general(
+            jnp.concatenate(pieces, axis=0),
             hot,
             (((1,), (1,)), ((), ())),
             preferred_element_type=F32,
         )
-        sampled = sampled + (part[0:32, :] + part[32:64, :]) * b_scale[z : z + 1, :]
+    sampled = sampled[0:32, :] + sampled[32:64, :]
+    upper, rest = halves(sampled)
     c = lax.dot_general(
-        sampled,
-        s_ref[...],
+        jnp.concatenate([upper, rest], axis=0),
+        upper_ref[...],
         (((1,), (1,)), ((), ())),
-        precision=lax.Precision.HIGHEST,
         preferred_element_type=F32,
+    )
+    c = (c[0:32, :] + c[32:64, :]) + lax.dot_general(
+        upper, rest_ref[...], (((1,), (1,)), ((), ())), preferred_element_type=F32
     )
     g_pairs = total.reshape(8, 2, 128)
     c_pairs = c.reshape(16, 2, 128)
@@ -273,32 +313,29 @@
             out_ref[at + 2] = c_pairs[p]
 
 
-def fold(parts, inverse):
+def fold(parts, upper, rest):
     return pl.pallas_call(
         fold_kernel,
         out_shape=jax.ShapeDtypeStruct((192, 2, 128), F32),
-        in_specs=[VMEM] * 2,
+        in_specs=[VMEM] * 3,
         out_specs=VMEM,
         compiler_params=PARAMS,
         name="fold",
-    )(parts, inverse)
+    )(parts, upper, rest)
 
 
 def finish_kernel(x_ref, out_ref):
-    result = jnp.zeros((2, 64), F32)
+    sums = [jnp.zeros((64, 128), F32), jnp.zeros((64, 128), F32)]
     for m in range(4):
         rows = [x_ref[3 * (4 * p + m) : 3 * (4 * p + m) + 2] for p in range(16)]
+        rows = jnp.concatenate(rows, axis=0).reshape(64, 128)
         c = x_ref[3 * m + 2]
         for p in range(1, 16):
             c = c + x_ref[3 * (4 * p + m) + 2]
-        result = result + lax.dot_general(
-            c,
-            jnp.concatenate(rows, axis=0).reshape(64, 128),
-            (((1,), (1,)), ((), ())),
-            precision=lax.Precision.HIGHEST,
-            preferred_element_type=F32,
-        )
-    out_ref[...] = result
+        sums = [sums[j] + rows * c[j : j + 1, :] for j in range(2)]
+    total = jnp.sum(jnp.concatenate(sums, axis=0).T, axis=0, keepdims=True)
+    out_ref[0:1, :] = total[:, 0:64]
+    out_ref[1:2, :] = total[:, 64:128]
 
 
 def finish(parts):
@@ -320,9 +357,11 @@
     across += [(target, source) for source, target in across]
     edge = lax.ppermute(own, ROWS, across)
     g_group = lax.all_to_all(g_part, GROUP, 0, 0, tiled=True)
-    sent = sample(g_group, nbr, edge, trial_basis.swapaxes(0, 1))
+    trial = trial_basis.swapaxes(0, 1)
+    mine, upper, rest = own_part(own, trial, sample_inverse)
+    sent = sample(g_group, nbr, edge, mine, trial)
     parts = lax.all_to_all(sent, "zh", 0, 0, tiled=True)
-    pieces = lax.all_to_all(fold(parts, sample_inverse), CUBE, 0, 0, tiled=True)
+    pieces = lax.all_to_all(fold(parts, upper, rest), CUBE, 0, 0, tiled=True)
     return finish(pieces).T
 
 

time: 65.2 us -> 64.4 us (0.988)
  waiting for transfers between devices: 6.08 us -> 4.87 us
  local copies, waits for them, and re-layouts: 0.01 us -> 0.7 us
    all_to_all x1, waiting for transfers between devices: 6.07 us -> 4.86 us  [shards(): g_group = lax.all_to_all(g_part, GROUP, 0, 0, tiled=True)]
    unnamed x6 -> x8, local copies, waits for them, and re-layouts: 0.01 us -> 0.7 us
  transfers between devices with their start and end apart: 2 -> 2, of which waited for: 1 -> 1; matrix products, arithmetic and copies ran while one was open for 0% -> 0% of each run, Pallas kernels for 0% -> 1%
where the time goes in v8:
time: 64.4 us; the launch traced here: 64.1 us
  blocking collectives  40.9 us (64%)
  starting transfers between devices  10.8 us (17%)
  Pallas kernels  5.89 us (9%)
  waiting for transfers between devices  4.87 us (8%)
  between operations  0.84 us (1%)
  local copies, waits for them, and re-layouts  0.7 us (1%)
    all_to_all x1, blocking collectives, shards(): parts = lax.all_to_all(sent, 'zh', 0, 0, tiled=True)  22.7 us
    all_to_all x1, blocking collectives, shards(): pieces = lax.all_to_all(fold(parts, upper, rest), CUBE, 0, 0, tiled=True)  18.3 us
    all_to_all x1, starting transfers between devices, shards(): g_group = lax.all_to_all(g_part, GROUP, 0, 0, tiled=True)  10.2 us
    all_to_all x1, waiting for transfers between devices, shards(): g_group = lax.all_to_all(g_part, GROUP, 0, 0, tiled=True)  4.86 us
    pallas_call x1, Pallas kernels, prepare(): pl.pallas_call(prepare_kernel, in_specs=[HBM, HBM, HBM, HBM, HBM], out_sp...  2.8 us
  transfers between devices with their start and end apart: 2, of which 1 were waited for; matrix products, arithmetic and copies ran while one was open for 0% of the time, Pallas kernels for 1%

profile of v8, /device:TPU:1, one launch (start us, length us, event | category | flops | bytes accessed | tf_op | source)
XLA Modules:
  0.0 64.1 jit_solution(15924374977061740589)
XLA Ops:
  0.0 0.0 copy-start.1
  0.0 0.0 copy-start
  0.8 2.8 %prepare.1 = (f32[192,2,128]{2,1,0:T(2,128)}, f32[16,128]{1,0:T(8,128)}) custom-call(bf16[5,512,256]{2,1,0:T(8,128)(2,1)} %bitcast.12, bf16[5,512,128]{2,1,0:T(8,128)(2,1)} %bitcast.13, f32[5,7,16]{2,1,0:T(8,128)} %bitcast.14, s32[7,16]{1,0:T(8,128)} %bitcast.10, s32[1,1]{1,0:T(1,128)} %bitcast.7.count_hbm), custom_call_target="tpu_custom_call" | custom-call | tf_op jit(solution)/shard_map/prepare/pallas_call | solution.py:119
  3.6 0.0 copy-start.2
  3.6 10.2 %all-to-all-start = ((f32[192,2,128]{2,1,0:T(2,128)}), f32[192,2,128]{2,1,0:T(2,128)S(1)}, u32[]{:S(2)}, u32[]{:S(2)}) async-start(f32[192,2,128]{2,1,0:T(2,128)} %get-tuple-element.10), calls=%async_computation | async-start | bytes 393216 | tf_op jit(solution)/shard_map/all_to_all | solution.py:359
  13.8 0.6 %collective-permute-start = (f32[16,128]{1,0:T(8,128)}, f32[16,128]{1,0:T(8,128)S(1)}, u32[]{:S(2)}, u32[]{:S(2)}) collective-permute-start(f32[16,128]{1,0:T(8,128)} %get-tuple-element.11.table_ref), channel_id=1, source_target_pairs={{60,64},{124,128},{188,192},{252,256},{316,320},{380,384},{444,448... | collective-permute-start | bytes 24584 | tf_op jit(solution)/shard_map/ppermute | solution.py:358
  14.4 0.0 copy-done.1
  14.5 0.0 copy-done
  14.5 0.0 copy-start.3
  14.5 0.7 %copy-done.3 = f32[16,128]{1,0:T(8,128)S(1)} copy-done((f32[16,128]{1,0:T(8,128)S(1)}, f32[16,128]{1,0:T(8,128)}, u32[]{:S(2)}) %copy-start.3) | copy-done | bytes 8216
  15.2 0.5 own_part.1
  15.7 0.0 collective-permute-done.edge_ref
  15.7 4.9 %all-to-all-done.x_ref = f32[192,2,128]{2,1,0:T(2,128)S(1)} async-done(((f32[192,2,128]{2,1,0:T(2,128)}), f32[192,2,128]{2,1,0:T(2,128)S(1)}, u32[]{:S(2)}, u32[]{:S(2)}) %all-to-all-start) | async-done | bytes 196640 | tf_op jit(solution)/shard_map/all_to_all | solution.py:359
  20.5 0.0 copy-done.2
  20.5 1.0 %sample.1 = s16[8,32,128]{2,1,0:T(8,128)(2,1)S(1)} custom-call(f32[192,2,128]{2,1,0:T(2,128)S(1)} %all-to-all-done.x_ref, s32[7,16]{1,0:T(8,128)S(1)} %bitcast.11, f32[16,128]{1,0:T(8,128)S(1)} %collective-permute-done.edge_ref, f32[16,256]{1,0:T(8,128)S(1)} %get-tuple-element.12.own_ref, bf16[5,512,256]{2,1,0:T(8,128)(2,1)S(1)} %bitcast.9), custom_call_target="tpu_custom_call" | custom-call | tf_op jit(solution)/shard_map/sample/pallas_call | solution.py:242
  21.6 22.7 %all_to_all.15.x_ref = s16[8,32,128]{2,1,0:T(8,128)(2,1)S(1)} all-to-all(s16[8,32,128]{2,1,0:T(8,128)(2,1)S(1)} %sample.1), channel_id=1, replica_groups=mesh['zh'=8,'zl'=2,'x'=4,'c'=2,'y'=4] {'zh'}, dimensions={0} | all-to-all | bytes 131072 | tf_op jit(solution)/shard_map/all_to_all | solution.py:363
  44.2 0.8 %fold.1 = f32[192,2,128]{2,1,0:T(2,128)S(1)} custom-call(s16[8,32,128]{2,1,0:T(8,128)(2,1)S(1)} %all_to_all.15.x_ref, bf16[128,512]{1,0:T(8,128)(2,1)S(1)} %get-tuple-element.13.upper_ref, bf16[128,512]{1,0:T(8,128)(2,1)S(1)} %get-tuple-element.14.rest_ref), custom_call_target="tpu_custom_call" | custom-call | tf_op jit(solution)/shard_map/fold/pallas_call | solution.py:317
  45.0 18.3 %all_to_all.16.x_ref = f32[192,2,128]{2,1,0:T(2,128)S(1)} all-to-all(f32[192,2,128]{2,1,0:T(2,128)S(1)} %fold.1), channel_id=1, replica_groups=mesh['zh'=8,'zl'=2,'x'=4,'c'=2,'y'=4] {'zl','x','c','y'}, dimensions={0} | all-to-all | bytes 393216 | tf_op jit(solution)/shard_map/all_to_all | solution.py:364
  63.3 0.8 %finish.1 = f32[2,64]{1,0:T(2,128)} custom-call(f32[192,2,128]{2,1,0:T(2,128)S(1)} %all_to_all.16.x_ref), custom_call_target="tpu_custom_call" | custom-call | tf_op jit(solution)/shard_map/finish/pallas_call | solution.py:342
Async XLA Ops:
  0.0 14.5 %copy-start.1 = (f32[128,512]{1,0:T(8,128)S(1)}, f32[128,512]{1,0:T(8,128)}, u32[]{:S(2)}) copy-start(f32[128,512]{1,0:T(8,128)} %s_ref.1) | copy-start | bytes 786436
  0.0 14.5 %copy-start = (bf16[512,5,256]{2,0,1:T(8,128)(2,1)S(1)}, bf16[512,5,256]{2,0,1:T(8,128)(2,1)}, u32[]{:S(2)}) copy-start(bf16[512,5,256]{2,0,1:T(8,128)(2,1)} %param.9) | copy-start | bytes 3932164
  3.6 17.0 %copy-start.2 = (s32[16,7]{0,1:T(8,128)S(1)}, s32[16,7]{0,1:T(8,128)}, u32[]{:S(2)}) copy-start(s32[16,7]{0,1:T(8,128)} %param.11) | copy-start | bytes 1348
  3.6 16.9 %all-to-all-start = ((f32[192,2,128]{2,1,0:T(2,128)}), f32[192,2,128]{2,1,0:T(2,128)S(1)}, u32[]{:S(2)}, u32[]{:S(2)}) async-start(f32[192,2,128]{2,1,0:T(2,128)} %get-tuple-element.10), calls=%async_computation | async-start | bytes 393216 | tf_op jit(solution)/shard_map/all_to_all | solution.py:359
  13.8 1.9 %collective-permute-start = (f32[16,128]{1,0:T(8,128)}, f32[16,128]{1,0:T(8,128)S(1)}, u32[]{:S(2)}, u32[]{:S(2)}) collective-permute-start(f32[16,128]{1,0:T(8,128)} %get-tuple-element.11.table_ref), channel_id=1, source_target_pairs={{60,64},{124,128},{188,192},{252,256},{316,320},{380,384},{444,448... | collective-permute-start | bytes 24584 | tf_op jit(solution)/shard_map/ppermute | solution.py:358
  14.5 0.7 %copy-start.3 = (f32[16,128]{1,0:T(8,128)S(1)}, f32[16,128]{1,0:T(8,128)}, u32[]{:S(2)}) copy-start(f32[16,128]{1,0:T(8,128)} %get-tuple-element.11.table_ref) | copy-start | bytes 24580

commit v9 on v8

--- a/solution.py
+++ b/solution.py
@@ -155,8 +155,9 @@
     return weight
 
 
-def own_kernel(table_ref, u_ref, s_ref, sums_ref, upper_ref, rest_ref):
+def own_kernel(table_ref, u_ref, s_ref, edge_ref, sums_ref, upper_ref, rest_ref):
     table = table_ref[...]
+    edge_ref[...] = table
     rank = jnp.floor(table[0:1, NBR : NBR + 1] * (1.0 / 512.0))
     own = alive(table)
     cell = lanes((16, 128)).astype(F32) + rank * 512.0
@@ -175,12 +176,13 @@
     return pl.pallas_call(
         own_kernel,
         out_shape=[
+            jax.ShapeDtypeStruct((16, 128), F32),
             jax.ShapeDtypeStruct((16, 256), F32),
             jax.ShapeDtypeStruct(inverse.shape, BF16),
             jax.ShapeDtypeStruct(inverse.shape, BF16),
         ],
         in_specs=[VMEM] * 3,
-        out_specs=[VMEM] * 3,
+        out_specs=[VMEM] * 4,
         compiler_params=PARAMS,
         name="own_part",
     )(table, trial, inverse)
@@ -355,10 +357,10 @@
     groups, group = lax.axis_size(ROWS), lax.axis_size(GROUP)
     across = [(i - 1, i) for i in range(group, groups, group)]
     across += [(target, source) for source, target in across]
-    edge = lax.ppermute(own, ROWS, across)
     g_group = lax.all_to_all(g_part, GROUP, 0, 0, tiled=True)
     trial = trial_basis.swapaxes(0, 1)
-    mine, upper, rest = own_part(own, trial, sample_inverse)
+    table, mine, upper, rest = own_part(own, trial, sample_inverse)
+    edge = lax.ppermute(table, ROWS, across)
     sent = sample(g_group, nbr, edge, mine, trial)
     parts = lax.all_to_all(sent, "zh", 0, 0, tiled=True)
     pieces = lax.all_to_all(fold(parts, upper, rest), CUBE, 0, 0, tiled=True)

time: 64.4 us -> 65.6 us (1.019)
  blocking collectives: 40.9 us -> 42.1 us
    all_to_all x1, blocking collectives: 18.3 us -> 19.4 us  [shards(): pieces = lax.all_to_all(fold(parts, upper, rest), CUBE, 0, 0, tiled=True)]
where the time goes in v9:
time: 65.6 us; the launch traced here: 65.3 us
  blocking collectives  42.1 us (64%)
  starting transfers between devices  10.9 us (17%)
  Pallas kernels  5.89 us (9%)
  waiting for transfers between devices  4.85 us (7%)
  between operations  0.84 us (1%)
  local copies, waits for them, and re-layouts  0.7 us (1%)
    all_to_all x1, blocking collectives, shards(): parts = lax.all_to_all(sent, 'zh', 0, 0, tiled=True)  22.7 us
    all_to_all x1, blocking collectives, shards(): pieces = lax.all_to_all(fold(parts, upper, rest), CUBE, 0, 0, tiled=True)  19.4 us
    all_to_all x1, starting transfers between devices, shards(): g_group = lax.all_to_all(g_part, GROUP, 0, 0, tiled=True)  10.2 us
    all_to_all x1, waiting for transfers between devices, shards(): g_group = lax.all_to_all(g_part, GROUP, 0, 0, tiled=True)  4.85 us
    pallas_call x1, Pallas kernels, prepare(): pl.pallas_call(prepare_kernel, in_specs=[HBM, HBM, HBM, HBM, HBM], out_sp...  2.8 us
  transfers between devices with their start and end apart: 2, of which 1 were waited for; matrix products, arithmetic and copies ran while one was open for 0% of the time, Pallas kernels for 1%

profile of v9, /device:TPU:1, one launch (start us, length us, event | category | flops | bytes accessed | tf_op | source)
XLA Modules:
  0.0 65.3 jit_solution(10435966157425045893)
XLA Ops:
  0.0 0.0 copy-start.1
  0.0 0.0 copy-start
  0.8 2.8 %prepare.1 = (f32[192,2,128]{2,1,0:T(2,128)}, f32[16,128]{1,0:T(8,128)}) custom-call(bf16[5,512,256]{2,1,0:T(8,128)(2,1)} %bitcast.12, bf16[5,512,128]{2,1,0:T(8,128)(2,1)} %bitcast.13, f32[5,7,16]{2,1,0:T(8,128)} %bitcast.14, s32[7,16]{1,0:T(8,128)} %bitcast.10, s32[1,1]{1,0:T(1,128)} %bitcast.7.count_hbm), custom_call_target="tpu_custom_call" | custom-call | tf_op jit(solution)/shard_map/prepare/pallas_call | solution.py:119
  3.6 0.0 copy-start.2
  3.6 10.2 %all-to-all-start = ((f32[192,2,128]{2,1,0:T(2,128)}), f32[192,2,128]{2,1,0:T(2,128)S(1)}, u32[]{:S(2)}, u32[]{:S(2)}) async-start(f32[192,2,128]{2,1,0:T(2,128)} %get-tuple-element.11), calls=%async_computation | async-start | bytes 393216 | tf_op jit(solution)/shard_map/all_to_all | solution.py:360
  13.8 0.0 copy-done.1
  13.8 0.0 copy-done
  13.8 0.0 copy-start.3
  13.8 0.7 %copy-done.3 = f32[16,128]{1,0:T(8,128)S(1)} copy-done((f32[16,128]{1,0:T(8,128)S(1)}, f32[16,128]{1,0:T(8,128)}, u32[]{:S(2)}) %copy-start.3) | copy-done | bytes 8216
  14.5 0.5 own_part.1
  15.0 0.7 %collective-permute-start = (f32[16,128]{1,0:T(8,128)S(1)}, f32[16,128]{1,0:T(8,128)S(1)}, u32[]{:S(2)}, u32[]{:S(2)}) collective-permute-start(f32[16,128]{1,0:T(8,128)S(1)} %get-tuple-element.13), channel_id=1, source_target_pairs={{60,64},{124,128},{188,192},{252,256},{316,320},{380,384},{444,448... | collective-permute-start | bytes 24584 | tf_op jit(solution)/shard_map/ppermute | solution.py:363
  15.7 0.0 collective-permute-done.edge_ref
  15.7 4.9 %all-to-all-done.x_ref = f32[192,2,128]{2,1,0:T(2,128)S(1)} async-done(((f32[192,2,128]{2,1,0:T(2,128)}), f32[192,2,128]{2,1,0:T(2,128)S(1)}, u32[]{:S(2)}, u32[]{:S(2)}) %all-to-all-start) | async-done | bytes 196640 | tf_op jit(solution)/shard_map/all_to_all | solution.py:360
  20.5 0.0 copy-done.2
  20.5 1.0 %sample.1 = s16[8,32,128]{2,1,0:T(8,128)(2,1)S(1)} custom-call(f32[192,2,128]{2,1,0:T(2,128)S(1)} %all-to-all-done.x_ref, s32[7,16]{1,0:T(8,128)S(1)} %bitcast.11, f32[16,128]{1,0:T(8,128)S(1)} %collective-permute-done.edge_ref, f32[16,256]{1,0:T(8,128)S(1)} %get-tuple-element.14.own_ref, bf16[5,512,256]{2,1,0:T(8,128)(2,1)S(1)} %bitcast.9), custom_call_target="tpu_custom_call" | custom-call | tf_op jit(solution)/shard_map/sample/pallas_call | solution.py:244
  21.6 22.7 %all_to_all.15.x_ref = s16[8,32,128]{2,1,0:T(8,128)(2,1)S(1)} all-to-all(s16[8,32,128]{2,1,0:T(8,128)(2,1)S(1)} %sample.1), channel_id=1, replica_groups=mesh['zh'=8,'zl'=2,'x'=4,'c'=2,'y'=4] {'zh'}, dimensions={0} | all-to-all | bytes 131072 | tf_op jit(solution)/shard_map/all_to_all | solution.py:365
  44.2 0.8 %fold.1 = f32[192,2,128]{2,1,0:T(2,128)S(1)} custom-call(s16[8,32,128]{2,1,0:T(8,128)(2,1)S(1)} %all_to_all.15.x_ref, bf16[128,512]{1,0:T(8,128)(2,1)S(1)} %get-tuple-element.15.upper_ref, bf16[128,512]{1,0:T(8,128)(2,1)S(1)} %get-tuple-element.16.rest_ref), custom_call_target="tpu_custom_call" | custom-call | tf_op jit(solution)/shard_map/fold/pallas_call | solution.py:319
  45.0 19.4 %all_to_all.16.x_ref = f32[192,2,128]{2,1,0:T(2,128)S(1)} all-to-all(f32[192,2,128]{2,1,0:T(2,128)S(1)} %fold.1), channel_id=1, replica_groups=mesh['zh'=8,'zl'=2,'x'=4,'c'=2,'y'=4] {'zl','x','c','y'}, dimensions={0} | all-to-all | bytes 393216 | tf_op jit(solution)/shard_map/all_to_all | solution.py:366
  64.5 0.8 %finish.1 = f32[2,64]{1,0:T(2,128)} custom-call(f32[192,2,128]{2,1,0:T(2,128)S(1)} %all_to_all.16.x_ref), custom_call_target="tpu_custom_call" | custom-call | tf_op jit(solution)/shard_map/finish/pallas_call | solution.py:344
Async XLA Ops:
  0.0 13.8 %copy-start.1 = (f32[128,512]{1,0:T(8,128)S(1)}, f32[128,512]{1,0:T(8,128)}, u32[]{:S(2)}) copy-start(f32[128,512]{1,0:T(8,128)} %s_ref.1) | copy-start | bytes 786436
  0.0 13.8 %copy-start = (bf16[512,5,256]{2,0,1:T(8,128)(2,1)S(1)}, bf16[512,5,256]{2,0,1:T(8,128)(2,1)}, u32[]{:S(2)}) copy-start(bf16[512,5,256]{2,0,1:T(8,128)(2,1)} %param.9) | copy-start | bytes 3932164
  3.6 17.0 %copy-start.2 = (s32[16,7]{0,1:T(8,128)S(1)}, s32[16,7]{0,1:T(8,128)}, u32[]{:S(2)}) copy-start(s32[16,7]{0,1:T(8,128)} %param.11) | copy-start | bytes 1348
  3.6 16.9 %all-to-all-start = ((f32[192,2,128]{2,1,0:T(2,128)}), f32[192,2,128]{2,1,0:T(2,128)S(1)}, u32[]{:S(2)}, u32[]{:S(2)}) async-start(f32[192,2,128]{2,1,0:T(2,128)} %get-tuple-element.11), calls=%async_computation | async-start | bytes 393216 | tf_op jit(solution)/shard_map/all_to_all | solution.py:360
  13.8 0.7 %copy-start.3 = (f32[16,128]{1,0:T(8,128)S(1)}, f32[16,128]{1,0:T(8,128)}, u32[]{:S(2)}) copy-start(f32[16,128]{1,0:T(8,128)} %get-tuple-element.12.table_ref) | copy-start | bytes 24580
  15.0 0.7 %collective-permute-start = (f32[16,128]{1,0:T(8,128)S(1)}, f32[16,128]{1,0:T(8,128)S(1)}, u32[]{:S(2)}, u32[]{:S(2)}) collective-permute-start(f32[16,128]{1,0:T(8,128)S(1)} %get-tuple-element.13), channel_id=1, source_target_pairs={{60,64},{124,128},{188,192},{252,256},{316,320},{380,384},{444,448... | collective-permute-start | bytes 24584 | tf_op jit(solution)/shard_map/ppermute | solution.py:363

commit v10 on v8

--- a/solution.py
+++ b/solution.py
@@ -155,38 +155,7 @@
     return weight
 
 
-def own_kernel(table_ref, u_ref, s_ref, sums_ref, upper_ref, rest_ref):
-    table = table_ref[...]
-    rank = jnp.floor(table[0:1, NBR : NBR + 1] * (1.0 / 512.0))
-    own = alive(table)
-    cell = lanes((16, 128)).astype(F32) + rank * 512.0
-    sums = jnp.zeros((32, 256), F32)
-    for j in range(NC):
-        parts = [weights(own, cell + 128.0 * part, j) for part in range(4)]
-        pieces = halves(jnp.concatenate(parts, axis=1))
-        sums = sums + jnp.dot(
-            jnp.concatenate(pieces, axis=0), u_ref[j], preferred_element_type=F32
-        )
-    sums_ref[...] = sums[0:16, :] + sums[16:32, :]
-    upper_ref[...], rest_ref[...] = halves(s_ref[...])
-
-
-def own_part(table, trial, inverse):
-    return pl.pallas_call(
-        own_kernel,
-        out_shape=[
-            jax.ShapeDtypeStruct((16, 256), F32),
-            jax.ShapeDtypeStruct(inverse.shape, BF16),
-            jax.ShapeDtypeStruct(inverse.shape, BF16),
-        ],
-        in_specs=[VMEM] * 3,
-        out_specs=[VMEM] * 3,
-        compiler_params=PARAMS,
-        name="own_part",
-    )(table, trial, inverse)
-
-
-def sample_kernel(x_ref, nbr_ref, edge_ref, own_ref, u_ref, out_ref):
+def sample_kernel(x_ref, nbr_ref, edge_ref, u_ref, out_ref):
     rank = jnp.floor(nbr_ref[0:1, 0:1].astype(F32) * (1.0 / 512.0))
     place = rank - 16.0 * jnp.floor(rank * 0.0625)
     lane = lanes((1, 128))
@@ -212,20 +181,20 @@
             extra = extra + jnp.where(lane == LOW_CNT + k, rows[0:1, CNT : CNT + 1], 0.0)
         tables.append(alive(rows))
     cell = lanes((16, 128)).astype(F32) + rank * 512.0
-    low = jnp.zeros((32, 256), F32)
-    high = jnp.zeros((32, 256), F32)
+    zero = jnp.zeros((16, 384), F32)
+    sums = jnp.zeros((96, 256), F32)
     for j in range(NC):
-        pieces = halves(weights(tables[0], cell, j))
-        low = low + jnp.dot(
-            jnp.concatenate(pieces, axis=0), u_ref[j, 0:128, :], preferred_element_type=F32
+        own = [weights(tables[1], cell + 128.0 * part, j) for part in range(4)]
+        rows = [
+            jnp.concatenate([weights(tables[0], cell, j), zero], axis=1),
+            jnp.concatenate(own, axis=1),
+            jnp.concatenate([zero, weights(tables[2], cell + 384.0, j)], axis=1),
+        ]
+        pieces = halves(jnp.concatenate(rows, axis=0))
+        sums = sums + jnp.dot(
+            jnp.concatenate(pieces, axis=0), u_ref[j], preferred_element_type=F32
         )
-        pieces = halves(weights(tables[2], cell + 384.0, j))
-        high = high + jnp.dot(
-            jnp.concatenate(pieces, axis=0), u_ref[j, 384:512, :], preferred_element_type=F32
-        )
-    rows = jnp.concatenate(
-        [low[0:16, :] + low[16:32, :], own_ref[...], high[0:16, :] + high[16:32, :]], axis=0
-    )
+    rows = sums[0:48, :] + sums[48:96, :]
     b_exp, g_exp = exponent(rows), exponent(total)
     rows = jnp.concatenate([coded(rows, b_exp), jnp.zeros((80, 256), F32)], axis=0)
     extra = extra + jnp.where(lane == RANK, rank, 0.0)
@@ -238,18 +207,19 @@
         out_ref[z] = to_i16(jnp.concatenate([code, left + right + extra], axis=0))
 
 
-def sample(g_parts, nbr, edge, own, trial):
+def sample(g_parts, nbr, edge, trial):
     return pl.pallas_call(
         sample_kernel,
         out_shape=jax.ShapeDtypeStruct((8, 32, 128), jnp.int16),
-        in_specs=[VMEM] * 5,
+        in_specs=[VMEM] * 4,
         out_specs=VMEM,
         compiler_params=PARAMS,
         name="sample",
-    )(g_parts, nbr, edge, own, trial)
-
-
-def fold_kernel(x_ref, upper_ref, rest_ref, out_ref):
+    )(g_parts, nbr, edge, trial)
+
+
+def fold_kernel(x_ref, s_ref, out_ref):
+    s_upper, s_rest = halves(s_ref[...])
     blocks = [from_i16(x_ref[z]) for z in range(8)]
     info = jnp.concatenate([block[16:17, :] for block in blocks], axis=0)
     lane = lanes((8, 128))
@@ -297,12 +267,12 @@
     upper, rest = halves(sampled)
     c = lax.dot_general(
         jnp.concatenate([upper, rest], axis=0),
-        upper_ref[...],
+        s_upper,
         (((1,), (1,)), ((), ())),
         preferred_element_type=F32,
     )
     c = (c[0:32, :] + c[32:64, :]) + lax.dot_general(
-        upper, rest_ref[...], (((1,), (1,)), ((), ())), preferred_element_type=F32
+        upper, s_rest, (((1,), (1,)), ((), ())), preferred_element_type=F32
     )
     g_pairs = total.reshape(8, 2, 128)
     c_pairs = c.reshape(16, 2, 128)
@@ -313,15 +283,15 @@
             out_ref[at + 2] = c_pairs[p]
 
 
-def fold(parts, upper, rest):
+def fold(parts, inverse):
     return pl.pallas_call(
         fold_kernel,
         out_shape=jax.ShapeDtypeStruct((192, 2, 128), F32),
-        in_specs=[VMEM] * 3,
+        in_specs=[VMEM] * 2,
         out_specs=VMEM,
         compiler_params=PARAMS,
         name="fold",
-    )(parts, upper, rest)
+    )(parts, inverse)
 
 
 def finish_kernel(x_ref, out_ref):
@@ -357,11 +327,9 @@
     across += [(target, source) for source, target in across]
     edge = lax.ppermute(own, ROWS, across)
     g_group = lax.all_to_all(g_part, GROUP, 0, 0, tiled=True)
-    trial = trial_basis.swapaxes(0, 1)
-    mine, upper, rest = own_part(own, trial, sample_inverse)
-    sent = sample(g_group, nbr, edge, mine, trial)
+    sent = sample(g_group, nbr, edge, trial_basis.swapaxes(0, 1))
     parts = lax.all_to_all(sent, "zh", 0, 0, tiled=True)
-    pieces = lax.all_to_all(fold(parts, upper, rest), CUBE, 0, 0, tiled=True)
+    pieces = lax.all_to_all(fold(parts, sample_inverse), CUBE, 0, 0, tiled=True)
     return finish(pieces).T
 
 

time: 64.4 us -> 64.8 us (level)
  waiting for transfers between devices: 4.87 us -> 6.08 us
  local copies, waits for them, and re-layouts: 0.7 us -> 0.01 us
    all_to_all x1, waiting for transfers between devices: 4.86 us -> 6.07 us  [shards(): g_group = lax.all_to_all(g_part, GROUP, 0, 0, tiled=True)]
    unnamed x8 -> x6, local copies, waits for them, and re-layouts: 0.7 us -> 0.01 us
  transfers between devices with their start and end apart: 2 -> 2, of which waited for: 1 -> 1; matrix products, arithmetic and copies ran while one was open for 0% -> 0% of each run, Pallas kernels for 1% -> 0%
where the time goes in v10:
time: 64.8 us; the launch traced here: 64.4 us
  blocking collectives  40.9 us (63%)
  starting transfers between devices  11 us (17%)
  waiting for transfers between devices  6.08 us (9%)
  Pallas kernels  5.6 us (9%)
  between operations  0.8 us (1%)
    all_to_all x1, blocking collectives, shards(): parts = lax.all_to_all(sent, 'zh', 0, 0, tiled=True)  22.7 us
    all_to_all x1, blocking collectives, shards(): pieces = lax.all_to_all(fold(parts, sample_inverse), CUBE, 0, 0, tiled=True)  18.3 us
    all_to_all x1, starting transfers between devices, shards(): g_group = lax.all_to_all(g_part, GROUP, 0, 0, tiled=True)  10.3 us
    all_to_all x1, waiting for transfers between devices, shards(): g_group = lax.all_to_all(g_part, GROUP, 0, 0, tiled=True)  6.07 us
    pallas_call x1, Pallas kernels, prepare(): pl.pallas_call(prepare_kernel, in_specs=[HBM, HBM, HBM, HBM, HBM], out_sp...  2.8 us
  transfers between devices with their start and end apart: 2, of which 1 were waited for; matrix products, arithmetic and copies ran while one was open for 0% of the time, Pallas kernels for 0%

profile of v10, /device:TPU:1, one launch (start us, length us, event | category | flops | bytes accessed | tf_op | source)
XLA Modules:
  0.0 64.4 jit_solution(1581966906980405401)
XLA Ops:
  0.0 0.0 copy-start.2
  0.0 0.0 copy-start
  0.8 2.8 %prepare.1 = (f32[192,2,128]{2,1,0:T(2,128)}, f32[16,128]{1,0:T(8,128)}) custom-call(bf16[5,512,256]{2,1,0:T(8,128)(2,1)} %bitcast.11, bf16[5,512,128]{2,1,0:T(8,128)(2,1)} %bitcast.12, f32[5,7,16]{2,1,0:T(8,128)} %bitcast.13, s32[7,16]{1,0:T(8,128)} %bitcast.9, s32[1,1]{1,0:T(1,128)} %bitcast.7.count_hbm), custom_call_target="tpu_custom_call" | custom-call | tf_op jit(solution)/shard_map/prepare/pallas_call | solution.py:119
  3.6 0.0 copy-start.1
  3.6 10.3 %all-to-all-start = ((f32[192,2,128]{2,1,0:T(2,128)}), f32[192,2,128]{2,1,0:T(2,128)S(1)}, u32[]{:S(2)}, u32[]{:S(2)}) async-start(f32[192,2,128]{2,1,0:T(2,128)} %get-tuple-element.7), calls=%async_computation | async-start | bytes 393216 | tf_op jit(solution)/shard_map/all_to_all | solution.py:329
  13.9 0.6 %collective-permute-start = (f32[16,128]{1,0:T(8,128)}, f32[16,128]{1,0:T(8,128)S(1)}, u32[]{:S(2)}, u32[]{:S(2)}) collective-permute-start(f32[16,128]{1,0:T(8,128)} %get-tuple-element.8), channel_id=1, source_target_pairs={{60,64},{124,128},{188,192},{252,256},{316,320},{380,384},{444,448... | collective-permute-start | bytes 24584 | tf_op jit(solution)/shard_map/ppermute | solution.py:328
  14.6 0.0 collective-permute-done.edge_ref
  14.6 6.1 %all-to-all-done.x_ref = f32[192,2,128]{2,1,0:T(2,128)S(1)} async-done(((f32[192,2,128]{2,1,0:T(2,128)}), f32[192,2,128]{2,1,0:T(2,128)S(1)}, u32[]{:S(2)}, u32[]{:S(2)}) %all-to-all-start) | async-done | bytes 196640 | tf_op jit(solution)/shard_map/all_to_all | solution.py:329
  20.7 0.0 copy-done.2
  20.7 0.0 copy-done
  20.7 1.2 %sample.1 = s16[8,32,128]{2,1,0:T(8,128)(2,1)S(1)} custom-call(f32[192,2,128]{2,1,0:T(2,128)S(1)} %all-to-all-done.x_ref, s32[7,16]{1,0:T(8,128)S(1)} %bitcast.10, f32[16,128]{1,0:T(8,128)S(1)} %collective-permute-done.edge_ref, bf16[5,512,256]{2,1,0:T(8,128)(2,1)S(1)} %bitcast.8), custom_call_target="tpu_custom_call" | custom-call | tf_op jit(solution)/shard_map/sample/pallas_call | solution.py:211
  21.9 22.7 %all_to_all.15.x_ref = s16[8,32,128]{2,1,0:T(8,128)(2,1)S(1)} all-to-all(s16[8,32,128]{2,1,0:T(8,128)(2,1)S(1)} %sample.1), channel_id=1, replica_groups=mesh['zh'=8,'zl'=2,'x'=4,'c'=2,'y'=4] {'zh'}, dimensions={0} | all-to-all | bytes 131072 | tf_op jit(solution)/shard_map/all_to_all | solution.py:331
  44.6 0.0 copy-done.1
  44.6 0.8 %fold.1 = f32[192,2,128]{2,1,0:T(2,128)S(1)} custom-call(s16[8,32,128]{2,1,0:T(8,128)(2,1)S(1)} %all_to_all.15.x_ref, f32[128,512]{1,0:T(8,128)S(1)} %copy-done.1), custom_call_target="tpu_custom_call" | custom-call | tf_op jit(solution)/shard_map/fold/pallas_call | solution.py:287
  45.3 18.3 %all_to_all.16.x_ref = f32[192,2,128]{2,1,0:T(2,128)S(1)} all-to-all(f32[192,2,128]{2,1,0:T(2,128)S(1)} %fold.1), channel_id=1, replica_groups=mesh['zh'=8,'zl'=2,'x'=4,'c'=2,'y'=4] {'zl','x','c','y'}, dimensions={0} | all-to-all | bytes 393216 | tf_op jit(solution)/shard_map/all_to_all | solution.py:332
  63.6 0.8 %finish.1 = f32[2,64]{1,0:T(2,128)} custom-call(f32[192,2,128]{2,1,0:T(2,128)S(1)} %all_to_all.16.x_ref), custom_call_target="tpu_custom_call" | custom-call | tf_op jit(solution)/shard_map/finish/pallas_call | solution.py:312
Async XLA Ops:
  0.0 20.7 %copy-start.2 = (s32[16,7]{0,1:T(8,128)S(1)}, s32[16,7]{0,1:T(8,128)}, u32[]{:S(2)}) copy-start(s32[16,7]{0,1:T(8,128)} %param.11) | copy-start | bytes 1348
  0.0 20.7 %copy-start = (bf16[512,5,256]{2,0,1:T(8,128)(2,1)S(1)}, bf16[512,5,256]{2,0,1:T(8,128)(2,1)}, u32[]{:S(2)}) copy-start(bf16[512,5,256]{2,0,1:T(8,128)(2,1)} %param.9) | copy-start | bytes 3932164
  3.6 41.0 %copy-start.1 = (f32[128,512]{1,0:T(8,128)S(1)}, f32[128,512]{1,0:T(8,128)}, u32[]{:S(2)}) copy-start(f32[128,512]{1,0:T(8,128)} %s_ref.1) | copy-start | bytes 786436
  3.6 17.1 %all-to-all-start = ((f32[192,2,128]{2,1,0:T(2,128)}), f32[192,2,128]{2,1,0:T(2,128)S(1)}, u32[]{:S(2)}, u32[]{:S(2)}) async-start(f32[192,2,128]{2,1,0:T(2,128)} %get-tuple-element.7), calls=%async_computation | async-start | bytes 393216 | tf_op jit(solution)/shard_map/all_to_all | solution.py:329
  13.9 0.7 %collective-permute-start = (f32[16,128]{1,0:T(8,128)}, f32[16,128]{1,0:T(8,128)S(1)}, u32[]{:S(2)}, u32[]{:S(2)}) collective-permute-start(f32[16,128]{1,0:T(8,128)} %get-tuple-element.8), channel_id=1, source_target_pairs={{60,64},{124,128},{188,192},{252,256},{316,320},{380,384},{444,448... | collective-permute-start | bytes 24584 | tf_op jit(solution)/shard_map/ppermute | solution.py:328

commit v11 on v8

--- a/solution.py
+++ b/solution.py
@@ -155,14 +155,13 @@
     return weight
 
 
-def own_kernel(table_ref, u_ref, s_ref, sums_ref, upper_ref, rest_ref):
-    table = table_ref[...]
+def own_kernel(jac_ref, nbr_ref, u_ref, s_ref, sums_ref, upper_ref, rest_ref):
+    table = table_of(jac_ref, nbr_ref, 0.0)
     rank = jnp.floor(table[0:1, NBR : NBR + 1] * (1.0 / 512.0))
-    own = alive(table)
     cell = lanes((16, 128)).astype(F32) + rank * 512.0
     sums = jnp.zeros((32, 256), F32)
     for j in range(NC):
-        parts = [weights(own, cell + 128.0 * part, j) for part in range(4)]
+        parts = [weights(table, cell + 128.0 * part, j) for part in range(4)]
         pieces = halves(jnp.concatenate(parts, axis=1))
         sums = sums + jnp.dot(
             jnp.concatenate(pieces, axis=0), u_ref[j], preferred_element_type=F32
@@ -171,7 +170,7 @@
     upper_ref[...], rest_ref[...] = halves(s_ref[...])
 
 
-def own_part(table, trial, inverse):
+def own_part(jac, nbr, trial, inverse):
     return pl.pallas_call(
         own_kernel,
         out_shape=[
@@ -179,11 +178,11 @@
             jax.ShapeDtypeStruct(inverse.shape, BF16),
             jax.ShapeDtypeStruct(inverse.shape, BF16),
         ],
-        in_specs=[VMEM] * 3,
+        in_specs=[VMEM] * 4,
         out_specs=[VMEM] * 3,
         compiler_params=PARAMS,
         name="own_part",
-    )(table, trial, inverse)
+    )(jac, nbr, trial, inverse)
 
 
 def sample_kernel(x_ref, nbr_ref, edge_ref, own_ref, u_ref, out_ref):
@@ -210,21 +209,24 @@
             rows = jnp.where(place == edge, edge_ref[...], rows)
         if k < 2:
             extra = extra + jnp.where(lane == LOW_CNT + k, rows[0:1, CNT : CNT + 1], 0.0)
-        tables.append(alive(rows))
+        tables.append(rows)
     cell = lanes((16, 128)).astype(F32) + rank * 512.0
+    low_table, high_table = alive(tables[0]), alive(tables[2])
+    slot = lax.broadcasted_iota(jnp.int32, (16, 256), 0).astype(F32)
+    own = jnp.where(slot < tables[1][:, CNT : CNT + 1], own_ref[...], 0.0)
     low = jnp.zeros((32, 256), F32)
     high = jnp.zeros((32, 256), F32)
     for j in range(NC):
-        pieces = halves(weights(tables[0], cell, j))
+        pieces = halves(weights(low_table, cell, j))
         low = low + jnp.dot(
             jnp.concatenate(pieces, axis=0), u_ref[j, 0:128, :], preferred_element_type=F32
         )
-        pieces = halves(weights(tables[2], cell + 384.0, j))
+        pieces = halves(weights(high_table, cell + 384.0, j))
         high = high + jnp.dot(
             jnp.concatenate(pieces, axis=0), u_ref[j, 384:512, :], preferred_element_type=F32
         )
     rows = jnp.concatenate(
-        [low[0:16, :] + low[16:32, :], own_ref[...], high[0:16, :] + high[16:32, :]], axis=0
+        [low[0:16, :] + low[16:32, :], own, high[0:16, :] + high[16:32, :]], axis=0
     )
     b_exp, g_exp = exponent(rows), exponent(total)
     rows = jnp.concatenate([coded(rows, b_exp), jnp.zeros((80, 256), F32)], axis=0)
@@ -358,7 +360,7 @@
     edge = lax.ppermute(own, ROWS, across)
     g_group = lax.all_to_all(g_part, GROUP, 0, 0, tiled=True)
     trial = trial_basis.swapaxes(0, 1)
-    mine, upper, rest = own_part(own, trial, sample_inverse)
+    mine, upper, rest = own_part(jac, nbr, trial, sample_inverse)
     sent = sample(g_group, nbr, edge, mine, trial)
     parts = lax.all_to_all(sent, "zh", 0, 0, tiled=True)
     pieces = lax.all_to_all(fold(parts, upper, rest), CUBE, 0, 0, tiled=True)

time: 64.4 us -> 64.4 us (level)
  local copies, waits for them, and re-layouts: 0.7 us -> 0.02 us
    unnamed x8, local copies, waits for them, and re-layouts: 0.7 us -> 0.02 us
where the time goes in v11:
time: 64.4 us; the launch traced here: 64.1 us
  blocking collectives  40.9 us (64%)
  starting transfers between devices  10.8 us (17%)
  Pallas kernels  5.94 us (9%)
  waiting for transfers between devices  5.49 us (9%)
  between operations  0.84 us (1%)
    all_to_all x1, blocking collectives, shards(): parts = lax.all_to_all(sent, 'zh', 0, 0, tiled=True)  22.7 us
    all_to_all x1, blocking collectives, shards(): pieces = lax.all_to_all(fold(parts, upper, rest), CUBE, 0, 0, tiled=True)  18.3 us
    all_to_all x1, starting transfers between devices, shards(): g_group = lax.all_to_all(g_part, GROUP, 0, 0, tiled=True)  10.2 us
    all_to_all x1, waiting for transfers between devices, shards(): g_group = lax.all_to_all(g_part, GROUP, 0, 0, tiled=True)  5.49 us
    pallas_call x1, Pallas kernels, prepare(): pl.pallas_call(prepare_kernel, in_specs=[HBM, HBM, HBM, HBM, HBM], out_sp...  2.8 us
  transfers between devices with their start and end apart: 2, of which 1 were waited for; matrix products, arithmetic and copies ran while one was open for 0% of the time, Pallas kernels for 1%

profile of v11, /device:TPU:1, one launch (start us, length us, event | category | flops | bytes accessed | tf_op | source)
XLA Modules:
  0.0 64.1 jit_solution(17596013115224054619)
XLA Ops:
  0.0 0.0 copy-start.3
  0.0 0.0 copy-start.2
  0.0 0.0 copy-start.1
  0.0 0.0 copy-start
  0.8 2.8 %prepare.1 = (f32[192,2,128]{2,1,0:T(2,128)}, f32[16,128]{1,0:T(8,128)}) custom-call(bf16[5,512,256]{2,1,0:T(8,128)(2,1)} %bitcast.15, bf16[5,512,128]{2,1,0:T(8,128)(2,1)} %bitcast.16, f32[5,7,16]{2,1,0:T(8,128)} %bitcast.10, s32[7,16]{1,0:T(8,128)} %bitcast.12, s32[1,1]{1,0:T(1,128)} %bitcast.7.count_hbm), custom_call_target="tpu_custom_call" | custom-call | tf_op jit(solution)/shard_map/prepare/pallas_call | solution.py:119
  3.6 10.2 %all-to-all-start = ((f32[192,2,128]{2,1,0:T(2,128)}), f32[192,2,128]{2,1,0:T(2,128)S(1)}, u32[]{:S(2)}, u32[]{:S(2)}) async-start(f32[192,2,128]{2,1,0:T(2,128)} %get-tuple-element.10), calls=%async_computation | async-start | bytes 393216 | tf_op jit(solution)/shard_map/all_to_all | solution.py:361
  13.8 0.6 %collective-permute-start = (f32[16,128]{1,0:T(8,128)}, f32[16,128]{1,0:T(8,128)S(1)}, u32[]{:S(2)}, u32[]{:S(2)}) collective-permute-start(f32[16,128]{1,0:T(8,128)} %get-tuple-element.11), channel_id=1, source_target_pairs={{60,64},{124,128},{188,192},{252,256},{316,320},{380,384},{444,448... | collective-permute-start | bytes 24584 | tf_op jit(solution)/shard_map/ppermute | solution.py:360
  14.4 0.0 copy-done.3
  14.5 0.0 copy-done.2
  14.5 0.0 copy-done.1
  14.5 0.0 copy-done
  14.5 0.5 own_part.1
  15.0 0.0 collective-permute-done.edge_ref
  15.0 5.5 %all-to-all-done.x_ref = f32[192,2,128]{2,1,0:T(2,128)S(1)} async-done(((f32[192,2,128]{2,1,0:T(2,128)}), f32[192,2,128]{2,1,0:T(2,128)S(1)}, u32[]{:S(2)}, u32[]{:S(2)}) %all-to-all-start) | async-done | bytes 196640 | tf_op jit(solution)/shard_map/all_to_all | solution.py:361
  20.5 1.0 %sample.1 = s16[8,32,128]{2,1,0:T(8,128)(2,1)S(1)} custom-call(f32[192,2,128]{2,1,0:T(2,128)S(1)} %all-to-all-done.x_ref, s32[7,16]{1,0:T(8,128)S(1)} %bitcast.14, f32[16,128]{1,0:T(8,128)S(1)} %collective-permute-done.edge_ref, f32[16,256]{1,0:T(8,128)S(1)} %get-tuple-element.12.own_ref, bf16[5,512,256]{2,1,0:T(8,128)(2,1)S(1)} %bitcast.9), custom_call_target="tpu_custom_call" | custom-call | tf_op jit(solution)/shard_map/sample/pallas_call | solution.py:244
  21.5 22.7 %all_to_all.15.x_ref = s16[8,32,128]{2,1,0:T(8,128)(2,1)S(1)} all-to-all(s16[8,32,128]{2,1,0:T(8,128)(2,1)S(1)} %sample.1), channel_id=1, replica_groups=mesh['zh'=8,'zl'=2,'x'=4,'c'=2,'y'=4] {'zh'}, dimensions={0} | all-to-all | bytes 131072 | tf_op jit(solution)/shard_map/all_to_all | solution.py:365
  44.2 0.8 %fold.1 = f32[192,2,128]{2,1,0:T(2,128)S(1)} custom-call(s16[8,32,128]{2,1,0:T(8,128)(2,1)S(1)} %all_to_all.15.x_ref, bf16[128,512]{1,0:T(8,128)(2,1)S(1)} %get-tuple-element.13.upper_ref, bf16[128,512]{1,0:T(8,128)(2,1)S(1)} %get-tuple-element.14.rest_ref), custom_call_target="tpu_custom_call" | custom-call | tf_op jit(solution)/shard_map/fold/pallas_call | solution.py:319
  45.0 18.3 %all_to_all.16.x_ref = f32[192,2,128]{2,1,0:T(2,128)S(1)} all-to-all(f32[192,2,128]{2,1,0:T(2,128)S(1)} %fold.1), channel_id=1, replica_groups=mesh['zh'=8,'zl'=2,'x'=4,'c'=2,'y'=4] {'zl','x','c','y'}, dimensions={0} | all-to-all | bytes 393216 | tf_op jit(solution)/shard_map/all_to_all | solution.py:366
  63.3 0.8 %finish.1 = f32[2,64]{1,0:T(2,128)} custom-call(f32[192,2,128]{2,1,0:T(2,128)S(1)} %all_to_all.16.x_ref), custom_call_target="tpu_custom_call" | custom-call | tf_op jit(solution)/shard_map/finish/pallas_call | solution.py:344
Async XLA Ops:
  0.0 14.4 %copy-start.3 = (s32[16,7]{0,1:T(8,128)S(1)}, s32[16,7]{0,1:T(8,128)}, u32[]{:S(2)}) copy-start(s32[16,7]{0,1:T(8,128)} %param.11) | copy-start | bytes 1348
  0.0 14.5 %copy-start.2 = (f32[16,7,5]{0,1,2:T(8,128)S(1)}, f32[16,7,5]{0,1,2:T(8,128)}, u32[]{:S(2)}) copy-start(f32[16,7,5]{0,1,2:T(8,128)} %param.10) | copy-start | bytes 6724
  0.0 14.5 %copy-start.1 = (f32[128,512]{1,0:T(8,128)S(1)}, f32[128,512]{1,0:T(8,128)}, u32[]{:S(2)}) copy-start(f32[128,512]{1,0:T(8,128)} %s_ref.1) | copy-start | bytes 786436
  0.0 14.5 %copy-start = (bf16[512,5,256]{2,0,1:T(8,128)(2,1)S(1)}, bf16[512,5,256]{2,0,1:T(8,128)(2,1)}, u32[]{:S(2)}) copy-start(bf16[512,5,256]{2,0,1:T(8,128)(2,1)} %param.9) | copy-start | bytes 3932164
  3.6 16.9 %all-to-all-start = ((f32[192,2,128]{2,1,0:T(2,128)}), f32[192,2,128]{2,1,0:T(2,128)S(1)}, u32[]{:S(2)}, u32[]{:S(2)}) async-start(f32[192,2,128]{2,1,0:T(2,128)} %get-tuple-element.10), calls=%async_computation | async-start | bytes 393216 | tf_op jit(solution)/shard_map/all_to_all | solution.py:361
  13.8 1.2 %collective-permute-start = (f32[16,128]{1,0:T(8,128)}, f32[16,128]{1,0:T(8,128)S(1)}, u32[]{:S(2)}, u32[]{:S(2)}) collective-permute-start(f32[16,128]{1,0:T(8,128)} %get-tuple-element.11), channel_id=1, source_target_pairs={{60,64},{124,128},{188,192},{252,256},{316,320},{380,384},{444,448... | collective-permute-start | bytes 24584 | tf_op jit(solution)/shard_map/ppermute | solution.py:360

commit v12 on v11

--- a/solution.py
+++ b/solution.py
@@ -28,7 +28,7 @@
 
 def exponent(x):
     top = jnp.max(jnp.abs(x), axis=(0, 1), keepdims=True)
-    return jnp.floor(-jnp.log2(jnp.maximum(top, 1e-30)))
+    return jnp.floor(-jnp.log2(jnp.maximum(top, 1e-37)))
 
 
 def coded(x, exp):

time: 64.4 us -> 64.4 us (level)
  no operation moved by 1% of the time
where the time goes in v12:
time: 64.4 us; the launch traced here: 64.1 us
  blocking collectives  40.9 us (64%)
  starting transfers between devices  10.8 us (17%)
  Pallas kernels  5.94 us (9%)
  waiting for transfers between devices  5.49 us (9%)
  between operations  0.84 us (1%)
    all_to_all x1, blocking collectives, shards(): parts = lax.all_to_all(sent, 'zh', 0, 0, tiled=True)  22.7 us
    all_to_all x1, blocking collectives, shards(): pieces = lax.all_to_all(fold(parts, upper, rest), CUBE, 0, 0, tiled=True)  18.3 us
    all_to_all x1, starting transfers between devices, shards(): g_group = lax.all_to_all(g_part, GROUP, 0, 0, tiled=True)  10.2 us
    all_to_all x1, waiting for transfers between devices, shards(): g_group = lax.all_to_all(g_part, GROUP, 0, 0, tiled=True)  5.49 us
    pallas_call x1, Pallas kernels, prepare(): pl.pallas_call(prepare_kernel, in_specs=[HBM, HBM, HBM, HBM, HBM], out_sp...  2.8 us
  transfers between devices with their start and end apart: 2, of which 1 were waited for; matrix products, arithmetic and copies ran while one was open for 0% of the time, Pallas kernels for 1%

profile of v12, /device:TPU:1, one launch (start us, length us, event | category | flops | bytes accessed | tf_op | source)
XLA Modules:
  0.0 64.1 jit_solution(812022351373966422)
XLA Ops:
  0.0 0.0 copy-start.3
  0.0 0.0 copy-start.2
  0.0 0.0 copy-start.1
  0.0 0.0 copy-start
  0.8 2.8 %prepare.1 = (f32[192,2,128]{2,1,0:T(2,128)}, f32[16,128]{1,0:T(8,128)}) custom-call(bf16[5,512,256]{2,1,0:T(8,128)(2,1)} %bitcast.15, bf16[5,512,128]{2,1,0:T(8,128)(2,1)} %bitcast.16, f32[5,7,16]{2,1,0:T(8,128)} %bitcast.10, s32[7,16]{1,0:T(8,128)} %bitcast.12, s32[1,1]{1,0:T(1,128)} %bitcast.7.count_hbm), custom_call_target="tpu_custom_call" | custom-call | tf_op jit(solution)/shard_map/prepare/pallas_call | solution.py:119
  3.6 10.2 %all-to-all-start = ((f32[192,2,128]{2,1,0:T(2,128)}), f32[192,2,128]{2,1,0:T(2,128)S(1)}, u32[]{:S(2)}, u32[]{:S(2)}) async-start(f32[192,2,128]{2,1,0:T(2,128)} %get-tuple-element.10), calls=%async_computation | async-start | bytes 393216 | tf_op jit(solution)/shard_map/all_to_all | solution.py:361
  13.8 0.6 %collective-permute-start = (f32[16,128]{1,0:T(8,128)}, f32[16,128]{1,0:T(8,128)S(1)}, u32[]{:S(2)}, u32[]{:S(2)}) collective-permute-start(f32[16,128]{1,0:T(8,128)} %get-tuple-element.11), channel_id=1, source_target_pairs={{60,64},{124,128},{188,192},{252,256},{316,320},{380,384},{444,448... | collective-permute-start | bytes 24584 | tf_op jit(solution)/shard_map/ppermute | solution.py:360
  14.4 0.0 copy-done.3
  14.5 0.0 copy-done.2
  14.5 0.0 copy-done.1
  14.5 0.0 copy-done
  14.5 0.5 own_part.1
  15.0 0.0 collective-permute-done.edge_ref
  15.0 5.5 %all-to-all-done.x_ref = f32[192,2,128]{2,1,0:T(2,128)S(1)} async-done(((f32[192,2,128]{2,1,0:T(2,128)}), f32[192,2,128]{2,1,0:T(2,128)S(1)}, u32[]{:S(2)}, u32[]{:S(2)}) %all-to-all-start) | async-done | bytes 196640 | tf_op jit(solution)/shard_map/all_to_all | solution.py:361
  20.5 1.0 %sample.1 = s16[8,32,128]{2,1,0:T(8,128)(2,1)S(1)} custom-call(f32[192,2,128]{2,1,0:T(2,128)S(1)} %all-to-all-done.x_ref, s32[7,16]{1,0:T(8,128)S(1)} %bitcast.14, f32[16,128]{1,0:T(8,128)S(1)} %collective-permute-done.edge_ref, f32[16,256]{1,0:T(8,128)S(1)} %get-tuple-element.12.own_ref, bf16[5,512,256]{2,1,0:T(8,128)(2,1)S(1)} %bitcast.9), custom_call_target="tpu_custom_call" | custom-call | tf_op jit(solution)/shard_map/sample/pallas_call | solution.py:244
  21.5 22.7 %all_to_all.15.x_ref = s16[8,32,128]{2,1,0:T(8,128)(2,1)S(1)} all-to-all(s16[8,32,128]{2,1,0:T(8,128)(2,1)S(1)} %sample.1), channel_id=1, replica_groups=mesh['zh'=8,'zl'=2,'x'=4,'c'=2,'y'=4] {'zh'}, dimensions={0} | all-to-all | bytes 131072 | tf_op jit(solution)/shard_map/all_to_all | solution.py:365
  44.2 0.8 %fold.1 = f32[192,2,128]{2,1,0:T(2,128)S(1)} custom-call(s16[8,32,128]{2,1,0:T(8,128)(2,1)S(1)} %all_to_all.15.x_ref, bf16[128,512]{1,0:T(8,128)(2,1)S(1)} %get-tuple-element.13.upper_ref, bf16[128,512]{1,0:T(8,128)(2,1)S(1)} %get-tuple-element.14.rest_ref), custom_call_target="tpu_custom_call" | custom-call | tf_op jit(solution)/shard_map/fold/pallas_call | solution.py:319
  45.0 18.3 %all_to_all.16.x_ref = f32[192,2,128]{2,1,0:T(2,128)S(1)} all-to-all(f32[192,2,128]{2,1,0:T(2,128)S(1)} %fold.1), channel_id=1, replica_groups=mesh['zh'=8,'zl'=2,'x'=4,'c'=2,'y'=4] {'zl','x','c','y'}, dimensions={0} | all-to-all | bytes 393216 | tf_op jit(solution)/shard_map/all_to_all | solution.py:366
  63.3 0.8 %finish.1 = f32[2,64]{1,0:T(2,128)} custom-call(f32[192,2,128]{2,1,0:T(2,128)S(1)} %all_to_all.16.x_ref), custom_call_target="tpu_custom_call" | custom-call | tf_op jit(solution)/shard_map/finish/pallas_call | solution.py:344
Async XLA Ops:
  0.0 14.4 %copy-start.3 = (s32[16,7]{0,1:T(8,128)S(1)}, s32[16,7]{0,1:T(8,128)}, u32[]{:S(2)}) copy-start(s32[16,7]{0,1:T(8,128)} %param.11) | copy-start | bytes 1348
  0.0 14.5 %copy-start.2 = (f32[16,7,5]{0,1,2:T(8,128)S(1)}, f32[16,7,5]{0,1,2:T(8,128)}, u32[]{:S(2)}) copy-start(f32[16,7,5]{0,1,2:T(8,128)} %param.10) | copy-start | bytes 6724
  0.0 14.5 %copy-start.1 = (f32[128,512]{1,0:T(8,128)S(1)}, f32[128,512]{1,0:T(8,128)}, u32[]{:S(2)}) copy-start(f32[128,512]{1,0:T(8,128)} %s_ref.1) | copy-start | bytes 786436
  0.0 14.5 %copy-start = (bf16[512,5,256]{2,0,1:T(8,128)(2,1)S(1)}, bf16[512,5,256]{2,0,1:T(8,128)(2,1)}, u32[]{:S(2)}) copy-start(bf16[512,5,256]{2,0,1:T(8,128)(2,1)} %param.9) | copy-start | bytes 3932164
  3.6 16.9 %all-to-all-start = ((f32[192,2,128]{2,1,0:T(2,128)}), f32[192,2,128]{2,1,0:T(2,128)S(1)}, u32[]{:S(2)}, u32[]{:S(2)}) async-start(f32[192,2,128]{2,1,0:T(2,128)} %get-tuple-element.10), calls=%async_computation | async-start | bytes 393216 | tf_op jit(solution)/shard_map/all_to_all | solution.py:361
  13.8 1.2 %collective-permute-start = (f32[16,128]{1,0:T(8,128)}, f32[16,128]{1,0:T(8,128)S(1)}, u32[]{:S(2)}, u32[]{:S(2)}) collective-permute-start(f32[16,128]{1,0:T(8,128)} %get-tuple-element.11), channel_id=1, source_target_pairs={{60,64},{124,128},{188,192},{252,256},{316,320},{380,384},{444,448... | collective-permute-start | bytes 24584 | tf_op jit(solution)/shard_map/ppermute | solution.py:360

commit v13 on v11

--- a/solution.py
+++ b/solution.py
@@ -96,9 +96,9 @@
         copy.wait()
     count = count_ref[0, 0].astype(F32)
     table = table_of(jac_ref, nbr_ref, count)
-    table_ref[...] = table
     packed = table[0:8, :] + pltpu.roll(table[8:16, :], 64, 1)
     packed = packed + jnp.where(lanes((8, 128)) >= GROUP_CNT, count, 0.0)
+    table_ref[...] = packed
     packed = packed.reshape(4, 2, 128)
     acc = jnp.zeros((128, 256), F32)
     for j in range(NC):
@@ -122,7 +122,7 @@
         out_specs=[VMEM, VMEM],
         out_shape=[
             jax.ShapeDtypeStruct((192, 2, 128), F32),
-            jax.ShapeDtypeStruct((16, 128), F32),
+            jax.ShapeDtypeStruct((8, 128), F32),
         ],
         scratch_shapes=[
             pltpu.VMEM(test.shape, BF16),
@@ -204,9 +204,9 @@
     tables = []
     for k, edge in ((0, 0.0), (1, None), (2, 15.0)):
         rows = near[k].reshape(8, 128)
-        rows = jnp.concatenate([rows, pltpu.roll(rows, 64, 1)], axis=0)
         if edge is not None:
             rows = jnp.where(place == edge, edge_ref[...], rows)
+        rows = jnp.concatenate([rows, pltpu.roll(rows, 64, 1)], axis=0)
         if k < 2:
             extra = extra + jnp.where(lane == LOW_CNT + k, rows[0:1, CNT : CNT + 1], 0.0)
         tables.append(rows)

time: 64.4 us -> 64.3 us (level)
  no operation moved by 1% of the time
where the time goes in v13:
time: 64.3 us; the launch traced here: 64 us
  blocking collectives  40.9 us (64%)
  starting transfers between devices  10.8 us (17%)
  Pallas kernels  5.94 us (9%)
  waiting for transfers between devices  5.49 us (9%)
  between operations  0.84 us (1%)
    all_to_all x1, blocking collectives, shards(): parts = lax.all_to_all(sent, 'zh', 0, 0, tiled=True)  22.7 us
    all_to_all x1, blocking collectives, shards(): pieces = lax.all_to_all(fold(parts, upper, rest), CUBE, 0, 0, tiled=True)  18.2 us
    all_to_all x1, starting transfers between devices, shards(): g_group = lax.all_to_all(g_part, GROUP, 0, 0, tiled=True)  10.2 us
    all_to_all x1, waiting for transfers between devices, shards(): g_group = lax.all_to_all(g_part, GROUP, 0, 0, tiled=True)  5.49 us
    pallas_call x1, Pallas kernels, prepare(): pl.pallas_call(prepare_kernel, in_specs=[HBM, HBM, HBM, HBM, HBM], out_sp...  2.8 us
  transfers between devices with their start and end apart: 2, of which 1 were waited for; matrix products, arithmetic and copies ran while one was open for 0% of the time, Pallas kernels for 1%

profile of v13, /device:TPU:1, one launch (start us, length us, event | category | flops | bytes accessed | tf_op | source)
XLA Modules:
  0.0 64.0 jit_solution(6576493664875149067)
XLA Ops:
  0.0 0.0 copy-start.3
  0.0 0.0 copy-start.2
  0.0 0.0 copy-start.1
  0.0 0.0 copy-start
  0.8 2.8 %prepare.1 = (f32[192,2,128]{2,1,0:T(2,128)}, f32[8,128]{1,0:T(8,128)}) custom-call(bf16[5,512,256]{2,1,0:T(8,128)(2,1)} %bitcast.15, bf16[5,512,128]{2,1,0:T(8,128)(2,1)} %bitcast.16, f32[5,7,16]{2,1,0:T(8,128)} %bitcast.10, s32[7,16]{1,0:T(8,128)} %bitcast.12, s32[1,1]{1,0:T(1,128)} %bitcast.7.count_hbm), custom_call_target="tpu_custom_call" | custom-call | tf_op jit(solution)/shard_map/prepare/pallas_call | solution.py:119
  3.6 10.2 %all-to-all-start = ((f32[192,2,128]{2,1,0:T(2,128)}), f32[192,2,128]{2,1,0:T(2,128)S(1)}, u32[]{:S(2)}, u32[]{:S(2)}) async-start(f32[192,2,128]{2,1,0:T(2,128)} %get-tuple-element.10), calls=%async_computation | async-start | bytes 393216 | tf_op jit(solution)/shard_map/all_to_all | solution.py:361
  13.8 0.6 %collective-permute-start = (f32[8,128]{1,0:T(8,128)}, f32[8,128]{1,0:T(8,128)S(1)}, u32[]{:S(2)}, u32[]{:S(2)}) collective-permute-start(f32[8,128]{1,0:T(8,128)} %get-tuple-element.11), channel_id=1, source_target_pairs={{60,64},{124,128},{188,192},{252,256},{316,320},{380,384},{444,448... | collective-permute-start | bytes 12296 | tf_op jit(solution)/shard_map/ppermute | solution.py:360
  14.4 0.0 copy-done.3
  14.5 0.0 copy-done.2
  14.5 0.0 copy-done.1
  14.5 0.0 copy-done
  14.5 0.5 own_part.1
  15.0 0.0 collective-permute-done.edge_ref
  15.0 5.5 %all-to-all-done.x_ref = f32[192,2,128]{2,1,0:T(2,128)S(1)} async-done(((f32[192,2,128]{2,1,0:T(2,128)}), f32[192,2,128]{2,1,0:T(2,128)S(1)}, u32[]{:S(2)}, u32[]{:S(2)}) %all-to-all-start) | async-done | bytes 196640 | tf_op jit(solution)/shard_map/all_to_all | solution.py:361
  20.5 1.0 %sample.1 = s16[8,32,128]{2,1,0:T(8,128)(2,1)S(1)} custom-call(f32[192,2,128]{2,1,0:T(2,128)S(1)} %all-to-all-done.x_ref, s32[7,16]{1,0:T(8,128)S(1)} %bitcast.14, f32[8,128]{1,0:T(8,128)S(1)} %collective-permute-done.edge_ref, f32[16,256]{1,0:T(8,128)S(1)} %get-tuple-element.12.own_ref, bf16[5,512,256]{2,1,0:T(8,128)(2,1)S(1)} %bitcast.9), custom_call_target="tpu_custom_call" | custom-call | tf_op jit(solution)/shard_map/sample/pallas_call | solution.py:244
  21.5 22.7 %all_to_all.15.x_ref = s16[8,32,128]{2,1,0:T(8,128)(2,1)S(1)} all-to-all(s16[8,32,128]{2,1,0:T(8,128)(2,1)S(1)} %sample.1), channel_id=1, replica_groups=mesh['zh'=8,'zl'=2,'x'=4,'c'=2,'y'=4] {'zh'}, dimensions={0} | all-to-all | bytes 131072 | tf_op jit(solution)/shard_map/all_to_all | solution.py:365
  44.2 0.8 %fold.1 = f32[192,2,128]{2,1,0:T(2,128)S(1)} custom-call(s16[8,32,128]{2,1,0:T(8,128)(2,1)S(1)} %all_to_all.15.x_ref, bf16[128,512]{1,0:T(8,128)(2,1)S(1)} %get-tuple-element.13.upper_ref, bf16[128,512]{1,0:T(8,128)(2,1)S(1)} %get-tuple-element.14.rest_ref), custom_call_target="tpu_custom_call" | custom-call | tf_op jit(solution)/shard_map/fold/pallas_call | solution.py:319
  45.0 18.2 %all_to_all.16.x_ref = f32[192,2,128]{2,1,0:T(2,128)S(1)} all-to-all(f32[192,2,128]{2,1,0:T(2,128)S(1)} %fold.1), channel_id=1, replica_groups=mesh['zh'=8,'zl'=2,'x'=4,'c'=2,'y'=4] {'zl','x','c','y'}, dimensions={0} | all-to-all | bytes 393216 | tf_op jit(solution)/shard_map/all_to_all | solution.py:366
  63.2 0.8 %finish.1 = f32[2,64]{1,0:T(2,128)} custom-call(f32[192,2,128]{2,1,0:T(2,128)S(1)} %all_to_all.16.x_ref), custom_call_target="tpu_custom_call" | custom-call | tf_op jit(solution)/shard_map/finish/pallas_call | solution.py:344
Async XLA Ops:
  0.0 14.4 %copy-start.3 = (s32[16,7]{0,1:T(8,128)S(1)}, s32[16,7]{0,1:T(8,128)}, u32[]{:S(2)}) copy-start(s32[16,7]{0,1:T(8,128)} %param.11) | copy-start | bytes 1348
  0.0 14.5 %copy-start.2 = (f32[16,7,5]{0,1,2:T(8,128)S(1)}, f32[16,7,5]{0,1,2:T(8,128)}, u32[]{:S(2)}) copy-start(f32[16,7,5]{0,1,2:T(8,128)} %param.10) | copy-start | bytes 6724
  0.0 14.5 %copy-start.1 = (f32[128,512]{1,0:T(8,128)S(1)}, f32[128,512]{1,0:T(8,128)}, u32[]{:S(2)}) copy-start(f32[128,512]{1,0:T(8,128)} %s_ref.1) | copy-start | bytes 786436
  0.0 14.5 %copy-start = (bf16[512,5,256]{2,0,1:T(8,128)(2,1)S(1)}, bf16[512,5,256]{2,0,1:T(8,128)(2,1)}, u32[]{:S(2)}) copy-start(bf16[512,5,256]{2,0,1:T(8,128)(2,1)} %param.9) | copy-start | bytes 3932164
  3.6 16.9 %all-to-all-start = ((f32[192,2,128]{2,1,0:T(2,128)}), f32[192,2,128]{2,1,0:T(2,128)S(1)}, u32[]{:S(2)}, u32[]{:S(2)}) async-start(f32[192,2,128]{2,1,0:T(2,128)} %get-tuple-element.10), calls=%async_computation | async-start | bytes 393216 | tf_op jit(solution)/shard_map/all_to_all | solution.py:361
  13.8 1.2 %collective-permute-start = (f32[8,128]{1,0:T(8,128)}, f32[8,128]{1,0:T(8,128)S(1)}, u32[]{:S(2)}, u32[]{:S(2)}) collective-permute-start(f32[8,128]{1,0:T(8,128)} %get-tuple-element.11), channel_id=1, source_target_pairs={{60,64},{124,128},{188,192},{252,256},{316,320},{380,384},{444,448... | collective-permute-start | bytes 12296 | tf_op jit(solution)/shard_map/ppermute | solution.py:360

commit v14 on v13

--- a/solution.py
+++ b/solution.py
@@ -8,7 +8,7 @@
 
 ROWS = ("zh", "zl", "x", "c")
 GROUP = ("zl", "x", "c")
-CUBE = ("zl", "x", "c", "y")
+CUBE = ("y", "zl", "x", "c")
 F32 = jnp.float32
 BF16 = jnp.bfloat16
 NC, NB = 5, 7
@@ -28,7 +28,7 @@
 
 def exponent(x):
     top = jnp.max(jnp.abs(x), axis=(0, 1), keepdims=True)
-    return jnp.floor(-jnp.log2(jnp.maximum(top, 1e-30)))
+    return jnp.floor(-jnp.log2(jnp.maximum(top, 1e-37)))
 
 
 def coded(x, exp):
@@ -310,7 +310,7 @@
     c_pairs = c.reshape(16, 2, 128)
     for p in range(16):
         for m in range(4):
-            at = 3 * (4 * p + m)
+            at = 3 * (16 * m + p)
             out_ref[at : at + 2] = g_pairs[2 * m : 2 * m + 2]
             out_ref[at + 2] = c_pairs[p]
 
@@ -329,11 +329,11 @@
 def finish_kernel(x_ref, out_ref):
     sums = [jnp.zeros((64, 128), F32), jnp.zeros((64, 128), F32)]
     for m in range(4):
-        rows = [x_ref[3 * (4 * p + m) : 3 * (4 * p + m) + 2] for p in range(16)]
+        rows = [x_ref[3 * (16 * m + p) : 3 * (16 * m + p) + 2] for p in range(16)]
         rows = jnp.concatenate(rows, axis=0).reshape(64, 128)
-        c = x_ref[3 * m + 2]
+        c = x_ref[48 * m + 2]
         for p in range(1, 16):
-            c = c + x_ref[3 * (4 * p + m) + 2]
+            c = c + x_ref[3 * (16 * m + p) + 2]
         sums = [sums[j] + rows * c[j : j + 1, :] for j in range(2)]
     total = jnp.sum(jnp.concatenate(sums, axis=0).T, axis=0, keepdims=True)
     out_ref[0:1, :] = total[:, 0:64]

time: 64.3 us -> 64.3 us (level)
  no operation moved by 1% of the time
where the time goes in v14:
time: 64.3 us; the launch traced here: 64 us
  blocking collectives  40.9 us (64%)
  starting transfers between devices  10.8 us (17%)
  Pallas kernels  5.94 us (9%)
  waiting for transfers between devices  5.49 us (9%)
  between operations  0.84 us (1%)
    all_to_all x1, blocking collectives, shards(): parts = lax.all_to_all(sent, 'zh', 0, 0, tiled=True)  22.7 us
    all_to_all x1, blocking collectives, shards(): pieces = lax.all_to_all(fold(parts, upper, rest), CUBE, 0, 0, tiled=True)  18.2 us
    all_to_all x1, starting transfers between devices, shards(): g_group = lax.all_to_all(g_part, GROUP, 0, 0, tiled=True)  10.2 us
    all_to_all x1, waiting for transfers between devices, shards(): g_group = lax.all_to_all(g_part, GROUP, 0, 0, tiled=True)  5.49 us
    pallas_call x1, Pallas kernels, prepare(): pl.pallas_call(prepare_kernel, in_specs=[HBM, HBM, HBM, HBM, HBM], out_sp...  2.8 us
  transfers between devices with their start and end apart: 2, of which 1 were waited for; matrix products, arithmetic and copies ran while one was open for 0% of the time, Pallas kernels for 1%

profile of v14, /device:TPU:1, one launch (start us, length us, event | category | flops | bytes accessed | tf_op | source)
XLA Modules:
  0.0 64.0 jit_solution(9775149479991157275)
XLA Ops:
  0.0 0.0 copy-start.3
  0.0 0.0 copy-start.2
  0.0 0.0 copy-start.1
  0.0 0.0 copy-start
  0.8 2.8 %prepare.1 = (f32[192,2,128]{2,1,0:T(2,128)}, f32[8,128]{1,0:T(8,128)}) custom-call(bf16[5,512,256]{2,1,0:T(8,128)(2,1)} %bitcast.15, bf16[5,512,128]{2,1,0:T(8,128)(2,1)} %bitcast.16, f32[5,7,16]{2,1,0:T(8,128)} %bitcast.10, s32[7,16]{1,0:T(8,128)} %bitcast.12, s32[1,1]{1,0:T(1,128)} %bitcast.7.count_hbm), custom_call_target="tpu_custom_call" | custom-call | tf_op jit(solution)/shard_map/prepare/pallas_call | solution.py:119
  3.6 10.2 %all-to-all-start = ((f32[192,2,128]{2,1,0:T(2,128)}), f32[192,2,128]{2,1,0:T(2,128)S(1)}, u32[]{:S(2)}, u32[]{:S(2)}) async-start(f32[192,2,128]{2,1,0:T(2,128)} %get-tuple-element.10), calls=%async_computation | async-start | bytes 393216 | tf_op jit(solution)/shard_map/all_to_all | solution.py:361
  13.8 0.6 %collective-permute-start = (f32[8,128]{1,0:T(8,128)}, f32[8,128]{1,0:T(8,128)S(1)}, u32[]{:S(2)}, u32[]{:S(2)}) collective-permute-start(f32[8,128]{1,0:T(8,128)} %get-tuple-element.11), channel_id=1, source_target_pairs={{60,64},{124,128},{188,192},{252,256},{316,320},{380,384},{444,448... | collective-permute-start | bytes 12296 | tf_op jit(solution)/shard_map/ppermute | solution.py:360
  14.4 0.0 copy-done.3
  14.5 0.0 copy-done.2
  14.5 0.0 copy-done.1
  14.5 0.0 copy-done
  14.5 0.5 own_part.1
  15.0 0.0 collective-permute-done.edge_ref
  15.0 5.5 %all-to-all-done.x_ref = f32[192,2,128]{2,1,0:T(2,128)S(1)} async-done(((f32[192,2,128]{2,1,0:T(2,128)}), f32[192,2,128]{2,1,0:T(2,128)S(1)}, u32[]{:S(2)}, u32[]{:S(2)}) %all-to-all-start) | async-done | bytes 196640 | tf_op jit(solution)/shard_map/all_to_all | solution.py:361
  20.5 1.0 %sample.1 = s16[8,32,128]{2,1,0:T(8,128)(2,1)S(1)} custom-call(f32[192,2,128]{2,1,0:T(2,128)S(1)} %all-to-all-done.x_ref, s32[7,16]{1,0:T(8,128)S(1)} %bitcast.14, f32[8,128]{1,0:T(8,128)S(1)} %collective-permute-done.edge_ref, f32[16,256]{1,0:T(8,128)S(1)} %get-tuple-element.12.own_ref, bf16[5,512,256]{2,1,0:T(8,128)(2,1)S(1)} %bitcast.9), custom_call_target="tpu_custom_call" | custom-call | tf_op jit(solution)/shard_map/sample/pallas_call | solution.py:244
  21.5 22.7 %all_to_all.15.x_ref = s16[8,32,128]{2,1,0:T(8,128)(2,1)S(1)} all-to-all(s16[8,32,128]{2,1,0:T(8,128)(2,1)S(1)} %sample.1), channel_id=1, replica_groups=mesh['zh'=8,'zl'=2,'x'=4,'c'=2,'y'=4] {'zh'}, dimensions={0} | all-to-all | bytes 131072 | tf_op jit(solution)/shard_map/all_to_all | solution.py:365
  44.2 0.8 %fold.1 = f32[192,2,128]{2,1,0:T(2,128)S(1)} custom-call(s16[8,32,128]{2,1,0:T(8,128)(2,1)S(1)} %all_to_all.15.x_ref, bf16[128,512]{1,0:T(8,128)(2,1)S(1)} %get-tuple-element.13.upper_ref, bf16[128,512]{1,0:T(8,128)(2,1)S(1)} %get-tuple-element.14.rest_ref), custom_call_target="tpu_custom_call" | custom-call | tf_op jit(solution)/shard_map/fold/pallas_call | solution.py:319
  45.0 18.2 %all_to_all.16.x_ref = f32[192,2,128]{2,1,0:T(2,128)S(1)} all-to-all(f32[192,2,128]{2,1,0:T(2,128)S(1)} %fold.1), channel_id=1, replica_groups=mesh['zh'=8,'zl'=2,'x'=4,'c'=2,'y'=4] {'y','zl','x','c'}, dimensions={0} | all-to-all | bytes 393216 | tf_op jit(solution)/shard_map/all_to_all | solution.py:366
  63.2 0.8 %finish.1 = f32[2,64]{1,0:T(2,128)} custom-call(f32[192,2,128]{2,1,0:T(2,128)S(1)} %all_to_all.16.x_ref), custom_call_target="tpu_custom_call" | custom-call | tf_op jit(solution)/shard_map/finish/pallas_call | solution.py:344
Async XLA Ops:
  0.0 14.4 %copy-start.3 = (s32[16,7]{0,1:T(8,128)S(1)}, s32[16,7]{0,1:T(8,128)}, u32[]{:S(2)}) copy-start(s32[16,7]{0,1:T(8,128)} %param.11) | copy-start | bytes 1348
  0.0 14.5 %copy-start.2 = (f32[16,7,5]{0,1,2:T(8,128)S(1)}, f32[16,7,5]{0,1,2:T(8,128)}, u32[]{:S(2)}) copy-start(f32[16,7,5]{0,1,2:T(8,128)} %param.10) | copy-start | bytes 6724
  0.0 14.5 %copy-start.1 = (f32[128,512]{1,0:T(8,128)S(1)}, f32[128,512]{1,0:T(8,128)}, u32[]{:S(2)}) copy-start(f32[128,512]{1,0:T(8,128)} %s_ref.1) | copy-start | bytes 786436
  0.0 14.5 %copy-start = (bf16[512,5,256]{2,0,1:T(8,128)(2,1)S(1)}, bf16[512,5,256]{2,0,1:T(8,128)(2,1)}, u32[]{:S(2)}) copy-start(bf16[512,5,256]{2,0,1:T(8,128)(2,1)} %param.9) | copy-start | bytes 3932164
  3.6 16.9 %all-to-all-start = ((f32[192,2,128]{2,1,0:T(2,128)}), f32[192,2,128]{2,1,0:T(2,128)S(1)}, u32[]{:S(2)}, u32[]{:S(2)}) async-start(f32[192,2,128]{2,1,0:T(2,128)} %get-tuple-element.10), calls=%async_computation | async-start | bytes 393216 | tf_op jit(solution)/shard_map/all_to_all | solution.py:361
  13.8 1.2 %collective-permute-start = (f32[8,128]{1,0:T(8,128)}, f32[8,128]{1,0:T(8,128)S(1)}, u32[]{:S(2)}, u32[]{:S(2)}) collective-permute-start(f32[8,128]{1,0:T(8,128)} %get-tuple-element.11), channel_id=1, source_target_pairs={{60,64},{124,128},{188,192},{252,256},{316,320},{380,384},{444,448... | collective-permute-start | bytes 12296 | tf_op jit(solution)/shard_map/ppermute | solution.py:360
